TPU v7x, 32 devices: a whole 2x2x4 slice. The times are simulated.
32 devices in a mesh: rep: 4 (over y, x), seq: 8 (over z, core).
Axes of the slice: x: 2, y: 2, z: 4, core: 2. Of those that a mesh axis runs over, the one named last changes fastest.
Arguments:
- inputs: bfloat16 [196608, 512], P(('rep', 'seq'))
- mel_frames: bfloat16 [80, 196608], P(None, ('rep', 'seq')), may hold values from -6 to 6
- utterance: int32 [196608], P(('rep', 'seq')), may hold values from 0 to 15, never falling along the last dimension, each value on 1 to 49152 neighbouring positions
- keep_mask: int32 [196608], P(('rep', 'seq')), may hold values 0 or 1
- res_grad: bfloat16 [196608, 512], P(('rep', 'seq')), may hold values from -6 to 6
- skip_grad: bfloat16 [196608, 512], P(('rep', 'seq')), may hold values from -6 to 6
- conv_weight: float32 [512, 2, 1024], P('seq'), may hold values from -0.1875 to 0.1875
- cond_weight: float32 [80, 1024], P(None, 'seq'), may hold values from -0.625 to 0.625
- out_weight: float32 [512, 1024], P('seq'), may hold values from -0.25 to 0.25
- biases: float32 [2048], P('seq'), may hold values from -2 to 2
- conv_first: float32 [512, 2, 1024], P('seq')
- conv_second: float32 [512, 2, 1024], P('seq')
- cond_first: float32 [80, 1024], P(None, 'seq')
- cond_second: float32 [80, 1024], P(None, 'seq')
- out_first: float32 [512, 1024], P('seq')
- out_second: float32 [512, 1024], P('seq')
- bias_first: float32 [2048], P('seq')
- bias_second: float32 [2048], P('seq')
Outputs:
- residual_out: bfloat16 [196608, 512], P(('rep', 'seq'))
- skip_out: bfloat16 [196608, 512], P(('rep', 'seq'))
- input_grad: bfloat16 [196608, 512], P(('rep', 'seq'))
- grad_norm: float32 [], replicated
- conv_first_new: float32 [512, 2, 1024], P('seq')
- conv_second_new: float32 [512, 2, 1024], P('seq')
- conv_weight_new: float32 [512, 2, 1024], P('seq')
- cond_first_new: float32 [80, 1024], P(None, 'seq')
- cond_second_new: float32 [80, 1024], P(None, 'seq')
- cond_weight_new: float32 [80, 1024], P(None, 'seq')
- out_first_new: float32 [512, 1024], P('seq')
- out_second_new: float32 [512, 1024], P('seq')
- out_weight_new: float32 [512, 1024], P('seq')
- bias_first_new: float32 [2048], P('seq')
- bias_second_new: float32 [2048], P('seq')
- bias_new: float32 [2048], P('seq')
Inputs may be any that keep to these rules, and one draw needn't show every extreme that they name: utterance never falls along time; every number below the count occurs; one utterance has exactly 49152 samples.
All inputs are finite; a program needn't handle non-finite values. No bound on the sum of `keep_mask` on one device may be relied on, other than what follows from the above.
Results may differ from a plain program's by a relative error of at most 0.007.
Values may be sent and summed in bfloat16 or wider, within the bound.
No kernel may reach another device: no remote copies, remote signals or barrier semaphores. Data moves between devices by JAX's collectives and lax.ppermute only.
A program may use at most 256 MiB of HBM per device.

v0:
```python
import jax
import jax.numpy as jnp
from jax import lax
from jax.sharding import PartitionSpec as P

DILATION_STEP = 512
STEP = 10


beta_one = 0.9
beta_two = 0.999
learn_rate = 0.05
weight_decay = 0.01
epsilon = 1e-08
clip_bound = 1.0


def from_behind(x, axis, by):
    count = lax.axis_size(axis)
    pairs = [(i, i + by) for i in range(count) if 0 <= i + by < count]
    return lax.ppermute(x, axis, pairs)


def contract_rows(left, right):
    return lax.dot_general(
        left, right, (((0,), (0,)), ((), ())), preferred_element_type=jnp.float32
    )


def contract_cols(left, right):
    return lax.dot_general(
        left, right, (((1,), (1,)), ((), ())), preferred_element_type=jnp.float32
    )


def adamw_update(grad, moment, second, weight, factor, decay):
    clipped = grad * factor
    moment_new = beta_one * moment + (1.0 - beta_one) * clipped
    second_new = beta_two * second + (1.0 - beta_two) * clipped * clipped
    mean_hat = moment_new / (1.0 - beta_one**STEP)
    square_hat = second_new / (1.0 - beta_two**STEP)
    weight_new = weight - learn_rate * (
        mean_hat / (jnp.sqrt(square_hat) + epsilon) + decay * weight
    )
    return (moment_new, second_new, weight_new)


def local(
    inputs,
    mel_frames,
    utterance,
    keep_mask,
    res_grad,
    skip_grad,
    conv_weight,
    cond_weight,
    out_weight,
    biases,
    conv_first,
    conv_second,
    cond_first,
    cond_second,
    out_first,
    out_second,
    bias_first,
    bias_second,
):
    rows, width = inputs.shape
    receptive_span = DILATION_STEP
    lowered = (
        conv_weight.astype(jnp.bfloat16),
        cond_weight.astype(jnp.bfloat16),
        out_weight.astype(jnp.bfloat16),
        biases.astype(jnp.bfloat16),
    )
    conv_all, cond_all, out_all, bias_all = (
        lax.all_gather(lowered[0], "seq", axis=0, tiled=True),
        lax.all_gather(lowered[1], "seq", axis=1, tiled=True),
        lax.all_gather(lowered[2], "seq", axis=0, tiled=True),
        lax.all_gather(lowered[3], "seq", axis=0, tiled=True),
    )
    gate_width = cond_all.shape[1]
    half = gate_width // 2
    bias_full = bias_all.astype(jnp.float32)
    prev_tail = from_behind(inputs[rows - receptive_span :], ("rep", "seq"), 1)
    prev_ids = from_behind(utterance[rows - receptive_span :], ("rep", "seq"), 1)
    shifted = jnp.concatenate([prev_tail, inputs[: rows - receptive_span]], 0)
    shifted_ids = jnp.concatenate([prev_ids, utterance[: rows - receptive_span]], 0)
    joined_pairs = shifted_ids == utterance
    preceding_rows = jnp.where(joined_pairs[:, None], shifted, jnp.zeros_like(shifted))
    now_taps = conv_all[:, 0, :]
    past_taps = conv_all[:, 1, :]
    pre = jnp.dot(inputs, now_taps, preferred_element_type=jnp.float32)
    pre = pre + jnp.dot(preceding_rows, past_taps, preferred_element_type=jnp.float32)
    pre = pre + contract_rows(mel_frames, cond_all) + bias_full[:gate_width]
    filt = jnp.tanh(pre[:, :half])
    gate = jax.nn.sigmoid(pre[:, half:])
    keep_float = keep_mask.astype(jnp.float32)[:, None]
    hidden = (keep_float * filt * gate).astype(jnp.bfloat16)
    mixed = jnp.dot(hidden, out_all, preferred_element_type=jnp.float32) + bias_full[gate_width:]
    residual_out = (inputs.astype(jnp.float32) + mixed[:, :width]).astype(jnp.bfloat16)
    skip_out = mixed[:, width:].astype(jnp.bfloat16)
    back_now, back_past, back_out = (now_taps, past_taps, out_all)
    upstream = jnp.concatenate([res_grad, skip_grad], 1)
    grad_out = contract_rows(hidden, upstream)
    hidden_grad = contract_cols(upstream, back_out)
    filt_grad = hidden_grad * keep_float * gate * (1.0 - filt * filt)
    gate_grad = hidden_grad * keep_float * filt * gate * (1.0 - gate)
    pre_grad = jnp.concatenate([filt_grad, gate_grad], 1).astype(jnp.bfloat16)
    grad_conv = jnp.stack(
        [contract_rows(inputs, pre_grad), contract_rows(preceding_rows, pre_grad)], 1
    )
    grad_cond = jnp.dot(mel_frames, pre_grad, preferred_element_type=jnp.float32)
    grad_bias = jnp.concatenate(
        [jnp.sum(pre_grad, 0, dtype=jnp.float32), jnp.sum(upstream, 0, dtype=jnp.float32)], 0
    )
    earlier_grad = jnp.where(joined_pairs[:, None], contract_cols(pre_grad, back_past), 0.0)
    returned = from_behind(
        earlier_grad[:receptive_span].astype(jnp.bfloat16), ("rep", "seq"), -1
    ).astype(jnp.float32)
    input_grad = res_grad.astype(jnp.float32) + contract_cols(pre_grad, back_now)
    input_grad = input_grad + jnp.concatenate([earlier_grad[receptive_span:], returned], 0)
    grads = (grad_conv, grad_cond, grad_out, grad_bias)
    parts = (
        lax.psum_scatter(grads[0], "seq", scatter_dimension=0, tiled=True),
        lax.psum_scatter(grads[1], "seq", scatter_dimension=1, tiled=True),
        lax.psum_scatter(grads[2], "seq", scatter_dimension=0, tiled=True),
        lax.psum_scatter(grads[3], "seq", scatter_dimension=0, tiled=True),
    )
    owned = lax.psum((parts[0], parts[1], parts[2], parts[3]), "rep")
    own_conv, own_cond, own_out, own_bias = owned
    squares = (
        jnp.sum(own_conv * own_conv)
        + jnp.sum(own_cond * own_cond)
        + jnp.sum(own_out * own_out)
        + jnp.sum(own_bias * own_bias)
    )
    total = lax.psum(squares, "seq")
    grad_norm = jnp.sqrt(total)
    factor = clip_bound / jnp.maximum(grad_norm, clip_bound)
    conv_new = adamw_update(own_conv, conv_first, conv_second, conv_weight, factor, weight_decay)
    cond_new = adamw_update(own_cond, cond_first, cond_second, cond_weight, factor, weight_decay)
    out_new = adamw_update(own_out, out_first, out_second, out_weight, factor, weight_decay)
    bias_new = adamw_update(own_bias, bias_first, bias_second, biases, factor, 0.0)
    return (
        residual_out,
        skip_out,
        input_grad.astype(jnp.bfloat16),
        grad_norm,
        conv_new[0],
        conv_new[1],
        conv_new[2],
        cond_new[0],
        cond_new[1],
        cond_new[2],
        out_new[0],
        out_new[1],
        out_new[2],
        bias_new[0],
        bias_new[1],
        bias_new[2],
    )


def solution(mesh):
    placed = (
        P(("rep", "seq"), None),
        P(None, ("rep", "seq")),
        P(("rep", "seq")),
        P(("rep", "seq")),
        P(("rep", "seq"), None),
        P(("rep", "seq"), None),
        P("seq", None, None),
        P(None, "seq"),
        P("seq", None),
        P("seq"),
        P("seq", None, None),
        P("seq", None, None),
        P(None, "seq"),
        P(None, "seq"),
        P("seq", None),
        P("seq", None),
        P("seq"),
        P("seq"),
    )
    return jax.shard_map(
        local,
        mesh=mesh,
        in_specs=placed,
        out_specs=(
            P(("rep", "seq"), None),
            P(("rep", "seq"), None),
            P(("rep", "seq"), None),
            P(),
            P("seq", None, None),
            P("seq", None, None),
            P("seq", None, None),
            P(None, "seq"),
            P(None, "seq"),
            P(None, "seq"),
            P("seq", None),
            P("seq", None),
            P("seq", None),
            P("seq"),
            P("seq"),
            P("seq"),
        ),
        check_vma=False,
    )
```

profile of v0, /device:TPU:0, one launch (start us, length us, event | category | flops | bytes accessed | tf_op | source)
XLA Modules:
  0.0 458.5 jit_solution(8760804919575507111)
XLA Ops:
  7.2 2.0 copy.74
  9.3 0.7 slice.45
  10.0 2.3 collective-permute-start
  12.3 1.9 slice.47
  14.2 5.4 %collective-permute-start.1 = (bf16[512,512]{1,0:T(8,128)(2,1)}, bf16[512,512]{1,0:T(8,128)(2,1)}, u32[]{:S(2)}, u32[]{:S(2)}) collective-permute-start(bf16[512,512]{1,0:T(8,128)(2,1)} %slice.47), channel_id=1, source_target_pairs={{0,1},{1,2},{2,3},{3,4},{4,5},{5,6},{6,7},{7,8},{8,9},{9,10},{10,1... | collective-permute-start | bytes 1572872 | tf_op jit(solution)/shard_map/ppermute | solution.py:21
  19.6 1.6 convert_element_type.52
  22.0 24.6 %all-gather = bf16[8,1,256]{2,1,0:T(2,128)(2,1)S(1)} all-gather(bf16[1,1,256]{2,1,0:T(2,128)(2,1)S(1)} %reshape.36), channel_id=1, replica_groups=mesh['rep'=4,'seq'=8] {'seq'}, dimensions={0}, use_global_device_ids=true | all-gather | bytes 4608 | tf_op jit(solution)/shard_map/all_gather | solution.py:80
  46.6 0.8 convert_element_type.48
  47.4 13.1 %all_gather.13 = bf16[80,1024]{1,0:T(8,128)(2,1)S(1)} all-gather(bf16[80,128]{1,0:T(8,128)(2,1)S(1)} %convert_element_type.48), channel_id=1, replica_groups=mesh['rep'=4,'seq'=8] {'seq'}, dimensions={1}, use_global_device_ids=true | all-gather | bytes 184320 | tf_op jit(solution)/shard_map/all_gather | solution.py:78
  60.5 6.6 %constant_dynamic-update-slice_fusion.1 = bf16[6144,1024]{1,0:T(8,128)(2,1)} fusion(bf16[6144,512]{1,0:T(8,128)(2,1)} %param.22), kind=kLoop, calls=%fused_computation.49 | loop fusion | bytes 12582912
  67.1 10.1 %fusion.21 = f32[6144,1024]{0,1:T(8,128)} fusion(bf16[80,6144]{1,0:T(8,128)(2,1)S(1)} %copy-done, bf16[80,1024]{1,0:T(8,128)(2,1)S(1)} %all_gather.13), kind=kOutput, calls=%fused_computation.61 | convolution fusion | flops 1006632960 | bytes 26312704 | tf_op jit(solution)/shard_map/dot_general | solution.py:25
  77.3 3.2 constant_dynamic-update-slice_fusion
  80.5 2.9 slice.48
  83.5 14.2 %fusion.5 = f32[6144,1024]{0,1:T(8,128)} fusion(bf16[6144,512]{1,0:T(8,128)(2,1)} %param.18, bf16[512,2,1024]{2,0,1:T(8,128)(2,1)} %all-gather.4.cloned.1.call-done), kind=kOutput, calls=%fused_computation.27 | convolution fusion | flops 6442450944 | bytes 32505856 | tf_op jit(solution)/shard_map/dot_general | solution.py:93
  97.7 27.9 %add_add_fusion = f32[6144,1024]{0,1:T(8,128)} fusion(f32[6144,1024]{0,1:T(8,128)} %fusion.21, f32[6144,1024]{0,1:T(8,128)} %fusion.5, f32[1024]{0:T(1024)S(1)} %bitcast.36, bf16[512,2,1024]{2,0,1:T(8,128)(2,1)S(1)} %copy-done.5, bf16[5632,512]{1,0:T(8,128)(2,1)} %slice.48, bf16[512,512]{1,0:T(8,128)(2,1)} %collective-permute-done.1, ...), kind=kOutput, calls=%fused_computation.2 | convolution fusion | flops 6477053952 | bytes 82847744 | tf_op jit(solution)/shard_map/dot_general | solution.py:94
  125.6 24.6 %multiply_convert_fusion.1 = (bf16[6144,512]{0,1:T(8,128)(2,1)S(1)}, bf16[6144,512]{0,1:T(8,128)(2,1)}, bf16[6144,512]{0,1:T(8,128)(2,1)}) fusion(f32[6144,1024]{0,1:T(8,128)} %add_add_fusion, f32[6144]{0:T(1024)S(1)} %convert_element_type.46, bf16[6144,1024]{1,0:T(8,128)(2,1)} %constant_dynamic-update-slice_fusion, ...), kind=kOutput, calls=%fused_computation.15 | convolution fusion | flops 6495928320 | bytes 57696256 | tf_op jit(solution)/shard_map/dot_general | solution.py:31
  150.2 12.4 %convolution_bitcast_fusion.1 = f32[512,1,1024]{0,2,1:T(8,128)S(1)} fusion(bf16[6144,512]{1,0:T(8,128)(2,1)} %param.18, bf16[6144,512]{0,1:T(8,128)(2,1)} %get-tuple-element.81, bf16[6144,512]{0,1:T(8,128)(2,1)S(1)} %get-tuple-element.80), kind=kOutput, calls=%fused_computation.22 | convolution fusion | flops 6467616768 | bytes 20971520 | tf_op jit(solution)/shard_map/dot_general | solution.py:25
  162.6 10.3 %convolution_bitcast_fusion = f32[512,1,1024]{0,2,1:T(8,128)S(1)} fusion(bf16[5632,512]{1,0:T(8,128)(2,1)} %slice.48, bf16[512,512]{1,0:T(8,128)(2,1)} %collective-permute-done.1, pred[6144]{0:T(1024)(128)(4,1)S(1)} %add_compare_fusion, bf16[6144,512]{0,1:T(8,128)(2,1)} %get-tuple-element.81, bf16[6144,512]{0,1:T(8,128)(2,1)S(1)} %get-tuple-element.80), kind=kOutput, calls=%fused_computation.21 | convolution fusion | flops 6483345408 | bytes 20977664 | tf_op jit(solution)/shard_map/dot_general | solution.py:25
  173.0 2.5 pad_maximum_fusion.1
  175.5 7.4 %copy.56 = f32[512,2,1024]{2,1,0:T(2,128)} copy(f32[512,2,1024]{0,2,1:T(8,128)} %pad_maximum_fusion.1) | data formatting | bytes 8388608 | tf_op jit(solution)/shard_map/stack | solution.py:110
  183.0 6.4 %convert_reduce_fusion = f32[1024]{0:T(1024)S(1)} fusion(bf16[6144,1024]{1,0:T(8,128)(2,1)} %constant_dynamic-update-slice_fusion), kind=kLoop, calls=%fused_computation | loop fusion | flops 12581888 | bytes 12587008 | tf_op jit(solution)/shard_map/reduce_sum | solution.py:115
  191.3 12.8 %fusion.22 = f32[512,1024]{1,0:T(8,128)} fusion(bf16[6144,512]{0,1:T(8,128)(2,1)} %get-tuple-element.82, bf16[6144,1024]{1,0:T(8,128)(2,1)} %constant_dynamic-update-slice_fusion), kind=kOutput, calls=%fused_computation.62 | convolution fusion | flops 6442450944 | bytes 20971520 | tf_op jit(solution)/shard_map/dot_general | solution.py:25
  204.1 7.7 %convolution_bitcast_fusion.2 = f32[80,1024]{1,0:T(8,128)} fusion(bf16[80,6144]{1,0:T(8,128)(2,1)S(1)} %copy-done, bf16[6144,512]{0,1:T(8,128)(2,1)} %get-tuple-element.81, bf16[6144,512]{0,1:T(8,128)(2,1)} %copy-done.1), kind=kOutput, calls=%fused_computation.23 | convolution fusion | flops 1031798784 | bytes 13893632 | tf_op jit(solution)/shard_map/dot_general | solution.py:113
  211.9 14.2 %broadcast_add_fusion = f32[6144,1024]{1,0:T(8,128)} fusion(f32[1024]{0:T(1024)S(1)} %bitcast.37, bf16[6144,512]{0,1:T(8,128)(2,1)} %get-tuple-element.82, bf16[512,1024]{1,0:T(8,128)(2,1)} %all-gather.6.cloned.1.call-done), kind=kOutput, calls=%fused_computation.16 | convolution fusion | flops 6448742400 | bytes 32509952 | tf_op jit(solution)/shard_map/dot_general | solution.py:100
  226.0 11.4 %fusion = bf16[6144,512]{1,0:T(8,128)(2,1)} fusion(f32[6144,1024]{1,0:T(8,128)} %broadcast_add_fusion, bf16[6144,512]{1,0:T(8,128)(2,1)} %param.18), kind=kLoop, calls=%fused_computation.5 | loop fusion | flops 9437184 | bytes 25165824 | tf_op jit(solution)/shard_map/convert_element_type | solution.py:101
  237.5 14.5 %convolution_select_fusion = f32[6144,512]{1,0:T(8,128)} fusion(pred[6144]{0:T(1024)(128)(4,1)S(1)} %add_compare_fusion, bf16[512,2,1024]{2,0,1:T(8,128)(2,1)S(1)} %copy-done.5, bf16[6144,512]{0,1:T(8,128)(2,1)} %get-tuple-element.81, bf16[6144,512]{0,1:T(8,128)(2,1)} %copy-done.1), kind=kOutput, calls=%fused_computation.18 | convolution fusion | flops 6470762496 | bytes 26220544 | tf_op jit(solution)/shard_map/dot_general | solution.py:31
  252.0 10.1 %slice.68 = f32[5632,512]{1,0:T(8,128)} slice(f32[6144,512]{1,0:T(8,128)} %convolution_select_fusion), slice={[512:6144], [0:512]} | slice | bytes 23068672 | tf_op jit(solution)/shard_map/slice | solution.py:122
  262.2 1.3 slice.102
  263.5 8.2 %slice.101 = bf16[6144,512]{1,0:T(8,128)(2,1)} slice(f32[6144,1024]{1,0:T(8,128)} %broadcast_add_fusion), slice={[0:6144], [512:1024]} | slice | bytes 12582912 | tf_op jit(solution)/shard_map/slice | solution.py:102
  271.7 1.3 collective-permute-start.2
  272.9 6.3 %all-reduce.7.cloned.1.call-done = f32[512,2,1024]{2,1,0:T(2,128)} async-done(((f32[512,2,1024]{2,1,0:T(2,128)}), f32[512,2,1024]{2,1,0:T(2,128)}) %all-reduce.7.cloned.1.call-update) | async-done | bytes 4194320
  279.2 1.1 constant_dynamic-slice_fusion
  280.3 1.0 copy.57
  281.2 36.5 %reduce-scatter.5.cloned.1.call-done = f32[64,1024]{1,0:T(8,128)} async-done(((f32[512,1024]{1,0:T(8,128)}), f32[64,1024]{1,0:T(8,128)}) %reduce-scatter.5.cloned.1.call-update) | async-done | bytes 262160 | tf_op jit(solution)/shard_map/reduce_scatter | solution.py:127
  317.8 6.6 %convert_reduce_fusion.1 = f32[1024]{0:T(1024)S(1)} fusion(bf16[6144,512]{0,1:T(8,128)(2,1)} %get-tuple-element.81, bf16[6144,512]{0,1:T(8,128)(2,1)} %copy-done.1), kind=kLoop, calls=%fused_computation.1 | loop fusion | flops 31456256 | bytes 12587008 | tf_op jit(solution)/shard_map/reduce_sum | solution.py:115
  324.5 14.9 %all-reduce.1 = f32[2048]{0:T(1024)S(1)} all-reduce(f32[2048]{0:T(1024)S(1)} %pad_maximum_fusion.2), channel_id=5, replica_groups=mesh['rep'=4,'seq'=8] {'seq'}, use_global_device_ids=true, to_apply=%region_11.12.clone | all-reduce | flops 2048 | bytes 16384
  339.6 9.9 %reduce-scatter.3.cloned.1.call-done = f32[80,128]{1,0:T(8,128)} async-done(((f32[80,1024]{1,0:T(8,128)}), f32[80,128]{1,0:T(8,128)}) %reduce-scatter.3.cloned.1.call-update) | async-done | bytes 40976 | tf_op jit(solution)/shard_map/reduce_scatter | solution.py:126
  349.6 17.4 %all-reduce.2 = (f32[80,128]{1,0:T(8,128)S(1)}, f32[256]{0:T(256)S(1)}) all-reduce(f32[80,128]{1,0:T(8,128)} %reduce-scatter.3.cloned.1.call-done, f32[256]{0:T(256)S(1)} %dynamic-slice.3), channel_id=1, replica_groups=mesh['rep'=4,'seq'=8] {'rep'}, use_global_device_ids=true, to_apply=%region_4.5 | all-reduce | flops 10496 | bytes 83968 | tf_op jit(solution)/shard_map/psum | solution.py:130
  368.1 32.8 %all-reduce.9.cloned.1.call-done = (f32[64,2,1024]{2,0,1:T(8,128)}, f32[64,1024]{1,0:T(8,128)}) async-done(((f32[64,2,1024]{2,0,1:T(8,128)}, f32[64,1024]{1,0:T(8,128)}), (f32[64,2,1024]{2,0,1:T(8,128)}, f32[64,1024]{1,0:T(8,128)})) %all-reduce.9.cloned.1.call-update) | async-done | bytes 786448 | tf_op jit(solution)/shard_map/psum | solution.py:130
  400.9 1.8 multiply_reduce_fusion
  402.7 1.6 multiply_reduce_fusion.1
  407.0 16.7 %fusion.4 = bf16[6144,512]{1,0:T(8,128)(2,1)} fusion(f32[512,512]{1,0:T(8,128)S(1)} %convert_element_type.55, f32[5632,512]{1,0:T(8,128)} %slice.68, bf16[6144,512]{1,0:T(8,128)(2,1)} %param.22, bf16[512,2,1024]{2,0,1:T(8,128)(2,1)} %all-gather.4.cloned.1.call-done, bf16[6144,512]{0,1:T(8,128)(2,1)} %get-tuple-element.81, bf16[6144,512]{0,1:T(8,128)(2,1)} %copy-done.1), kind=kOutput, calls=%fused_computation.13 | convolution fusion | flops 6483345408 | bytes 38797312 | tf_op jit(solution)/shard_map/dot_general | solution.py:31
  423.7 16.8 %psum.39 = f32[]{:T(128)} all-reduce(f32[]{:T(128)S(6)} %add.133), channel_id=1, replica_groups=mesh['rep'=4,'seq'=8] {'seq'}, use_global_device_ids=true, to_apply=%region_14.15 | all-reduce | flops 1 | bytes 8 | tf_op jit(solution)/shard_map/psum | solution.py:138
  441.3 2.0 multiply_subtract_fusion
  443.3 1.2 copy.62
  444.5 1.2 copy.63
  445.7 1.2 copy.64
  447.5 2.1 multiply_subtract_fusion.1
  (70 shorter events, 4.4 us)
Async XLA Ops:
  7.2 59.9 %copy-start = (bf16[80,6144]{1,0:T(8,128)(2,1)S(1)}, bf16[80,6144]{1,0:T(8,128)(2,1)}, u32[]{:S(2)}) copy-start(bf16[80,6144]{1,0:T(8,128)(2,1)} %param.19) | copy-start | bytes 2949124
  7.2 76.3 %all-gather.4.cloned.1.call-start = ((), (), s32[]{:S(2)}) async-start(), calls=%async_computation.2 | async-start | bytes 2359296 | tf_op jit(solution)/shard_map/all_gather | solution.py:77
  9.2 116.3 %all-gather.6.cloned.1.call-start = ((), (), s32[]{:S(2)}) async-start(), calls=%async_computation.3 | async-start | bytes 1179648 | tf_op jit(solution)/shard_map/all_gather | solution.py:79
  10.0 73.4 %collective-permute-start = (s32[512]{0:T(512)S(1)}, s32[512]{0:T(512)S(1)}, u32[]{:S(2)}, u32[]{:S(2)}) collective-permute-start(s32[512]{0:T(512)S(1)} %slice.45), channel_id=1, source_target_pairs={{0,1},{1,2},{2,3},{3,4},{4,5},{5,6},{6,7},{7,8},{8,9},{9,10},{10,1... | collective-permute-start | bytes 6152 | tf_op jit(solution)/shard_map/ppermute | solution.py:21
  14.2 83.5 %collective-permute-start.1 = (bf16[512,512]{1,0:T(8,128)(2,1)}, bf16[512,512]{1,0:T(8,128)(2,1)}, u32[]{:S(2)}, u32[]{:S(2)}) collective-permute-start(bf16[512,512]{1,0:T(8,128)(2,1)} %slice.47), channel_id=1, source_target_pairs={{0,1},{1,2},{2,3},{3,4},{4,5},{5,6},{6,7},{7,8},{8,9},{9,10},{10,1... | collective-permute-start | bytes 1572872 | tf_op jit(solution)/shard_map/ppermute | solution.py:21
  21.3 258.0 %all-reduce.7.cloned.1.call-start = ((), (), s32[]{:S(2)}) async-start(), calls=%async_computation.6 | async-start | bytes 8388608
  60.5 16.8 %slice-start.2 = ((s8[6291456]{0:T(1024)(128)(4,1)}), s8[4194304]{0:T(1024)(128)(4,1)S(1)}, s32[]{:S(2)}) async-start(s8[6291456]{0:T(1024)(128)(4,1)} %bitcast.33), calls=%async_computation.10 | async-start | bytes 8388608
  60.5 20.0 %slice-start = ((s8[6291456]{0:T(1024)(128)(4,1)}), s8[4194304]{0:T(1024)(128)(4,1)S(1)}, s32[]{:S(2)}) async-start(s8[6291456]{0:T(1024)(128)(4,1)} %bitcast.31), calls=%async_computation.8 | async-start | bytes 8388608
  67.1 10.2 %slice-start.3 = ((s8[6291456]{0:T(1024)(128)(4,1)}), s8[2097152]{0:T(1024)(128)(4,1)S(1)}, s32[]{:S(2)}) async-start(s8[6291456]{0:T(1024)(128)(4,1)} %bitcast.33), calls=%async_computation.11 | async-start | bytes 4194304
  67.1 13.4 %slice-start.1 = ((s8[6291456]{0:T(1024)(128)(4,1)}), s8[2097152]{0:T(1024)(128)(4,1)S(1)}, s32[]{:S(2)}) async-start(s8[6291456]{0:T(1024)(128)(4,1)} %bitcast.31), calls=%async_computation.9 | async-start | bytes 4194304
  77.2 6.2 %copy-start.10 = (s32[6144]{0:T(1024)S(1)}, s32[6144]{0:T(1024)}, u32[]{:S(2)}) copy-start(s32[6144]{0:T(1024)} %param.21) | copy-start | bytes 73732
  77.2 6.2 %copy-start.7 = (s32[6144]{0:T(1024)S(1)}, s32[6144]{0:T(1024)}, u32[]{:S(2)}) copy-start(s32[6144]{0:T(1024)} %param.20) | copy-start | bytes 73732
  83.5 14.2 %copy-start.5 = (bf16[512,2,1024]{2,0,1:T(8,128)(2,1)S(1)}, bf16[512,2,1024]{2,0,1:T(8,128)(2,1)}, u32[]{:S(2)}) copy-start(bf16[512,2,1024]{2,0,1:T(8,128)(2,1)} %all-gather.4.cloned.1.call-done) | copy-start | bytes 6291460
  150.2 12.4 %copy-start.1 = (bf16[6144,512]{0,1:T(8,128)(2,1)}, bf16[6144,512]{0,1:T(8,128)(2,1)S(1)}, u32[]{:S(2)}) copy-start(bf16[6144,512]{0,1:T(8,128)(2,1)S(1)} %get-tuple-element.80) | copy-start | bytes 18874372
  175.5 13.9 %copy-start.14 = (u32[32]{0:T(128)S(1)}, u32[32]{0:T(128)}, u32[]{:S(2)}) copy-start(u32[32]{0:T(128)} %constant.10) | copy-start | bytes 388
  182.9 134.9 %reduce-scatter.5.cloned.1.call-start = ((), (), s32[]{:S(2)}) async-start(), calls=%async_computation.5 | async-start | bytes 2359296 | tf_op jit(solution)/shard_map/reduce_scatter | solution.py:127
  204.1 145.5 %reduce-scatter.3.cloned.1.call-start = ((), (), s32[]{:S(2)}) async-start(), calls=%async_computation.4 | async-start | bytes 368640 | tf_op jit(solution)/shard_map/reduce_scatter | solution.py:126
  237.5 163.5 %all-reduce.9.cloned.1.call-start = ((), (), s32[]{:S(2)}) async-start(), calls=%async_computation.7 | async-start | bytes 1572864 | tf_op jit(solution)/shard_map/psum | solution.py:130
  271.7 67.8 %collective-permute-start.2 = (bf16[512,512]{1,0:T(8,128)(2,1)S(1)}, bf16[512,512]{1,0:T(8,128)(2,1)S(1)}, u32[]{:S(2)}, u32[]{:S(2)}) collective-permute-start(bf16[512,512]{1,0:T(8,128)(2,1)S(1)} %slice.102), channel_id=1, source_target_pairs={{1,0},{2,1},{3,2},{4,3},{5,4},{6,5},{7,6},{8,7},{9,8},{10,9},{11,1... | collective-permute-start | bytes 1572872 | tf_op jit(solution)/shard_map/ppermute | solution.py:21
  406.9 34.4 %copy-start.2 = (f32[64,2,1024]{2,1,0:T(2,128)S(1)}, f32[64,2,1024]{2,1,0:T(2,128)}, u32[]{:S(2)}) copy-start(f32[64,2,1024]{2,1,0:T(2,128)} %param.24) | copy-start | bytes 1572868
  406.9 34.4 %copy-start.3 = (f32[64,2,1024]{2,0,1:T(8,128)S(1)}, f32[64,2,1024]{2,0,1:T(8,128)}, u32[]{:S(2)}) copy-start(f32[64,2,1024]{2,0,1:T(8,128)} %get-tuple-element.66) | copy-start | bytes 1572868
  406.9 39.9 %copy-start.11 = (f32[256]{0:T(256)S(1)}, f32[256]{0:T(256)}, u32[]{:S(2)}) copy-start(f32[256]{0:T(256)} %param.27) | copy-start | bytes 3076
  407.0 39.9 %copy-start.12 = (f32[256]{0:T(256)S(1)}, f32[256]{0:T(256)}, u32[]{:S(2)}) copy-start(f32[256]{0:T(256)} %param.35) | copy-start | bytes 3076
  407.0 39.9 %copy-start.13 = (f32[256]{0:T(256)S(1)}, f32[256]{0:T(256)}, u32[]{:S(2)}) copy-start(f32[256]{0:T(256)} %param.34) | copy-start | bytes 3076
  407.0 40.5 %copy-start.4 = (f32[64,1024]{1,0:T(8,128)S(1)}, f32[64,1024]{1,0:T(8,128)}, u32[]{:S(2)}) copy-start(f32[64,1024]{1,0:T(8,128)} %param.26) | copy-start | bytes 786436
  407.0 42.6 %copy-start.6 = (f32[80,128]{1,0:T(8,128)S(1)}, f32[80,128]{1,0:T(8,128)}, u32[]{:S(2)}) copy-start(f32[80,128]{1,0:T(8,128)} %param.25) | copy-start | bytes 122884
  407.0 42.6 %copy-start.8 = (f32[80,128]{1,0:T(8,128)S(1)}, f32[80,128]{1,0:T(8,128)}, u32[]{:S(2)}) copy-start(f32[80,128]{1,0:T(8,128)} %param.31) | copy-start | bytes 122884
  407.0 42.6 %copy-start.9 = (f32[80,128]{1,0:T(8,128)S(1)}, f32[80,128]{1,0:T(8,128)}, u32[]{:S(2)}) copy-start(f32[80,128]{1,0:T(8,128)} %param.30) | copy-start | bytes 122884
Sparse Core Ops, SparseCore 0:
  10.2 36.8 all-gather.3
  49.3 21.0 all-gather.5
  183.0 96.1 all-reduce.6
  281.4 36.3 reduce-scatter.4
  320.4 29.0 reduce-scatter.2
  353.4 47.4 all-reduce.8
where the time goes:
time: 467 us; the launch traced here: 459 us
  matrix products  165 us (35%)
  blocking collectives  86.8 us (19%)
  waiting for transfers between devices  85.7 us (18%)
  local copies, waits for them, and re-layouts  50.7 us (11%)
  other arithmetic  40.2 us (9%)
  between operations  20.4 us (4%)
  starting transfers between devices  9.27 us (2%)
    dot_general x3, matrix products, contract_cols(): lax.dot_general(left, right, (((1,), (1,)), ((), ())), preferred_element_...  55.9 us
    dot_general x4, matrix products, contract_rows(): lax.dot_general(left, right, (((0,), (0,)), ((), ())), preferred_element_...  45.6 us
    reduce_scatter x1, waiting for transfers between devices, local(): lax.psum_scatter(grads[2], 'seq', scatter_dimension=0, tiled=True)  36.5 us
    psum x1, waiting for transfers between devices, local(): owned = lax.psum((parts[0], parts[1], parts[2], parts[3]), 'rep')  32.8 us
    dot_general x1, matrix products, local(): jnp.dot(preceding_rows, past_taps, preferred_element_type=jnp.float32)  27.9 us
    all_gather x1, blocking collectives, local(): lax.all_gather(lowered[3], 'seq', axis=0, tiled=True)  24.6 us
    psum x1, blocking collectives, local(): owned = lax.psum((parts[0], parts[1], parts[2], parts[3]), 'rep')  17.4 us
    psum x1, blocking collectives, local(): total = lax.psum(squares, 'seq')  16.8 us
  transfers between devices with their start and end apart: 9, of which 4 were waited for; matrix products, arithmetic and copies ran while one was open for 37% of the time, Pallas kernels for 0%

commit v1 on v0

v1 whole, which is shorter than its diff:
```python
import functools

import jax
import jax.numpy as jnp
from jax import lax
from jax.experimental import pallas as pl
from jax.experimental.pallas import tpu as pltpu
from jax.sharding import PartitionSpec as P

DILATION_STEP = 512
STEP = 10

beta_one = 0.9
beta_two = 0.999
learn_rate = 0.05
weight_decay = 0.01
epsilon = 1e-08
clip_bound = 1.0

LANES = 128
TILE = 16
AUX = 128
MEL = 80
ONES = 80
KEEP = 81
LINK = 82
ROWS = 512
BF = jnp.bfloat16
F32 = jnp.float32
BOTH = ("rep", "seq")


def from_behind(x, axis, by):
    count = lax.axis_size(axis)
    pairs = [(i, i + by) for i in range(count) if 0 <= i + by < count]
    return lax.ppermute(x, axis, pairs)


def swap(x, rep_bits, seq_bits):
    reps, seqs = lax.axis_size("rep"), lax.axis_size("seq")
    pairs = [
        (r * seqs + s, (r ^ rep_bits) * seqs + (s ^ seq_bits))
        for r in range(reps)
        for s in range(seqs)
    ]
    return lax.ppermute(x, BOTH, pairs)


def nt_dot(left, right):
    return lax.dot_general(
        left, right, (((1,), (1,)), ((), ())), preferred_element_type=F32
    )


def tn_dot(left, right):
    return lax.dot_general(
        left, right, (((0,), (0,)), ((), ())), preferred_element_type=F32
    )


def dot(left, right):
    return jnp.dot(left, right, preferred_element_type=F32)


def params(**more):
    return pltpu.CompilerParams(vmem_limit_bytes=58 * 2**20, **more)


def cost(flops, moved):
    return pl.CostEstimate(flops=int(flops), bytes_accessed=int(moved), transcendentals=0)


def whole(shape):
    return pl.BlockSpec(shape, lambda *_: (0,) * len(shape))


HEAD = 96
QUARTER = 3 * 8 * TILE


def pack_body(where, conv, out, cond, bias, own, first):
    own[0:MEL, :] = cond[...].astype(BF)
    own[MEL:HEAD, :] = jnp.concatenate(
        [bias[...], jnp.zeros((HEAD - MEL - 2, LANES), F32)], 0
    ).astype(BF)
    for k in range(4):
        start = pl.multiple_of((where[1] ^ k) * TILE, TILE)
        base = HEAD + k * QUARTER
        parts = (
            conv[0, pl.ds(start, TILE), :],
            conv[1, pl.ds(start, TILE), :],
            out[pl.ds(start, TILE), :].astype(BF),
        )
        for t, part in enumerate(parts):
            for j in range(8):
                own[pl.ds(base + t * 128 + j * TILE, TILE), :] = part[:, j * LANES : (j + 1) * LANES]
    first[...] = own[0 : HEAD + QUARTER, :]


def pack_weights(where, conv, out, cond, bias):
    spec = pl.BlockSpec(memory_space=pltpu.VMEM)
    return pl.pallas_call(
        pack_body,
        in_specs=[pl.BlockSpec(memory_space=pltpu.SMEM)] + [spec] * 4,
        out_specs=[spec, spec],
        out_shape=[
            jax.ShapeDtypeStruct((HEAD + 4 * QUARTER, LANES), BF),
            jax.ShapeDtypeStruct((HEAD + QUARTER, LANES), BF),
        ],
        compiler_params=params(),
        name="pack_weights",
    )(where, conv, out, cond, bias)


def mixed_block(block):
    low, mid, top = block & 1, (block >> 1) & 1, (block >> 2) & 1
    return low + 4 * mid + 2 * top


def unpack_body(where, *refs):
    owns, stacks, sides = refs[0:2], refs[2:4], (refs[4:7], refs[7:10])
    w, o, bias_out = refs[10:13]
    w[1120:1152, :] = jnp.zeros((32, w.shape[1]), BF)
    blank = jnp.zeros((TILE - 1, LANES), BF)
    for c in range(2):
        for j in range(4):
            shard = 2 * (where[2] ^ j) + (where[0] ^ c)
            small = owns[c][0:HEAD, :] if j == 0 else stacks[c][j - 1, 0:HEAD, :]
            lane = pl.multiple_of(mixed_block(shard) * LANES, LANES)
            w[1024 : 1024 + MEL, pl.ds(lane, LANES)] = small[0:MEL]
            tail = small[MEL:HEAD]

            @pl.when(shard < 4)
            def _():
                for e in range(2):
                    at = pl.multiple_of(mixed_block(2 * shard + e) * LANES, LANES)
                    w[1104:1120, pl.ds(at, LANES)] = jnp.concatenate([tail[e : e + 1], blank], 0)

            @pl.when(shard >= 4)
            def _():
                for e in range(2):
                    at = pl.multiple_of((2 * (shard - 4) + e) * LANES, LANES)
                    bias_out[:, pl.ds(at, LANES)] = jnp.broadcast_to(
                        tail[e : e + 1].astype(F32), (8, LANES)
                    )

            for k in range(4):
                row = pl.multiple_of(64 * shard + TILE * (where[1] ^ k), TILE)
                if j == 0:
                    source = owns[c].at[pl.ds(HEAD + k * QUARTER, QUARTER), :]
                elif k == 0:
                    source = stacks[c].at[j - 1, pl.ds(HEAD, QUARTER), :]
                else:
                    source = sides[c][k - 1].at[pl.ds((j - 1) * QUARTER, QUARTER), :]
                for b in range(8):
                    lanes = pl.ds(mixed_block(b) * LANES, LANES)
                    w[pl.ds(row, TILE), lanes] = source[b * TILE : (b + 1) * TILE, :]
                    w[pl.ds(512 + row, TILE), lanes] = source[128 + b * TILE : 128 + (b + 1) * TILE, :]
                    o[pl.ds(row, TILE), b * LANES : (b + 1) * LANES] = source[
                        256 + b * TILE : 256 + (b + 1) * TILE, :
                    ]


def gather_quarters(where, conv, out, cond, bias):
    own, first = pack_weights(where, conv, out, cond, bias)
    own_other = swap(own, 0, 1)
    along = [swap(first, 0, 2 * j) for j in (1, 2, 3)]
    stack = jnp.stack(along, 0)
    send = stack[:, HEAD:, :].reshape(3 * QUARTER, LANES)
    across = [swap(send, k, 0) for k in (1, 2, 3)]
    stack_other = swap(stack, 0, 1)
    across_other = [swap(a, 0, 1) for a in across]
    spec = pl.BlockSpec(memory_space=pltpu.VMEM)
    return pl.pallas_call(
        unpack_body,
        in_specs=[pl.BlockSpec(memory_space=pltpu.SMEM)] + [spec] * 10,
        out_specs=[spec] * 3,
        out_shape=[
            jax.ShapeDtypeStruct((1024 + AUX, 1024), BF),
            jax.ShapeDtypeStruct((512, 1024), BF),
            jax.ShapeDtypeStruct((8, 1024), F32),
        ],
        compiler_params=params(),
        name="unpack_weights",
    )(where, own, own_other, stack, stack_other, *across, *across_other)


def mixed_columns(x):
    rows, columns = x.shape
    return x.reshape(rows, 2, 2, columns // 4).transpose(0, 2, 1, 3).reshape(rows, columns)


def gather_plain(conv, out_weight, cond_weight, biases):
    conv_all = lax.all_gather(conv, "seq", axis=1, tiled=True)
    cond_all = lax.all_gather(cond_weight.astype(BF), "seq", axis=1, tiled=True)
    out_all = lax.all_gather(out_weight.astype(BF), "seq", axis=0, tiled=True)
    bias_all = lax.all_gather(biases.astype(BF), "seq", axis=0, tiled=True)
    gates = cond_all.shape[1]
    w = jnp.concatenate(
        [
            conv_all[0],
            conv_all[1],
            cond_all,
            bias_all[None, :gates],
            jnp.zeros((AUX - MEL - 1, gates), BF),
        ],
        0,
    )
    bias_out = jnp.broadcast_to(bias_all[None, gates:].astype(F32), (8, gates))
    return mixed_columns(w), out_all, bias_out


def fill_window(xe, x, tail, aux, carry, first):
    rows = x.shape[0]

    @pl.when(first)
    def _():
        carry[...] = tail[...]

    side = aux[...].T
    link = side[:, LINK : LINK + 1]
    xe[:, 0:512] = x[...]
    xe[0:ROWS, 512:1024] = carry[...] * link[0:ROWS]
    if rows > ROWS:
        xe[ROWS:, 512:1024] = x[0 : rows - ROWS, :] * link[ROWS:]
    xe[:, 1024:1152] = side
    carry[...] = x[rows - ROWS :, :]
    return side[:, KEEP : KEEP + 1].astype(F32), link.astype(F32)


def gated(xe, w, o, res, skp, keep):
    half = o.shape[0]
    pre = dot(xe[...], w[...])
    hg = nt_dot(res[...], o[:, 0:512]) + nt_dot(skp[...], o[:, 512:1024])
    filt = jnp.tanh(pre[:, :half])
    gate = 0.5 * jnp.tanh(0.5 * pre[:, half:]) + 0.5
    kept = keep * gate
    hidden = filt * kept
    filt_grad = hg * kept * (1.0 - filt * filt)
    gate_grad = hg * hidden * (1.0 - gate)
    return hidden.astype(BF), jnp.concatenate([filt_grad, gate_grad], 1).astype(BF)


def emit_pieces(where, keep_out, send_out, write):
    for c, dest in ((0, keep_out), (1, send_out)):

        def one(n, carry, c=c, dest=dest):
            k, j = n // 4, n % 4
            shard = 2 * (where[2] ^ j) + (where[0] ^ c)
            write(dest.at[k, j], shard, where[1] ^ k)
            return carry

        lax.fori_loop(0, 16, one, 0)


def put_tiles(dest, base, value):
    value = value.astype(dest.dtype)
    for b in range(value.shape[1] // LANES):
        dest[pl.ds(base + b * TILE, TILE), :] = value[:, b * LANES : (b + 1) * LANES]


def conv_piece(dest, acc, shard, quarter):
    row = pl.multiple_of(64 * shard + TILE * quarter, TILE)
    put_tiles(dest, 0, acc[pl.ds(row, TILE), :])
    put_tiles(dest, 64, acc[pl.ds(512 + row, TILE), :])


def first_body(split, where, x, tail, aux, res, skp, w, o, p, hid, *rest):
    if split:
        keep_out, send_out, aux_grad, sums, xe, carry, acc = rest
    else:
        grad, sums, xe, carry, acc = rest
    step, last = pl.program_id(0), pl.num_programs(0) - 1
    keep, _ = fill_window(xe, x, tail, aux, carry, step == 0)

    @pl.when(step == 0)
    def _():
        acc[...] = jnp.zeros_like(acc)
        sums[...] = jnp.zeros_like(sums)

    hidden, grad_pre = gated(xe, w, o, res, skp, keep)
    hid[...] = hidden
    p[...] = grad_pre
    acc[...] += tn_dot(xe[...], grad_pre)
    for n, part in enumerate((res, skp)):
        total = jnp.sum(part[...].astype(F32), 0, keepdims=True)
        sums[:, n * 512 : (n + 1) * 512] += jnp.broadcast_to(total, (8, 512))

    @pl.when(step == last)
    def _():
        if split:
            aux_grad[...] = acc[1024:1152, :]
            emit_pieces(
                where,
                keep_out,
                send_out,
                lambda dest, shard, quarter: conv_piece(dest, acc, shard, quarter),
            )
        else:
            grad[...] = acc[...]


def second_body(split, where, x, tail, aux, res, skp, w, o, hid_one, p_one, w_past, *rest):
    if split:
        aux_one, sums = rest[:2]
        p, hid, edge, keep_out, send_out, xe, carry, acc, acc_out, small = rest[2:]
    else:
        p, hid, edge, grad, grad_out, xe, carry, acc, acc_out = rest
    step, last = pl.program_id(0), pl.num_programs(0) - 1
    middle = pl.num_programs(0) // 2
    keep, link = fill_window(xe, x, tail, aux, carry, step == 0)

    @pl.when(step == 0)
    def _():
        acc[...] = jnp.zeros_like(acc)
        acc_out[...] = jnp.zeros_like(acc_out)

    hidden, grad_pre = gated(xe, w, o, res, skp, keep)
    hid[...] = hidden
    p[...] = grad_pre
    acc[...] += tn_dot(xe[...], grad_pre)
    both = jnp.concatenate([hid_one[...], hidden], 1)
    acc_out[:, 0:512] += tn_dot(both, res[...])
    acc_out[:, 512:1024] += tn_dot(both, skp[...])

    @pl.when((step == 0) | (step == middle))
    def _():
        cut = w.shape[1]
        past = nt_dot(p_one[...], w_past[...]) + nt_dot(p[0:ROWS, :], w[512:1024, :])
        edge[...] = (past * link[0:ROWS]).astype(BF)[None]

    @pl.when(step == last)
    def _():
        if not split:
            grad[...] = acc[...]
            grad_out[...] = acc_out[...]
            return
        small[...] = jnp.zeros_like(small)
        for s in range(8):
            block = mixed_block(s)
            source = aux_one if block < 4 else acc.at[pl.ds(1024, AUX), :]
            lane = (block % 4) * LANES
            small[s, 0:MEL, :] = source[0:MEL, lane : lane + LANES]
            for e in range(2):
                if s < 4:
                    block = mixed_block(2 * s + e)
                    source = aux_one if block < 4 else acc.at[pl.ds(1024, AUX), :]
                    lane = (block % 4) * LANES
                    line = source[ONES : ONES + 1, lane : lane + LANES]
                else:
                    lane = (2 * (s - 4) + e) * LANES
                    line = sums[0:1, lane : lane + LANES]
                small[s, MEL + e : MEL + e + 1, :] = line

        def write(dest, shard, quarter):
            conv_piece(dest, acc, shard, quarter)
            row = pl.multiple_of(64 * shard + TILE * quarter, TILE)
            put_tiles(dest, 128, acc_out[pl.ds(row, TILE), :])
            dest[256:288, :] = small[shard, pl.ds(pl.multiple_of(32 * quarter, 32), 32), :].astype(
                dest.dtype
            )

        emit_pieces(where, keep_out, send_out, write)


def half_layer(number, split, rows, where, x, tail, aux, res, skp, w, o, extra):
    total = x.shape[0]
    half = o.shape[0] // 2
    wide = 2 * half
    by_row = lambda columns: pl.BlockSpec((rows, columns), lambda i: (i, 0))
    steps = total // rows
    in_specs = [
        pl.BlockSpec(memory_space=pltpu.SMEM),
        by_row(512),
        whole((ROWS, 512)),
        pl.BlockSpec((AUX, rows), lambda i: (0, i)),
        by_row(512),
        by_row(512),
        pl.BlockSpec((1024 + AUX, wide), lambda i: (0, number)),
        pl.BlockSpec((half, 1024), lambda i: (number, 0)),
    ]
    out_specs = [by_row(wide), by_row(half)]
    out_shape = [
        jax.ShapeDtypeStruct((total, wide), BF),
        jax.ShapeDtypeStruct((total, half), BF),
    ]
    scratch = [
        pltpu.VMEM((rows, 1024 + AUX), BF),
        pltpu.VMEM((ROWS, 512), BF),
        pltpu.VMEM((1024 + AUX, wide), F32),
    ]
    units = 2.5 / 2 + 0.5 + 1.125

    def add_out(shape, dtype):
        out_specs.append(whole(shape))
        out_shape.append(jax.ShapeDtypeStruct(shape, dtype))

    if number == 0:
        body = first_body
        if split:
            add_out((4, 4, 128, LANES), F32)
            add_out((4, 4, 128, LANES), BF)
            add_out((AUX, wide), F32)
        else:
            add_out((1024 + AUX, wide), F32)
        add_out((8, 1024), F32)
    else:
        body = second_body
        units += 1
        middle = steps // 2
        in_specs += [
            by_row(half),
            pl.BlockSpec((ROWS, wide), lambda i: (jnp.where(i < middle, 0, middle * (rows // ROWS)), 0)),
            pl.BlockSpec((512, wide), lambda i: (1, 0)),
        ]
        if split:
            in_specs += [whole((AUX, wide)), whole((8, 1024))]
        out_specs.append(pl.BlockSpec((1, ROWS, 512), lambda i: (jnp.where(i < middle, 0, 1), 0, 0)))
        out_shape.append(jax.ShapeDtypeStruct((2, ROWS, 512), BF))
        if split:
            add_out((4, 4, 288, LANES), F32)
            add_out((4, 4, 288, LANES), BF)
        else:
            add_out((1024 + AUX, wide), F32)
            add_out((512, 1024), F32)
        scratch.append(pltpu.VMEM((512, 1024), F32))
        if split:
            scratch.append(pltpu.VMEM((8, AUX, LANES), F32))
    return pl.pallas_call(
        functools.partial(body, split),
        grid=(steps,),
        in_specs=in_specs,
        out_specs=out_specs,
        out_shape=out_shape,
        scratch_shapes=scratch,
        compiler_params=params(),
        cost_estimate=cost(units * 2 * total * 512 * 1024, total * 6000),
        name="half_layer_%d" % number,
    )(where, x, tail, aux, res, skp, w, o, *extra)


def mixed_body(x, one, two, o, bias, residual, skip):
    half = one.shape[1]
    mixed = dot(one[...], o[0:half, :]) + dot(two[...], o[half:, :]) + bias[0:1, :]
    residual[...] = (x[...].astype(F32) + mixed[:, 0:512]).astype(BF)
    skip[...] = mixed[:, 512:1024].astype(BF)


def mixed_layer(rows, x, one, two, o, bias):
    total, half = one.shape
    by_row = lambda columns: pl.BlockSpec((rows, columns), lambda i: (i, 0))
    return pl.pallas_call(
        mixed_body,
        grid=(total // rows,),
        in_specs=[by_row(512), by_row(half), by_row(half), whole((512, 1024)), whole((8, 1024))],
        out_specs=[by_row(512), by_row(512)],
        out_shape=[jax.ShapeDtypeStruct((total, 512), BF)] * 2,
        compiler_params=params(),
        cost_estimate=cost(2 * total * 512 * 1024, total * 4096),
        name="mixed_layer",
    )(x, one, two, o, bias)


def input_body(res, one, two, flags, w, edge, *rest):
    out, carry = rest[-2:]
    step = pl.program_id(0)
    rows = res.shape[0]
    wide = one.shape[1]

    @pl.when(step == 0)
    def _():
        carry[...] = edge[0]

    link = flags[...].T[:, LINK - MEL : LINK - MEL + 1].astype(F32)
    both = nt_dot(one[...], w[:, 0:wide]) + nt_dot(two[...], w[:, wide:])
    past = both[:, 512:1024] * link
    now = res[...].astype(F32) + both[:, 0:512]
    if rows > ROWS:
        out[0 : rows - ROWS, :] = (now[0 : rows - ROWS] + past[ROWS:]).astype(BF)
    out[rows - ROWS :, :] = (now[rows - ROWS :] + carry[...].astype(F32)).astype(BF)
    carry[...] = past[0:ROWS].astype(BF)


def input_layer(rows, part, parts, res, one, two, aux, w, edge, number, partial):
    total, wide = one.shape
    steps = total // rows // parts
    at = lambda i: steps * (part + 1) - 1 - i
    by_row = lambda columns: pl.BlockSpec((rows, columns), lambda i: (at(i), 0))
    in_specs = [
        by_row(512),
        by_row(wide),
        by_row(wide),
        pl.BlockSpec((TILE, rows), lambda i: (MEL // TILE, at(i))),
        pl.BlockSpec((1024, 2 * wide), lambda i: (0, 0)),
        pl.BlockSpec((1, ROWS, 512), lambda i: (number, 0, 0)),
    ]
    operands = [res, one, two, aux, w, edge]
    aliases = {}
    if partial is not None:
        in_specs.append(pl.BlockSpec(memory_space=pl.ANY))
        operands.append(partial)
        aliases = {6: 0}
    return pl.pallas_call(
        input_body,
        grid=(steps,),
        in_specs=in_specs,
        out_specs=by_row(512),
        out_shape=jax.ShapeDtypeStruct((total, 512), BF),
        scratch_shapes=[pltpu.VMEM((ROWS, 512), BF)],
        input_output_aliases=aliases,
        compiler_params=params(),
        cost_estimate=cost(4 * total * 512 * 1024 // parts, total * 4096 // parts),
        name="input_layer_%d" % part,
    )(*operands)


def between_cores(keep, send):
    return keep + swap(send, 0, 1).astype(F32)


def across_rep(total):
    got = [swap(total[k].astype(BF), k, 0) for k in (1, 2, 3)]
    return total[0], got


def along_z(total):
    got = [swap(total[j].astype(BF), 0, 2 * j) for j in (1, 2, 3)]
    return total[0], got


def gather_rep(piece):
    return [piece] + [swap(piece, k, 0) for k in (1, 2, 3)]


def add_up(kept, got):
    return kept + got[0].astype(F32) + got[1].astype(F32) + got[2].astype(F32)


def rebuild_body(where, *refs):
    ones, twos = refs[0:4], refs[4:8]
    conv, out, cond, bias, square, small = refs[8:]
    for k in range(4):
        quarter = where[1] ^ k
        row = pl.multiple_of(quarter * TILE, TILE)
        for t in range(2):
            for b in range(4):
                lane = (b & 1) * LANES + (b >> 1) * 512
                conv[t, pl.ds(row, TILE), pl.ds(lane, LANES)] = ones[k][
                    t * 64 + b * TILE : t * 64 + (b + 1) * TILE, :
                ]
                conv[t, pl.ds(row, TILE), pl.ds(lane + 256, LANES)] = twos[k][
                    t * 64 + b * TILE : t * 64 + (b + 1) * TILE, :
                ]
        for b in range(8):
            out[pl.ds(row, TILE), b * LANES : (b + 1) * LANES] = twos[k][
                128 + b * TILE : 128 + (b + 1) * TILE, :
            ]
        small[pl.ds(pl.multiple_of(quarter * 32, 32), 32), :] = twos[k][256:288, :]
    cond[...] = small[0:MEL, :]
    bias[...] = small[MEL : MEL + 2, :]
    total = (
        jnp.sum(conv[...] * conv[...])
        + jnp.sum(out[...] * out[...])
        + jnp.sum(cond[...] * cond[...])
        + jnp.sum(bias[...] * bias[...])
    )
    square[...] = jnp.full((8, LANES), total, F32)


def rebuild(where, ones, twos):
    spec = pl.BlockSpec(memory_space=pltpu.VMEM)
    return pl.pallas_call(
        rebuild_body,
        in_specs=[pl.BlockSpec(memory_space=pltpu.SMEM)] + [spec] * 8,
        out_specs=[spec] * 5,
        out_shape=[
            jax.ShapeDtypeStruct((2, 64, 1024), F32),
            jax.ShapeDtypeStruct((64, 1024), F32),
            jax.ShapeDtypeStruct((MEL, LANES), F32),
            jax.ShapeDtypeStruct((2, LANES), F32),
            jax.ShapeDtypeStruct((8, LANES), F32),
        ],
        scratch_shapes=[pltpu.VMEM((AUX, LANES), F32)],
        compiler_params=params(),
        name="rebuild",
    )(where, *ones, *twos)


def adamw_update(grad, moment, second, weight, factor, decay):
    clipped = grad * factor
    moment_new = beta_one * moment + (1.0 - beta_one) * clipped
    second_new = beta_two * second + (1.0 - beta_two) * clipped * clipped
    mean_hat = moment_new / (1.0 - beta_one**STEP)
    square_hat = second_new / (1.0 - beta_two**STEP)
    weight_new = weight - learn_rate * (
        mean_hat / (jnp.sqrt(square_hat) + epsilon) + decay * weight
    )
    return (moment_new, second_new, weight_new)


def local(
    inputs,
    mel_frames,
    utterance,
    keep_mask,
    res_grad,
    skip_grad,
    conv_weight,
    cond_weight,
    out_weight,
    biases,
    conv_first,
    conv_second,
    cond_first,
    cond_second,
    out_first,
    out_second,
    bias_first,
    bias_second,
):
    rows, width = inputs.shape
    span = DILATION_STEP
    split = lax.axis_size("rep") == 4 and lax.axis_size("seq") == 8
    seq, rep = lax.axis_index("seq"), lax.axis_index("rep")
    where = jnp.stack([seq % 2, rep, seq // 2]).astype(jnp.int32)

    conv_low = conv_weight.astype(BF).transpose(1, 0, 2)
    if split:
        w, o, bias_out = gather_quarters(
            where, conv_low, out_weight, cond_weight, biases.reshape(2, LANES)
        )
    else:
        w, o, bias_out = gather_plain(conv_low, out_weight, cond_weight, biases)

    tail = from_behind(inputs[rows - span :], BOTH, 1)
    prev_ids = from_behind(utterance[rows - span :], BOTH, 1)
    index = lax.axis_index(BOTH)
    shifted_ids = jnp.concatenate([prev_ids, utterance[: rows - span]], 0)
    linked = shifted_ids == utterance
    linked = linked & ((jnp.arange(rows) >= span) | (index > 0))
    aux = jnp.concatenate(
        [
            mel_frames,
            jnp.ones((1, rows), BF),
            keep_mask.astype(BF)[None],
            linked.astype(BF)[None],
            jnp.zeros((AUX - MEL - 3, rows), BF),
        ],
        0,
    )

    tile = 512
    if split:
        p_one, hid_one, keep_one, send_one, aux_one, sums = half_layer(
            0, split, tile, where, inputs, tail, aux, res_grad, skip_grad, w, o, ()
        )
        one = between_cores(keep_one, send_one)
        one = across_rep(one)
        p_two, hid_two, edge, keep_two, send_two = half_layer(
            1, split, tile, where, inputs, tail, aux, res_grad, skip_grad, w, o,
            (hid_one, p_one, w, aux_one, sums),
        )
    else:
        p_one, hid_one, grad_one, sums = half_layer(
            0, split, tile, where, inputs, tail, aux, res_grad, skip_grad, w, o, ()
        )
        p_two, hid_two, edge, grad_two, grad_out = half_layer(
            1, split, tile, where, inputs, tail, aux, res_grad, skip_grad, w, o,
            (hid_one, p_one, w),
        )

    returned = from_behind(edge[0], BOTH, -1)[None]
    if split:
        two = across_rep(between_cores(keep_two, send_two))
    input_part = input_layer(tile, 0, 2, res_grad, p_one, p_two, aux, w, edge, 1, None)
    if split:
        one = along_z(add_up(*one))
        two = along_z(add_up(*two))
    residual_out, skip_out = mixed_layer(tile, inputs, hid_one, hid_two, o, bias_out)
    if split:
        one = gather_rep(add_up(*one))
        two = gather_rep(add_up(*two))
    input_grad = input_layer(
        tile, 1, 2, res_grad, p_one, p_two, aux, w, returned, 0, input_part
    )

    if split:
        own_conv, own_out, own_cond, own_bias, square = rebuild(where, one, two)
        own_conv = own_conv.transpose(1, 0, 2)
        own_bias = own_bias.reshape(-1)
        parts = [[swap(square, 0, 2 * j + c) if j + c else square for c in (0, 1)] for j in range(4)]
        pairs = [(a + b)[0, 0] for a, b in parts]
        total = (pairs[0] + pairs[1]) + (pairs[2] + pairs[3])
    else:
        unmix = lambda g: mixed_columns(g)
        grad = unmix(jnp.concatenate([grad_one, grad_two], 1))
        grad_conv = jnp.stack([grad[0:512], grad[512:1024]], 1)
        grad_bias = jnp.concatenate([grad[1024 + ONES], sums[0]], 0)
        own = (
            lax.psum_scatter(grad_conv, "seq", scatter_dimension=0, tiled=True),
            lax.psum_scatter(grad[1024 : 1024 + MEL], "seq", scatter_dimension=1, tiled=True),
            lax.psum_scatter(grad_out, "seq", scatter_dimension=0, tiled=True),
            lax.psum_scatter(grad_bias, "seq", scatter_dimension=0, tiled=True),
        )
        own_conv, own_cond, own_out, own_bias = lax.psum(own, "rep")
        squares = (
            jnp.sum(own_conv * own_conv)
            + jnp.sum(own_cond * own_cond)
            + jnp.sum(own_out * own_out)
            + jnp.sum(own_bias * own_bias)
        )
        total = lax.psum(squares, "seq")

    grad_norm = jnp.sqrt(total)
    factor = clip_bound / jnp.maximum(grad_norm, clip_bound)
    conv_new = adamw_update(own_conv, conv_first, conv_second, conv_weight, factor, weight_decay)
    cond_new = adamw_update(own_cond, cond_first, cond_second, cond_weight, factor, weight_decay)
    out_new = adamw_update(own_out, out_first, out_second, out_weight, factor, weight_decay)
    bias_new = adamw_update(own_bias, bias_first, bias_second, biases, factor, 0.0)
    return (
        residual_out,
        skip_out,
        input_grad,
        grad_norm,
        *conv_new,
        *cond_new,
        *out_new,
        *bias_new,
    )


def solution(mesh):
    rows = P(BOTH, None)
    line = P(BOTH)
    conv = P("seq", None, None)
    cond = P(None, "seq")
    out = P("seq", None)
    bias = P("seq")
    placed = (
        rows,
        P(None, BOTH),
        line,
        line,
        rows,
        rows,
        conv,
        cond,
        out,
        bias,
        conv,
        conv,
        cond,
        cond,
        out,
        out,
        bias,
        bias,
    )
    return jax.shard_map(
        local,
        mesh=mesh,
        in_specs=placed,
        out_specs=(rows, rows, rows, P()) + (conv,) * 3 + (cond,) * 3 + (out,) * 3 + (bias,) * 3,
        check_vma=False,
    )
```

time: 467 us -> 243 us (0.52); the launches traced: 459 us -> 241 us
  matrix products: 165 us -> 0 us
  Pallas kernels: 0 us -> 130 us
  blocking collectives: 86.8 us -> 0 us
  waiting for transfers between devices: 85.7 us -> 21.6 us
  starting transfers between devices: 9.27 us -> 58.2 us
  other arithmetic: 40.2 us -> 4.54 us
  local copies, waits for them, and re-layouts: 50.7 us -> 21.7 us
  between operations: 20.4 us -> 5.03 us
    dot_general x11 -> x0, matrix products: 165 us -> none  [the longest x3 55.9 us: contract_cols(): lax.dot_general(left, right, (((1,), (1,)), ((), ())), preferred_element_...]
    pallas_call x0 -> x8, Pallas kernels: none -> 130 us  [the longest x2 84.2 us: half_layer(): pl.pallas_call(functools.partial(body, split), grid=(steps,), in_specs=in...]
    ppermute x0 -> x38, starting transfers between devices: none -> 50.1 us  [swap(): return lax.ppermute(x, BOTH, pairs)]
    reduce_scatter x2 -> x0, waiting for transfers between devices: 46.5 us -> none  [the longest x1 36.5 us: local(): lax.psum_scatter(grads[2], 'seq', scatter_dimension=0, tiled=True)]
    all_gather x2 -> x0, blocking collectives: 37.7 us -> none  [the longest x1 24.6 us: local(): lax.all_gather(lowered[3], 'seq', axis=0, tiled=True)]
    psum x2 -> x0, blocking collectives: 34.2 us -> none  [the longest x1 17.4 us: local(): owned = lax.psum((parts[0], parts[1], parts[2], parts[3]), 'rep')]
    psum x1 -> x0, waiting for transfers between devices: 32.8 us -> none  [local(): owned = lax.psum((parts[0], parts[1], parts[2], parts[3]), 'rep')]
    slice x7, local copies, waits for them, and re-layouts: 25.1 us -> 3.16 us  [the longest x4 2.06 us: local(): pairs = [(a + b)[0, 0] for a, b in parts]]
  transfers between devices with their start and end apart: 9 -> 41, of which waited for: 4 -> 12; matrix products, arithmetic and copies ran while one was open for 37% -> 6% of each run, Pallas kernels for 0% -> 18%
where the time goes in v1:
time: 243 us; the launch traced here: 241 us
  Pallas kernels  130 us (53%)
  starting transfers between devices  58.2 us (24%)
  local copies, waits for them, and re-layouts  21.7 us (9%)
  waiting for transfers between devices  21.6 us (9%)
  between operations  5.03 us (2%)
  other arithmetic  4.54 us (2%)
    pallas_call x2, Pallas kernels, half_layer(): pl.pallas_call(functools.partial(body, split), grid=(steps,), in_specs=in...  84.2 us
    ppermute x38, starting transfers between devices, swap(): return lax.ppermute(x, BOTH, pairs)  50.1 us
    pallas_call x2, Pallas kernels, input_layer(): pl.pallas_call(input_body, grid=(steps,), in_specs=in_specs, out_specs=by...  22.2 us
    ppermute x38, waiting for transfers between devices, swap(): return lax.ppermute(x, BOTH, pairs)  21.6 us
    pallas_call x1, Pallas kernels, mixed_layer(): pl.pallas_call(mixed_body, grid=(total // rows,), in_specs=[by_row(512),...  15.1 us
    concatenate x1, local copies, waits for them, and re-layouts, local(): jnp.concatenate([mel_frames, jnp.ones((1, rows), BF), keep_mask.astype(BF...  9.36 us
    ppermute x3, starting transfers between devices, from_behind(): return lax.ppermute(x, axis, pairs)  8.11 us
    unnamed x78, local copies, waits for them, and re-layouts  7.09 us
  transfers between devices with their start and end apart: 41, of which 12 were waited for; matrix products, arithmetic and copies ran while one was open for 6% of the time, Pallas kernels for 18%

profile of v1, /device:TPU:0, one launch (start us, length us, event | category | flops | bytes accessed | tf_op | source)
XLA Modules:
  0.0 241.2 jit_solution(9333526082245326693)
XLA Ops:
  0.7 2.0 copy.55
  3.3 1.9 pack_weights.1
  5.1 3.0 %collective-permute-start.3 = (bf16[480,128]{1,0:T(8,128)(2,1)}, bf16[480,128]{1,0:T(8,128)(2,1)S(1)}, u32[]{:S(2)}, u32[]{:S(2)}) collective-permute-start(bf16[480,128]{1,0:T(8,128)(2,1)} %get-tuple-element.40), channel_id=1, source_target_pairs={{0,2},{1,3},{2,0},{3,1},{4,6},{5,7},{6,4},{7,5},{8,10},{9,11},{10,... | collective-permute-start | bytes 368648 | tf_op jit(solution)/shard_map/ppermute | solution.py:46
  8.2 2.6 %collective-permute-start.4 = (bf16[480,128]{1,0:T(8,128)(2,1)}, bf16[480,128]{1,0:T(8,128)(2,1)S(1)}, u32[]{:S(2)}, u32[]{:S(2)}) collective-permute-start(bf16[480,128]{1,0:T(8,128)(2,1)} %get-tuple-element.40), channel_id=1, source_target_pairs={{0,4},{1,5},{2,6},{3,7},{4,0},{5,1},{6,2},{7,3},{8,12},{9,13},{10,... | collective-permute-start | bytes 368648 | tf_op jit(solution)/shard_map/ppermute | solution.py:46
  10.8 2.3 collective-permute-done.3
  13.0 7.7 %collective-permute-done.4 = bf16[480,128]{1,0:T(8,128)(2,1)S(1)} collective-permute-done((bf16[480,128]{1,0:T(8,128)(2,1)}, bf16[480,128]{1,0:T(8,128)(2,1)S(1)}, u32[]{:S(2)}, u32[]{:S(2)}) %collective-permute-start.4) | collective-permute-done | bytes 122912 | tf_op jit(solution)/shard_map/ppermute | solution.py:46
  20.8 1.6 collective-permute-start.7
  22.4 1.5 collective-permute-start.8
  24.4 1.3 collective-permute-start.1
  25.6 1.1 slice.87
  26.7 5.3 %collective-permute-start = (bf16[512,512]{1,0:T(8,128)(2,1)S(1)}, bf16[512,512]{1,0:T(8,128)(2,1)}, u32[]{:S(2)}, u32[]{:S(2)}) collective-permute-start(bf16[512,512]{1,0:T(8,128)(2,1)S(1)} %slice.87), channel_id=1, source_target_pairs={{0,1},{1,2},{2,3},{3,4},{4,5},{5,6},{6,7},{7,8},{8,9},{9,10},{10,1... | collective-permute-start | bytes 1572872 | tf_op jit(solution)/shard_map/ppermute | solution.py:36
  32.1 1.2 collective-permute-start.6
  33.2 1.6 collective-permute-done.8.refs_5_
  37.4 9.4 %concatenate.7.aux.flags = bf16[128,6144]{1,0:T(8,128)(2,1)} concatenate(bf16[80,6144]{1,0:T(8,128)(2,1)S(1)} %copy-done.6, bf16[1,6144]{1,0:T(2,128)(2,1)} %broadcast_in_dim.18, bf16[1,6144]{1,0:T(2,128)(2,1)} %broadcast_in_dim.19, bf16[1,6144]{1,0:T(2,128)(2,1)} %reshape.59, bf16[45,6144]{1,0:T(8,128)(2,1)S(1)} %broadcast_in_dim.22), dimensions={0} | concatenate | bytes 3145728 | tf_op jit(solution)/shard_map/concatenate | solution.py:641
  47.5 4.5 %unpack_weights.1 = (bf16[1152,1024]{1,0:T(8,128)(2,1)}, bf16[512,1024]{1,0:T(8,128)(2,1)}, f32[8,1024]{1,0:T(8,128)}) custom-call(s32[3]{0:T(128)} %pad_add_fusion.where, bf16[1632,128]{1,0:T(8,128)(2,1)} %get-tuple-element.39.refs_0_, bf16[1632,128]{1,0:T(8,128)(2,1)} %copy-done.12, bf16[3,480,128]{2,1,0:T(8,128)(2,1)} %copy-done, ...), custom_call_target="tpu_custom_call" | custom-call | tf_op jit(solution)/shard_map/unpack_weights/pallas_call | solution.py:174
  52.1 37.7 %half_layer_0.1 = (bf16[6144,512]{1,0:T(8,128)(2,1)}, bf16[6144,256]{1,0:T(8,128)(2,1)}, f32[4,4,128,128]{3,2,1,0:T(8,128)}, bf16[4,4,128,128]{3,2,1,0:T(8,128)(...) custom-call(s32[3]{0:T(128)} %pad_add_fusion.where, bf16[6144,512]{1,0:T(8,128)(2,1)} %x.5, ...), custom_call_target="tpu_custom_call" | custom-call | flops 18522046464 | bytes 36864000 | tf_op jit(solution)/shard_map/half_layer_0/pallas_call | solution.py:429
  89.8 46.5 %half_layer_1.1 = (bf16[6144,512]{1,0:T(8,128)(2,1)}, bf16[6144,256]{1,0:T(8,128)(2,1)}, bf16[2,512,512]{2,1,0:T(8,128)(2,1)}, f32[4,4,288,128]{3,2,1,0:T(8,128)}, bf16[4,4,288,128]{3,2,1,0:T(8,128)(2,1)}) custom-call(s32[3]{0:T(128)} %pad_add_fusion.where, bf16[6144,512]{1,0:T(8,128)(2,1)} %x.5, bf16[512,512]{1,0:T(8,128)(2,1)} %collective-permute-done.tail, ...), custom_call_target="tpu_custom_call" | custom-call | flops 24964497408 | bytes 36864000 | tf_op jit(solution)/shard_map/half_layer_1/pallas_call | solution.py:429
  136.9 11.1 %input_layer_0.1.rest_0_ = bf16[6144,512]{1,0:T(8,128)(2,1)} custom-call(bf16[6144,512]{1,0:T(8,128)(2,1)} %res.7, bf16[6144,512]{1,0:T(8,128)(2,1)} %get-tuple-element.44.p_one.one, bf16[6144,512]{1,0:T(8,128)(2,1)} %get-tuple-element.51.two, bf16[128,6144]{1,0:T(8,128)(2,1)} %concatenate.7.aux.flags, bf16[1152,1024]{1,0:T(8,128)(2,1)} %get-tuple-element.41.w.w_past, ...), custom_call_target="tpu_custom_call" | custom-call | flops 6442450944 | bytes 12582912 | tf_op jit(solution)/shard_map/input_layer_0/pallas_call | solution.py:503
  148.2 1.2 collective-permute-start.15
  149.4 1.5 collective-permute-start.16
  152.3 1.2 collective-permute-start.25
  153.5 1.5 collective-permute-start.26
  154.9 1.2 collective-permute-start.27
  156.7 2.3 collective-permute-done.17
  159.1 2.4 collective-permute-start.18
  161.4 3.2 %collective-permute-start.19 = (bf16[128,128]{1,0:T(8,128)(2,1)S(1)}, bf16[128,128]{1,0:T(8,128)(2,1)S(1)}, u32[]{:S(2)}, u32[]{:S(2)}) collective-permute-start(bf16[128,128]{1,0:T(8,128)(2,1)S(1)} %get-tuple-element.109), channel_id=1, source_target_pairs={{0,4},{1,5},{2,6},{3,7},{4,0},{5,1},{6,2},{7,3},{8,12},{9,13},{10,... | collective-permute-start | bytes 98312 | tf_op jit(solution)/shard_map/ppermute | solution.py:46
  164.7 4.3 %collective-permute-start.20 = (bf16[128,128]{1,0:T(8,128)(2,1)S(1)}, bf16[128,128]{1,0:T(8,128)(2,1)S(1)}, u32[]{:S(2)}, u32[]{:S(2)}) collective-permute-start(bf16[128,128]{1,0:T(8,128)(2,1)S(1)} %get-tuple-element.108), channel_id=1, source_target_pairs={{0,6},{1,7},{2,4},{3,5},{4,2},{5,3},{6,0},{7,1},{8,14},{9,15},{10,... | collective-permute-start | bytes 98312 | tf_op jit(solution)/shard_map/ppermute | solution.py:46
  169.1 1.7 collective-permute-done.27
  171.0 2.7 %collective-permute-start.28 = (bf16[288,128]{1,0:T(8,128)(2,1)S(1)}, bf16[288,128]{1,0:T(8,128)(2,1)S(1)}, u32[]{:S(2)}, u32[]{:S(2)}) collective-permute-start(bf16[288,128]{1,0:T(8,128)(2,1)S(1)} %get-tuple-element.104), channel_id=1, source_target_pairs={{0,2},{1,3},{2,0},{3,1},{4,6},{5,7},{6,4},{7,5},{8,10},{9,11},{10,... | collective-permute-start | bytes 221192 | tf_op jit(solution)/shard_map/ppermute | solution.py:46
  173.7 2.9 %collective-permute-start.29 = (bf16[288,128]{1,0:T(8,128)(2,1)S(1)}, bf16[288,128]{1,0:T(8,128)(2,1)S(1)}, u32[]{:S(2)}, u32[]{:S(2)}) collective-permute-start(bf16[288,128]{1,0:T(8,128)(2,1)S(1)} %get-tuple-element.106), channel_id=1, source_target_pairs={{0,4},{1,5},{2,6},{3,7},{4,0},{5,1},{6,2},{7,3},{8,12},{9,13},{10,... | collective-permute-start | bytes 221192 | tf_op jit(solution)/shard_map/ppermute | solution.py:46
  177.4 1.5 collective-permute-start.22
  178.9 1.3 collective-permute-start.23
  180.2 1.2 collective-permute-done.29
  181.4 1.4 collective-permute-done.30
  183.3 1.4 collective-permute-start.32
  184.7 1.7 collective-permute-start.33
  186.5 1.5 collective-permute-start.13
  189.1 1.7 collective-permute-done.33.refs_7_
  191.5 2.2 rebuild.1
  193.7 3.9 %collective-permute-start.39 = (f32[8,128]{1,0:T(8,128)}, f32[8,128]{1,0:T(8,128)S(1)}, u32[]{:S(2)}, u32[]{:S(2)}) collective-permute-start(f32[8,128]{1,0:T(8,128)} %get-tuple-element.57), channel_id=1, source_target_pairs={{0,6},{1,7},{2,4},{3,5},{4,2},{5,3},{6,0},{7,1},{8,14},{9,15},{10,... | collective-permute-start | bytes 12296 | tf_op jit(solution)/shard_map/ppermute | solution.py:46
  197.6 15.1 %mixed_layer.1 = (bf16[6144,512]{1,0:T(8,128)(2,1)}, bf16[6144,512]{1,0:T(8,128)(2,1)}) custom-call(bf16[6144,512]{1,0:T(8,128)(2,1)} %x.5, bf16[6144,256]{1,0:T(8,128)(2,1)} %get-tuple-element.43.hid_one.one, bf16[6144,256]{1,0:T(8,128)(2,1)} %get-tuple-element.47.two, bf16[512,1024]{1,0:T(8,128)(2,1)} %get-tuple-element.42.o, f32[8,1024]{1,0:T(8,128)} %get-tuple-element.48.bias), custom_call_target="tpu_custom_call" | custom-call | flops 6442450944 | bytes 25165824 | tf_op jit(solution)/shard_map/mixed_layer/pallas_call | solution.py:452
  213.2 1.9 collective-permute-start.38
  215.1 1.8 collective-permute-start.35
  217.3 11.1 %input_layer_1.1 = bf16[6144,512]{1,0:T(8,128)(2,1)} custom-call(bf16[6144,512]{1,0:T(8,128)(2,1)} %res.7, bf16[6144,512]{1,0:T(8,128)(2,1)} %get-tuple-element.44.p_one.one, bf16[6144,512]{1,0:T(8,128)(2,1)} %get-tuple-element.51.two, bf16[128,6144]{1,0:T(8,128)(2,1)} %concatenate.7.aux.flags, ...), custom_call_target="tpu_custom_call", output_to_operand_aliasing={{}: (6, {})} | custom-call | flops 6442450944 | bytes 12582912 | tf_op jit(solution)/shard_map/input_layer_1/pallas_call | solution.py:503
  234.1 1.2 copy.40
  235.3 1.2 copy.41
  236.5 1.2 copy.42
  238.4 1.0 multiply_subtract_fusion.1
  (155 shorter events, 15.7 us)
Async XLA Ops:
  0.6 23.7 %copy-start.23 = (s32[6144]{0:T(1024)S(1)}, s32[6144]{0:T(1024)}, u32[]{:S(2)}) copy-start(s32[6144]{0:T(1024)} %param.20) | copy-start | bytes 73732
  0.7 34.8 %copy-start.30 = (s32[6144]{0:T(1024)S(1)}, s32[6144]{0:T(1024)}, u32[]{:S(2)}) copy-start(s32[6144]{0:T(1024)} %param.21) | copy-start | bytes 73732
  0.7 36.8 %copy-start.6 = (bf16[80,6144]{1,0:T(8,128)(2,1)S(1)}, bf16[80,6144]{1,0:T(8,128)(2,1)}, u32[]{:S(2)}) copy-start(bf16[80,6144]{1,0:T(8,128)(2,1)} %param.19) | copy-start | bytes 2949124
  5.1 7.9 %collective-permute-start.3 = (bf16[480,128]{1,0:T(8,128)(2,1)}, bf16[480,128]{1,0:T(8,128)(2,1)S(1)}, u32[]{:S(2)}, u32[]{:S(2)}) collective-permute-start(bf16[480,128]{1,0:T(8,128)(2,1)} %get-tuple-element.40), channel_id=1, source_target_pairs={{0,2},{1,3},{2,0},{3,1},{4,6},{5,7},{6,4},{7,5},{8,10},{9,11},{10,... | collective-permute-start | bytes 368648 | tf_op jit(solution)/shard_map/ppermute | solution.py:46
  8.2 12.5 %collective-permute-start.4 = (bf16[480,128]{1,0:T(8,128)(2,1)}, bf16[480,128]{1,0:T(8,128)(2,1)S(1)}, u32[]{:S(2)}, u32[]{:S(2)}) collective-permute-start(bf16[480,128]{1,0:T(8,128)(2,1)} %get-tuple-element.40), channel_id=1, source_target_pairs={{0,4},{1,5},{2,6},{3,7},{4,0},{5,1},{6,2},{7,3},{8,12},{9,13},{10,... | collective-permute-start | bytes 368648 | tf_op jit(solution)/shard_map/ppermute | solution.py:46
  10.8 9.9 %collective-permute-start.5 = (bf16[480,128]{1,0:T(8,128)(2,1)}, bf16[480,128]{1,0:T(8,128)(2,1)S(1)}, u32[]{:S(2)}, u32[]{:S(2)}) collective-permute-start(bf16[480,128]{1,0:T(8,128)(2,1)} %get-tuple-element.40), channel_id=1, source_target_pairs={{0,6},{1,7},{2,4},{3,5},{4,2},{5,3},{6,0},{7,1},{8,14},{9,15},{10,... | collective-permute-start | bytes 368648 | tf_op jit(solution)/shard_map/ppermute | solution.py:46
  10.8 24.6 %collective-permute-start.2 = (bf16[1632,128]{1,0:T(8,128)(2,1)}, bf16[1632,128]{1,0:T(8,128)(2,1)S(1)}, u32[]{:S(2)}, u32[]{:S(2)}) collective-permute-start(bf16[1632,128]{1,0:T(8,128)(2,1)} %get-tuple-element.39.refs_0_), channel_id=1, source_target_pairs={{0,1},{1,0},{2,3},{3,2},{4,5},{5,4},{6,7},{7,6},{8,9},{9,8},{10,11... | collective-permute-start | bytes 1253384 | tf_op jit(solution)/shard_map/ppermute | solution.py:46
  20.8 26.0 %copy-start = (bf16[3,480,128]{2,1,0:T(8,128)(2,1)}, bf16[3,480,128]{2,1,0:T(8,128)(2,1)S(1)}, u32[]{:S(2)}) copy-start(bf16[3,480,128]{2,1,0:T(8,128)(2,1)S(1)} %pad_maximum_fusion.refs_2_) | copy-start | bytes 1105924
  20.8 11.3 %collective-permute-start.7 = (bf16[1152,128]{1,0:T(8,128)(2,1)S(1)}, bf16[1152,128]{1,0:T(8,128)(2,1)S(1)}, u32[]{:S(2)}, u32[]{:S(2)}) collective-permute-start(bf16[1152,128]{1,0:T(8,128)(2,1)S(1)} %bitcast.90), channel_id=1, source_target_pairs={{0,8},{1,9},{2,10},{3,11},{4,12},{5,13},{6,14},{7,15},{8,0},{9,1},... | collective-permute-start | bytes 884744 | tf_op jit(solution)/shard_map/ppermute | solution.py:46
  22.4 12.5 %collective-permute-start.8 = (bf16[1152,128]{1,0:T(8,128)(2,1)S(1)}, bf16[1152,128]{1,0:T(8,128)(2,1)}, u32[]{:S(2)}, u32[]{:S(2)}) collective-permute-start(bf16[1152,128]{1,0:T(8,128)(2,1)S(1)} %bitcast.91), channel_id=1, source_target_pairs={{0,16},{1,17},{2,18},{3,19},{4,20},{5,21},{6,22},{7,23},{8,24},{9,... | collective-permute-start | bytes 884744 | tf_op jit(solution)/shard_map/ppermute | solution.py:46
  23.9 11.0 %collective-permute-start.9 = (bf16[1152,128]{1,0:T(8,128)(2,1)S(1)}, bf16[1152,128]{1,0:T(8,128)(2,1)}, u32[]{:S(2)}, u32[]{:S(2)}) collective-permute-start(bf16[1152,128]{1,0:T(8,128)(2,1)S(1)} %bitcast.92), channel_id=1, source_target_pairs={{0,24},{1,25},{2,26},{3,27},{4,28},{5,29},{6,30},{7,31},{8,16},{9,... | collective-permute-start | bytes 884744 | tf_op jit(solution)/shard_map/ppermute | solution.py:46
  24.4 2.4 collective-permute-start.1
  26.7 25.3 %collective-permute-start = (bf16[512,512]{1,0:T(8,128)(2,1)S(1)}, bf16[512,512]{1,0:T(8,128)(2,1)}, u32[]{:S(2)}, u32[]{:S(2)}) collective-permute-start(bf16[512,512]{1,0:T(8,128)(2,1)S(1)} %slice.87), channel_id=1, source_target_pairs={{0,1},{1,2},{2,3},{3,4},{4,5},{5,6},{6,7},{7,8},{8,9},{9,10},{10,1... | collective-permute-start | bytes 1572872 | tf_op jit(solution)/shard_map/ppermute | solution.py:36
  32.1 14.7 %collective-permute-start.6 = (bf16[3,480,128]{2,1,0:T(8,128)(2,1)S(1)}, bf16[3,480,128]{2,1,0:T(8,128)(2,1)S(1)}, u32[]{:S(2)}, u32[]{:S(2)}) collective-permute-start(bf16[3,480,128]{2,1,0:T(8,128)(2,1)S(1)} %pad_maximum_fusion.refs_2_), channel_id=1, source_target_pairs={{0,1},{1,0},{2,3},{3,2},{4,5},{5,4},{6,7},{7,6},{8,9},{9,8},{10,11... | collective-permute-start | bytes 1105928 | tf_op jit(solution)/shard_map/ppermute | solution.py:46
  34.9 11.9 %collective-permute-start.10 = (bf16[1152,128]{1,0:T(8,128)(2,1)S(1)}, bf16[1152,128]{1,0:T(8,128)(2,1)}, u32[]{:S(2)}, u32[]{:S(2)}) collective-permute-start(bf16[1152,128]{1,0:T(8,128)(2,1)S(1)} %collective-permute-done.7.refs_4_), channel_id=1, source_target_pairs={{0,1},{1,0},{2,3},{3,2},{4,5},{5,4},{6,7},{7,6},{8,9},{9,8},{10,11... | collective-permute-start | bytes 884744 | tf_op jit(solution)/shard_map/ppermute | solution.py:46
  34.9 12.0 %collective-permute-start.11 = (bf16[1152,128]{1,0:T(8,128)(2,1)}, bf16[1152,128]{1,0:T(8,128)(2,1)}, u32[]{:S(2)}, u32[]{:S(2)}) collective-permute-start(bf16[1152,128]{1,0:T(8,128)(2,1)} %collective-permute-done.8.refs_5_), channel_id=1, source_target_pairs={{0,1},{1,0},{2,3},{3,2},{4,5},{5,4},{6,7},{7,6},{8,9},{9,8},{10,11... | collective-permute-start | bytes 884744 | tf_op jit(solution)/shard_map/ppermute | solution.py:46
  35.4 11.4 %collective-permute-start.12 = (bf16[1152,128]{1,0:T(8,128)(2,1)}, bf16[1152,128]{1,0:T(8,128)(2,1)}, u32[]{:S(2)}, u32[]{:S(2)}) collective-permute-start(bf16[1152,128]{1,0:T(8,128)(2,1)} %collective-permute-done.9.refs_6_), channel_id=1, source_target_pairs={{0,1},{1,0},{2,3},{3,2},{4,5},{5,4},{6,7},{7,6},{8,9},{9,8},{10,11... | collective-permute-start | bytes 884744 | tf_op jit(solution)/shard_map/ppermute | solution.py:46
  89.8 47.0 %copy-start.36 = (bf16[4,4,128,128]{3,2,1,0:T(8,128)(2,1)S(1)}, bf16[4,4,128,128]{3,2,1,0:T(8,128)(2,1)}, u32[]{:S(2)}) copy-start(bf16[4,4,128,128]{3,2,1,0:T(8,128)(2,1)} %get-tuple-element.54) | copy-start | bytes 1572868
  136.3 15.5 %collective-permute-start.24 = (bf16[4,4,288,128]{3,2,1,0:T(8,128)(2,1)}, bf16[4,4,288,128]{3,2,1,0:T(8,128)(2,1)S(1)}, u32[]{:S(2)}, u32[]{:S(2)}) collective-permute-start(bf16[4,4,288,128]{3,2,1,0:T(8,128)(2,1)} %get-tuple-element.56), channel_id=1, source_target_pairs={{0,1},{1,0},{2,3},{3,2},{4,5},{5,4},{6,7},{7,6},{8,9},{9,8},{10,11... | collective-permute-start | bytes 3538952 | tf_op jit(solution)/shard_map/ppermute | solution.py:46
  136.8 11.2 %collective-permute-start.14 = (bf16[4,4,128,128]{3,2,1,0:T(8,128)(2,1)S(1)}, bf16[4,4,128,128]{3,2,1,0:T(8,128)(2,1)S(1)}, u32[]{:S(2)}, u32[]{:S(2)}) collective-permute-start(bf16[4,4,128,128]{3,2,1,0:T(8,128)(2,1)S(1)} %copy-done.36), channel_id=1, source_target_pairs={{0,1},{1,0},{2,3},{3,2},{4,5},{5,4},{6,7},{7,6},{8,9},{9,8},{10,11... | collective-permute-start | bytes 1572872 | tf_op jit(solution)/shard_map/ppermute | solution.py:46
  148.2 6.7 %collective-permute-start.15 = (bf16[4,128,128]{2,1,0:T(8,128)(2,1)S(1)}, bf16[4,128,128]{2,1,0:T(8,128)(2,1)S(1)}, u32[]{:S(2)}, u32[]{:S(2)}) collective-permute-start(bf16[4,128,128]{2,1,0:T(8,128)(2,1)S(1)} %get-tuple-element.101), channel_id=1, source_target_pairs={{0,8},{1,9},{2,10},{3,11},{4,12},{5,13},{6,14},{7,15},{8,0},{9,1},... | collective-permute-start | bytes 393224 | tf_op jit(solution)/shard_map/ppermute | solution.py:46
  149.4 7.3 %collective-permute-start.16 = (bf16[4,128,128]{2,1,0:T(8,128)(2,1)S(1)}, bf16[4,128,128]{2,1,0:T(8,128)(2,1)S(1)}, u32[]{:S(2)}, u32[]{:S(2)}) collective-permute-start(bf16[4,128,128]{2,1,0:T(8,128)(2,1)S(1)} %get-tuple-element.103), channel_id=1, source_target_pairs={{0,16},{1,17},{2,18},{3,19},{4,20},{5,21},{6,22},{7,23},{8,24},{9,... | collective-permute-start | bytes 393224 | tf_op jit(solution)/shard_map/ppermute | solution.py:46
  150.9 8.1 %collective-permute-start.17 = (bf16[4,128,128]{2,1,0:T(8,128)(2,1)S(1)}, bf16[4,128,128]{2,1,0:T(8,128)(2,1)S(1)}, u32[]{:S(2)}, u32[]{:S(2)}) collective-permute-start(bf16[4,128,128]{2,1,0:T(8,128)(2,1)S(1)} %get-tuple-element.102), channel_id=1, source_target_pairs={{0,24},{1,25},{2,26},{3,27},{4,28},{5,29},{6,30},{7,31},{8,16},{9,... | collective-permute-start | bytes 393224 | tf_op jit(solution)/shard_map/ppermute | solution.py:46
  152.3 12.3 %collective-permute-start.25 = (bf16[4,288,128]{2,1,0:T(8,128)(2,1)S(1)}, bf16[4,288,128]{2,1,0:T(8,128)(2,1)S(1)}, u32[]{:S(2)}, u32[]{:S(2)}) collective-permute-start(bf16[4,288,128]{2,1,0:T(8,128)(2,1)S(1)} %get-tuple-element.98), channel_id=1, source_target_pairs={{0,8},{1,9},{2,10},{3,11},{4,12},{5,13},{6,14},{7,15},{8,0},{9,1},... | collective-permute-start | bytes 884744 | tf_op jit(solution)/shard_map/ppermute | solution.py:46
  153.5 15.6 %collective-permute-start.26 = (bf16[4,288,128]{2,1,0:T(8,128)(2,1)S(1)}, bf16[4,288,128]{2,1,0:T(8,128)(2,1)S(1)}, u32[]{:S(2)}, u32[]{:S(2)}) collective-permute-start(bf16[4,288,128]{2,1,0:T(8,128)(2,1)S(1)} %get-tuple-element.100), channel_id=1, source_target_pairs={{0,16},{1,17},{2,18},{3,19},{4,20},{5,21},{6,22},{7,23},{8,24},{9,... | collective-permute-start | bytes 884744 | tf_op jit(solution)/shard_map/ppermute | solution.py:46
  154.9 15.8 %collective-permute-start.27 = (bf16[4,288,128]{2,1,0:T(8,128)(2,1)S(1)}, bf16[4,288,128]{2,1,0:T(8,128)(2,1)S(1)}, u32[]{:S(2)}, u32[]{:S(2)}) collective-permute-start(bf16[4,288,128]{2,1,0:T(8,128)(2,1)S(1)} %get-tuple-element.99), channel_id=1, source_target_pairs={{0,24},{1,25},{2,26},{3,27},{4,28},{5,29},{6,30},{7,31},{8,16},{9,... | collective-permute-start | bytes 884744 | tf_op jit(solution)/shard_map/ppermute | solution.py:46
  159.0 27.5 %copy-start.2 = (bf16[2,512,512]{2,1,0:T(8,128)(2,1)S(1)}, bf16[2,512,512]{2,1,0:T(8,128)(2,1)}, u32[]{:S(2)}) copy-start(bf16[2,512,512]{2,1,0:T(8,128)(2,1)} %get-tuple-element.52.edge) | copy-start | bytes 3145732
  159.1 17.5 %collective-permute-start.18 = (bf16[128,128]{1,0:T(8,128)(2,1)S(1)}, bf16[128,128]{1,0:T(8,128)(2,1)S(1)}, u32[]{:S(2)}, u32[]{:S(2)}) collective-permute-start(bf16[128,128]{1,0:T(8,128)(2,1)S(1)} %get-tuple-element.107), channel_id=1, source_target_pairs={{0,2},{1,3},{2,0},{3,1},{4,6},{5,7},{6,4},{7,5},{8,10},{9,11},{10,... | collective-permute-start | bytes 98312 | tf_op jit(solution)/shard_map/ppermute | solution.py:46
  161.4 15.1 %collective-permute-start.19 = (bf16[128,128]{1,0:T(8,128)(2,1)S(1)}, bf16[128,128]{1,0:T(8,128)(2,1)S(1)}, u32[]{:S(2)}, u32[]{:S(2)}) collective-permute-start(bf16[128,128]{1,0:T(8,128)(2,1)S(1)} %get-tuple-element.109), channel_id=1, source_target_pairs={{0,4},{1,5},{2,6},{3,7},{4,0},{5,1},{6,2},{7,3},{8,12},{9,13},{10,... | collective-permute-start | bytes 98312 | tf_op jit(solution)/shard_map/ppermute | solution.py:46
  164.7 11.9 %collective-permute-start.20 = (bf16[128,128]{1,0:T(8,128)(2,1)S(1)}, bf16[128,128]{1,0:T(8,128)(2,1)S(1)}, u32[]{:S(2)}, u32[]{:S(2)}) collective-permute-start(bf16[128,128]{1,0:T(8,128)(2,1)S(1)} %get-tuple-element.108), channel_id=1, source_target_pairs={{0,6},{1,7},{2,4},{3,5},{4,2},{5,3},{6,0},{7,1},{8,14},{9,15},{10,... | collective-permute-start | bytes 98312 | tf_op jit(solution)/shard_map/ppermute | solution.py:46
  171.0 8.0 %collective-permute-start.28 = (bf16[288,128]{1,0:T(8,128)(2,1)S(1)}, bf16[288,128]{1,0:T(8,128)(2,1)S(1)}, u32[]{:S(2)}, u32[]{:S(2)}) collective-permute-start(bf16[288,128]{1,0:T(8,128)(2,1)S(1)} %get-tuple-element.104), channel_id=1, source_target_pairs={{0,2},{1,3},{2,0},{3,1},{4,6},{5,7},{6,4},{7,5},{8,10},{9,11},{10,... | collective-permute-start | bytes 221192 | tf_op jit(solution)/shard_map/ppermute | solution.py:46
  173.7 7.7 %collective-permute-start.29 = (bf16[288,128]{1,0:T(8,128)(2,1)S(1)}, bf16[288,128]{1,0:T(8,128)(2,1)S(1)}, u32[]{:S(2)}, u32[]{:S(2)}) collective-permute-start(bf16[288,128]{1,0:T(8,128)(2,1)S(1)} %get-tuple-element.106), channel_id=1, source_target_pairs={{0,4},{1,5},{2,6},{3,7},{4,0},{5,1},{6,2},{7,3},{8,12},{9,13},{10,... | collective-permute-start | bytes 221192 | tf_op jit(solution)/shard_map/ppermute | solution.py:46
  176.6 6.3 %collective-permute-start.30 = (bf16[288,128]{1,0:T(8,128)(2,1)S(1)}, bf16[288,128]{1,0:T(8,128)(2,1)S(1)}, u32[]{:S(2)}, u32[]{:S(2)}) collective-permute-start(bf16[288,128]{1,0:T(8,128)(2,1)S(1)} %get-tuple-element.105), channel_id=1, source_target_pairs={{0,6},{1,7},{2,4},{3,5},{4,2},{5,3},{6,0},{7,1},{8,14},{9,15},{10,... | collective-permute-start | bytes 221192 | tf_op jit(solution)/shard_map/ppermute | solution.py:46
  176.6 8.1 %collective-permute-start.21 = (f32[128,128]{1,0:T(8,128)S(1)}, f32[128,128]{1,0:T(8,128)S(1)}, u32[]{:S(2)}, u32[]{:S(2)}) collective-permute-start(f32[128,128]{1,0:T(8,128)S(1)} %fusion.15.refs_0_), channel_id=1, source_target_pairs={{0,8},{1,9},{2,10},{3,11},{4,12},{5,13},{6,14},{7,15},{8,0},{9,1},... | collective-permute-start | bytes 196616 | tf_op jit(solution)/shard_map/ppermute | solution.py:46
  177.4 9.1 %collective-permute-start.22 = (f32[128,128]{1,0:T(8,128)S(1)}, f32[128,128]{1,0:T(8,128)S(1)}, u32[]{:S(2)}, u32[]{:S(2)}) collective-permute-start(f32[128,128]{1,0:T(8,128)S(1)} %fusion.15.refs_0_), channel_id=1, source_target_pairs={{0,16},{1,17},{2,18},{3,19},{4,20},{5,21},{6,22},{7,23},{8,24},{9,... | collective-permute-start | bytes 196616 | tf_op jit(solution)/shard_map/ppermute | solution.py:46
  178.9 9.1 %collective-permute-start.23 = (f32[128,128]{1,0:T(8,128)S(1)}, f32[128,128]{1,0:T(8,128)S(1)}, u32[]{:S(2)}, u32[]{:S(2)}) collective-permute-start(f32[128,128]{1,0:T(8,128)S(1)} %fusion.15.refs_0_), channel_id=1, source_target_pairs={{0,24},{1,25},{2,26},{3,27},{4,28},{5,29},{6,30},{7,31},{8,16},{9,... | collective-permute-start | bytes 196616 | tf_op jit(solution)/shard_map/ppermute | solution.py:46
  182.9 5.6 %collective-permute-start.31 = (f32[288,128]{1,0:T(8,128)S(1)}, f32[288,128]{1,0:T(8,128)S(1)}, u32[]{:S(2)}, u32[]{:S(2)}) collective-permute-start(f32[288,128]{1,0:T(8,128)S(1)} %fusion.12.refs_4_), channel_id=1, source_target_pairs={{0,8},{1,9},{2,10},{3,11},{4,12},{5,13},{6,14},{7,15},{8,0},{9,1},... | collective-permute-start | bytes 442376 | tf_op jit(solution)/shard_map/ppermute | solution.py:46
  183.3 5.8 %collective-permute-start.32 = (f32[288,128]{1,0:T(8,128)S(1)}, f32[288,128]{1,0:T(8,128)S(1)}, u32[]{:S(2)}, u32[]{:S(2)}) collective-permute-start(f32[288,128]{1,0:T(8,128)S(1)} %fusion.12.refs_4_), channel_id=1, source_target_pairs={{0,16},{1,17},{2,18},{3,19},{4,20},{5,21},{6,22},{7,23},{8,24},{9,... | collective-permute-start | bytes 442376 | tf_op jit(solution)/shard_map/ppermute | solution.py:46
  184.7 6.0 %collective-permute-start.33 = (f32[288,128]{1,0:T(8,128)S(1)}, f32[288,128]{1,0:T(8,128)S(1)}, u32[]{:S(2)}, u32[]{:S(2)}) collective-permute-start(f32[288,128]{1,0:T(8,128)S(1)} %fusion.12.refs_4_), channel_id=1, source_target_pairs={{0,24},{1,25},{2,26},{3,27},{4,28},{5,29},{6,30},{7,31},{8,16},{9,... | collective-permute-start | bytes 442376 | tf_op jit(solution)/shard_map/ppermute | solution.py:46
  186.5 28.6 %collective-permute-start.13 = (bf16[512,512]{1,0:T(8,128)(2,1)S(1)}, bf16[512,512]{1,0:T(8,128)(2,1)S(1)}, u32[]{:S(2)}, u32[]{:S(2)}) collective-permute-start(bf16[512,512]{1,0:T(8,128)(2,1)S(1)} %slice_bitcast_fusion.1), channel_id=1, source_target_pairs={{1,0},{2,1},{3,2},{4,3},{5,4},{6,5},{7,6},{8,7},{9,8},{10,9},{11,1... | collective-permute-start | bytes 1572872 | tf_op jit(solution)/shard_map/ppermute | solution.py:36
  193.7 23.2 %collective-permute-start.39 = (f32[8,128]{1,0:T(8,128)}, f32[8,128]{1,0:T(8,128)S(1)}, u32[]{:S(2)}, u32[]{:S(2)}) collective-permute-start(f32[8,128]{1,0:T(8,128)} %get-tuple-element.57), channel_id=1, source_target_pairs={{0,6},{1,7},{2,4},{3,5},{4,2},{5,3},{6,0},{7,1},{8,14},{9,15},{10,... | collective-permute-start | bytes 12296 | tf_op jit(solution)/shard_map/ppermute | solution.py:46
  197.6 19.5 %collective-permute-start.40 = (f32[8,128]{1,0:T(8,128)}, f32[8,128]{1,0:T(8,128)S(1)}, u32[]{:S(2)}, u32[]{:S(2)}) collective-permute-start(f32[8,128]{1,0:T(8,128)} %get-tuple-element.57), channel_id=1, source_target_pairs={{0,7},{1,6},{2,5},{3,4},{4,3},{5,2},{6,1},{7,0},{8,15},{9,14},{10,... | collective-permute-start | bytes 12296 | tf_op jit(solution)/shard_map/ppermute | solution.py:46
  212.6 16.3 %collective-permute-start.37 = (f32[8,128]{1,0:T(8,128)S(1)}, f32[8,128]{1,0:T(8,128)S(1)}, u32[]{:S(2)}, u32[]{:S(2)}) collective-permute-start(f32[8,128]{1,0:T(8,128)S(1)} %copy-done.32), channel_id=1, source_target_pairs={{0,4},{1,5},{2,6},{3,7},{4,0},{5,1},{6,2},{7,3},{8,12},{9,13},{10,... | collective-permute-start | bytes 12296 | tf_op jit(solution)/shard_map/ppermute | solution.py:46
  213.2 15.7 %collective-permute-start.38 = (f32[8,128]{1,0:T(8,128)S(1)}, f32[8,128]{1,0:T(8,128)S(1)}, u32[]{:S(2)}, u32[]{:S(2)}) collective-permute-start(f32[8,128]{1,0:T(8,128)S(1)} %copy-done.32), channel_id=1, source_target_pairs={{0,5},{1,4},{2,7},{3,6},{4,1},{5,0},{6,3},{7,2},{8,13},{9,12},{10,... | collective-permute-start | bytes 12296 | tf_op jit(solution)/shard_map/ppermute | solution.py:46
  215.1 14.4 %collective-permute-start.35 = (f32[8,128]{1,0:T(8,128)S(1)}, f32[8,128]{1,0:T(8,128)S(1)}, u32[]{:S(2)}, u32[]{:S(2)}) collective-permute-start(f32[8,128]{1,0:T(8,128)S(1)} %copy-done.32), channel_id=1, source_target_pairs={{0,2},{1,3},{2,0},{3,1},{4,6},{5,7},{6,4},{7,5},{8,10},{9,11},{10,... | collective-permute-start | bytes 12296 | tf_op jit(solution)/shard_map/ppermute | solution.py:46
  216.9 12.6 %collective-permute-start.36 = (f32[8,128]{1,0:T(8,128)S(1)}, f32[8,128]{1,0:T(8,128)S(1)}, u32[]{:S(2)}, u32[]{:S(2)}) collective-permute-start(f32[8,128]{1,0:T(8,128)S(1)} %copy-done.32), channel_id=1, source_target_pairs={{0,3},{1,2},{2,1},{3,0},{4,7},{5,6},{6,5},{7,4},{8,11},{9,10},{10,... | collective-permute-start | bytes 12296 | tf_op jit(solution)/shard_map/ppermute | solution.py:46
  217.1 12.9 %collective-permute-start.34 = (f32[8,128]{1,0:T(8,128)S(1)}, f32[8,128]{1,0:T(8,128)S(1)}, u32[]{:S(2)}, u32[]{:S(2)}) collective-permute-start(f32[8,128]{1,0:T(8,128)S(1)} %copy-done.32), channel_id=1, source_target_pairs={{0,1},{1,0},{2,3},{3,2},{4,5},{5,4},{6,7},{7,6},{8,9},{9,8},{10,11... | collective-permute-start | bytes 12296 | tf_op jit(solution)/shard_map/ppermute | solution.py:46
  217.3 16.0 %copy-start.11 = (f32[2,64,1024]{2,1,0:T(8,128)S(1)}, f32[2,64,1024]{2,1,0:T(8,128)}, u32[]{:S(2)}) copy-start(f32[2,64,1024]{2,1,0:T(8,128)} %get-tuple-element.58) | copy-start | bytes 1572868
  (30 other events, 200.0 us)

commit v2 on v0

v2 whole, which is shorter than its diff:
```python
import functools

import jax
import jax.numpy as jnp
from jax import lax
from jax.experimental import pallas as pl
from jax.experimental.pallas import tpu as pltpu
from jax.sharding import PartitionSpec as P

DILATION_STEP = 512
STEP = 10

beta_one = 0.9
beta_two = 0.999
learn_rate = 0.05
weight_decay = 0.01
epsilon = 1e-08
clip_bound = 1.0

LANES = 128
TILE = 16
AUX = 128
MEL = 80
ONES = 80
KEEP = 81
LINK = 82
ROWS = 512
BF = jnp.bfloat16
F32 = jnp.float32
BOTH = ("rep", "seq")


def from_behind(x, axis, by):
    count = lax.axis_size(axis)
    pairs = [(i, i + by) for i in range(count) if 0 <= i + by < count]
    return lax.ppermute(x, axis, pairs)


def swap(x, rep_bits, seq_bits):
    reps, seqs = lax.axis_size("rep"), lax.axis_size("seq")
    pairs = [
        (r * seqs + s, (r ^ rep_bits) * seqs + (s ^ seq_bits))
        for r in range(reps)
        for s in range(seqs)
    ]
    return lax.ppermute(x, BOTH, pairs)


def nt_dot(left, right):
    return lax.dot_general(
        left, right, (((1,), (1,)), ((), ())), preferred_element_type=F32
    )


def tn_dot(left, right):
    return lax.dot_general(
        left, right, (((0,), (0,)), ((), ())), preferred_element_type=F32
    )


def dot(left, right):
    return jnp.dot(left, right, preferred_element_type=F32)


def params(**more):
    return pltpu.CompilerParams(vmem_limit_bytes=58 * 2**20, **more)


def cost(flops, moved):
    return pl.CostEstimate(flops=int(flops), bytes_accessed=int(moved), transcendentals=0)


def whole(shape):
    return pl.BlockSpec(shape, lambda *_: (0,) * len(shape))


def spot():
    seq = lax.axis_index("seq")
    return seq % 2, lax.axis_index("rep"), seq // 2


VMEM = pl.BlockSpec(memory_space=pltpu.VMEM)
ANY = pl.BlockSpec(memory_space=pl.ANY)


OUT_PART = 8 * TILE
GATE_PART = 2 * 8 * TILE + 32
PART = GATE_PART + OUT_PART


def pack_body(conv, cond, bias, out, own, first, small):
    _, rep, _ = spot()
    small[0:MEL, :] = cond[...].astype(BF)
    small[MEL:96, :] = jnp.concatenate([bias[...], jnp.zeros((14, LANES), F32)], 0).astype(BF)
    small[96:AUX, :] = jnp.zeros((32, LANES), BF)
    for k in range(4):
        start = pl.multiple_of((rep ^ k) * TILE, TILE)
        for t in range(2):
            put_tiles(own.at[k], t * 128, conv[pl.ds(start, TILE), t, :])
        own[k, 256:GATE_PART, :] = small[pl.ds(2 * start, 32), :]
        put_tiles(own.at[k], GATE_PART, out[pl.ds(start, TILE), :])
    first[...] = own[0]


def pack_weights(conv, cond, bias, out):
    return pl.pallas_call(
        pack_body,
        in_specs=[VMEM] * 4,
        out_specs=[VMEM] * 2,
        out_shape=[
            jax.ShapeDtypeStruct((4, PART, LANES), BF),
            jax.ShapeDtypeStruct((PART, LANES), BF),
        ],
        scratch_shapes=[pltpu.VMEM((AUX, LANES), BF)],
        compiler_params=params(),
        name="pack_weights",
    )(conv, cond, bias, out)


def tail_body(x, _, tail):
    tail[...] = x[...]


def last_rows(x, after):
    return pl.pallas_call(
        tail_body,
        grid=(1,),
        in_specs=[pl.BlockSpec((ROWS, x.shape[1]), lambda i: (x.shape[0] // ROWS - 1, 0)), ANY],
        out_specs=whole((ROWS, x.shape[1])),
        out_shape=jax.ShapeDtypeStruct((ROWS, x.shape[1]), x.dtype),
        compiler_params=params(),
        name="last_rows",
    )(x, after)


def mixed_block(block):
    low, mid, top = block & 1, (block >> 1) & 1, (block >> 2) & 1
    return low + 4 * mid + 2 * top


def each_part(own, stack, sides, write):
    core, rep, z = spot()
    for c in range(2):
        for j in range(4):
            for k in range(4):
                if j == 0:
                    source = own[c].at[k]
                elif k == 0:
                    source = stack[c].at[pl.ds((j - 1) * PART, PART), :]
                else:
                    source = sides[c][k - 1].at[pl.ds((j - 1) * PART, PART), :]
                write(source, 2 * (z ^ j) + (core ^ c), rep ^ k)


def unpack(refs, w, o, bias_out, small):
    def write(source, shard, quarter):
        row = pl.multiple_of(64 * shard + TILE * quarter, TILE)
        for b in range(8):
            lanes = pl.ds(mixed_block(b) * LANES, LANES)
            w[pl.ds(row, TILE), lanes] = source[b * TILE : (b + 1) * TILE, :]
            w[pl.ds(512 + row, TILE), lanes] = source[128 + b * TILE : 128 + (b + 1) * TILE, :]
        small[shard, pl.ds(pl.multiple_of(32 * quarter, 32), 32), :] = source[256:GATE_PART, :]
        for b in range(8):
            base = GATE_PART + b * TILE
            o[pl.ds(row, TILE), b * LANES : (b + 1) * LANES] = source[base : base + TILE, :]

    each_part(refs[0:2], refs[2:4], (refs[4:7], refs[7:10]), write)
    blank = jnp.zeros((TILE - 1, LANES), BF)
    for s in range(8):
        lane = mixed_block(s) * LANES
        w[1024 : 1024 + MEL, lane : lane + LANES] = small[s, 0:MEL, :]
        tail = small[s, MEL : MEL + TILE, :]
        for e in range(2):
            if s < 4:
                at = mixed_block(2 * s + e) * LANES
                w[1104:1120, at : at + LANES] = jnp.concatenate([tail[e : e + 1], blank], 0)
            else:
                at = (2 * (s - 4) + e) * LANES
                bias_out[:, at : at + LANES] = jnp.broadcast_to(tail[e : e + 1].astype(F32), (8, LANES))
    w[1120:1152, :] = jnp.zeros((32, w.shape[1]), BF)


def across_hops(own, stack):
    across = [swap(stack, k, 0) for k in (1, 2, 3)]
    return [own, swap(own, 0, 1), stack, swap(stack, 0, 1), *across, *[swap(a, 0, 1) for a in across]]


def mixed_columns(x):
    rows, columns = x.shape
    return x.reshape(rows, 2, 2, columns // 4).transpose(0, 2, 1, 3).reshape(rows, columns)


def gather_plain(conv_weight, out_weight, cond_weight, biases):
    conv = conv_weight.astype(BF).transpose(1, 0, 2)
    conv_all = lax.all_gather(conv, "seq", axis=1, tiled=True)
    cond_all = lax.all_gather(cond_weight.astype(BF), "seq", axis=1, tiled=True)
    out_all = lax.all_gather(out_weight.astype(BF), "seq", axis=0, tiled=True)
    bias_all = lax.all_gather(biases.astype(BF), "seq", axis=0, tiled=True)
    gates = cond_all.shape[1]
    w = jnp.concatenate(
        [
            conv_all[0],
            conv_all[1],
            cond_all,
            bias_all[None, :gates],
            jnp.zeros((AUX - MEL - 1, gates), BF),
        ],
        0,
    )
    bias_out = jnp.broadcast_to(bias_all[None, gates:].astype(F32), (8, gates))
    return mixed_columns(w), out_all, bias_out


def sums_body(res, skp, *refs):
    sums = refs[-1]

    @pl.when(pl.program_id(0) == 0)
    def _():
        sums[...] = jnp.zeros_like(sums)

    for n, part in enumerate((res, skp)):
        total = jnp.sum(part[...].astype(F32), 0, keepdims=True)
        sums[:, n * 512 : (n + 1) * 512] += jnp.broadcast_to(total, (8, 512))


def sum_columns(rows, res, skp, after):
    total = res.shape[0]
    by_row = pl.BlockSpec((rows, 512), lambda i: (i, 0))
    return pl.pallas_call(
        sums_body,
        grid=(total // rows,),
        in_specs=[by_row, by_row] + [ANY] * len(after),
        out_specs=whole((8, 1024)),
        out_shape=jax.ShapeDtypeStruct((8, 1024), F32),
        compiler_params=params(),
        cost_estimate=cost(total * 1024, total * 2048),
        name="sum_columns",
    )(res, skp, *after)


def emit_pieces(outs, write):
    core, rep, z = spot()
    for c, dest in enumerate(outs):

        def one(n, carry, c=c, dest=dest):
            k, j = n // 4, n % 4
            write(dest.at[k, j], 2 * (z ^ j) + (core ^ c), rep ^ k)
            return carry

        lax.fori_loop(0, 16, one, 0)


def put_tiles(dest, base, value, order=lambda b: b):
    value = value.astype(dest.dtype)
    for b in range(value.shape[1] // LANES):
        lane = order(b) * LANES
        dest[base + b * TILE : base + (b + 1) * TILE, :] = value[:, lane : lane + LANES]


def gates_body(split, subs, x, tail, mel, keep, ids, tail_ids, res, skp, *refs):
    if split:
        sums, parts, refs = refs[0], refs[1:11], refs[11:]
        p, hid, flags, edge, w, o, bias_out, keep_out, send_out = refs[:9]
        xe, carry, carry_ids, acc, acc_out, small, small_low = refs[9:]
    else:
        w, o, p, hid, flags, edge, grad, grad_out, xe, carry, carry_ids, acc, acc_out = refs
    step, last = pl.program_id(0), pl.num_programs(0) - 1
    rows, half = x.shape[0], p.shape[1] // 4

    @pl.when(step == 0)
    def _():
        carry[...] = tail[...]
        carry_ids[...] = jnp.where(lax.axis_index(BOTH) > 0, tail_ids[...], -1)
        acc[...] = jnp.zeros_like(acc)
        acc_out[...] = jnp.zeros_like(acc_out)
        if split:
            unpack(parts, w, o, bias_out, small_low)

    ids_now = ids[...]
    ids_past = carry_ids[...]
    if rows > ROWS:
        ids_past = jnp.concatenate([ids_past, ids_now[:, 0 : rows - ROWS]], 1)
    place = lax.broadcasted_iota(jnp.int32, (TILE, rows), 0)
    mark = jnp.where(
        place == 0,
        1.0,
        jnp.where(
            place == KEEP - ONES,
            keep[...].astype(F32),
            jnp.where(place == LINK - ONES, (ids_now == ids_past).astype(F32), 0.0),
        ),
    ).astype(BF)
    flags[...] = mark
    side = jnp.concatenate([mel[...], mark, jnp.zeros((32, rows), BF)], 0).T
    link = side[:, LINK : LINK + 1]
    kept_rows = side[:, KEEP : KEEP + 1].astype(F32)
    xe[:, 0:512] = x[...]
    xe[0:ROWS, 512:1024] = carry[...] * link[0:ROWS]
    if rows > ROWS:
        xe[ROWS:, 512:1024] = x[0 : rows - ROWS, :] * link[ROWS:]
    xe[:, 1024:1152] = side
    carry[...] = x[rows - ROWS :, :]
    carry_ids[...] = ids_now[:, rows - ROWS :]

    size = rows // subs
    for s in range(subs):
        at = slice(s * size, (s + 1) * size)
        up_all = nt_dot(res[at, :], o[:, 0:512]) + nt_dot(skp[at, :], o[:, 512:1024])
        for n in range(2):
            base = n * 2 * half
            pre = dot(xe[at, :], w[:, base : base + 2 * half])
            up = up_all[:, n * half : (n + 1) * half]
            filt = jnp.tanh(pre[:, :half])
            gate = 0.5 * jnp.tanh(0.5 * pre[:, half:]) + 0.5
            kept = kept_rows[at] * gate
            hidden = filt * kept
            hid[at, n * half : (n + 1) * half] = hidden.astype(BF)
            p[at, base : base + half] = (up * kept * (1.0 - filt * filt)).astype(BF)
            p[at, base + half : base + 2 * half] = (up * hidden * (1.0 - gate)).astype(BF)
    acc[...] += tn_dot(xe[...], p[...])
    acc_out[:, 0:512] += tn_dot(hid[...], res[...])
    acc_out[:, 512:1024] += tn_dot(hid[...], skp[...])

    @pl.when(step == 0)
    def _():
        past = nt_dot(p[0:ROWS, :], w[512:1024, :])
        edge[...] = (past * link[0:ROWS].astype(F32)).astype(BF)

    @pl.when(step == last)
    def _():
        if not split:
            grad[...] = acc[...]
            grad_out[...] = acc_out[...]
            return
        small[...] = jnp.zeros_like(small)
        for s in range(8):
            lane = mixed_block(s) * LANES
            small[s, 0:MEL, :] = acc[1024 : 1024 + MEL, lane : lane + LANES]
            for e in range(2):
                if s < 4:
                    lane = mixed_block(2 * s + e) * LANES
                    line = acc[1024 + ONES : 1024 + ONES + 1, lane : lane + LANES]
                else:
                    lane = (2 * (s - 4) + e) * LANES
                    line = sums[0:1, lane : lane + LANES]
                small[s, MEL + e : MEL + e + 1, :] = line

        def write(dest, shard, quarter):
            row = pl.multiple_of(64 * shard + TILE * quarter, TILE)
            put_tiles(dest, 0, acc[pl.ds(row, TILE), :], mixed_block)
            put_tiles(dest, 128, acc[pl.ds(512 + row, TILE), :], mixed_block)
            at = pl.multiple_of(32 * quarter, 32)
            dest[256:GATE_PART, :] = small[shard, pl.ds(at, 32), :].astype(dest.dtype)
            put_tiles(dest, GATE_PART, acc_out[pl.ds(row, TILE), :])

        emit_pieces((keep_out, send_out), write)


def gates_layer(split, rows, subs, x, tail, mel, keep, ids, tail_ids, res, skp, extra):
    total = x.shape[0]
    steps = total // rows
    by_row = lambda columns: pl.BlockSpec((rows, columns), lambda i: (i, 0))
    by_lane = lambda high: pl.BlockSpec((high, rows), lambda i: (0, i))
    in_specs = [
        by_row(512),
        whole((ROWS, 512)),
        by_lane(MEL),
        by_lane(1),
        by_lane(1),
        whole((1, ROWS)),
        by_row(512),
        by_row(512),
    ] + [whole(e.shape) for e in extra]
    out_specs = [
        by_row(1024),
        by_row(512),
        by_lane(TILE),
        whole((ROWS, 512)),
    ]
    out_shape = [
        jax.ShapeDtypeStruct((total, 1024), BF),
        jax.ShapeDtypeStruct((total, 512), BF),
        jax.ShapeDtypeStruct((TILE, total), BF),
        jax.ShapeDtypeStruct((ROWS, 512), BF),
    ]
    if split:
        more = [
            ((1024 + AUX, 1024), BF),
            ((512, 1024), BF),
            ((8, 1024), F32),
            ((4, 4, PART, LANES), BF),
            ((4, 4, PART, LANES), BF),
        ]
    else:
        more = [((1024 + AUX, 1024), F32), ((512, 1024), F32)]
    for shape, dtype in more:
        out_specs.append(whole(shape))
        out_shape.append(jax.ShapeDtypeStruct(shape, dtype))
    scratch = [
        pltpu.VMEM((rows, 1024 + AUX), BF),
        pltpu.VMEM((ROWS, 512), BF),
        pltpu.VMEM((1, ROWS), jnp.int32),
        pltpu.VMEM((1024 + AUX, 1024), F32),
        pltpu.VMEM((512, 1024), F32),
    ]
    if split:
        scratch += [pltpu.VMEM((8, AUX, LANES), F32), pltpu.VMEM((8, AUX, LANES), BF)]
    return pl.pallas_call(
        functools.partial(gates_body, split, subs),
        grid=(steps,),
        in_specs=in_specs,
        out_specs=out_specs,
        out_shape=out_shape,
        scratch_shapes=scratch,
        compiler_params=params(),
        cost_estimate=cost(6.75 * 2 * total * 512 * 1024, total * 8000),
        name="gates_layer",
    )(x, tail, mel, keep, ids, tail_ids, res, skp, *extra)


def mixed_body(x, hid, o, bias, rest, edge, *refs):
    residual, skip, patch = refs[-3:]
    mixed = dot(hid[...], o[...]) + bias[0:1, :]
    residual[...] = (x[...].astype(F32) + mixed[:, 0:512]).astype(BF)
    skip[...] = mixed[:, 512:1024].astype(BF)

    @pl.when(pl.program_id(0) == 0)
    def _():
        patch[...] = (rest[...] + edge[...].astype(F32)).astype(BF)


def mixed_layer(rows, x, hid, o, bias, rest, edge, input_grad, after):
    total = x.shape[0]
    by_row = pl.BlockSpec((rows, 512), lambda i: (i, 0))
    last = pl.BlockSpec((ROWS, 512), lambda i: (total // ROWS - 1, 0))
    operands = (x, hid, o, bias, rest, edge, input_grad, *after)
    return pl.pallas_call(
        mixed_body,
        grid=(total // rows,),
        in_specs=[by_row, by_row, whole((512, 1024)), whole((8, 1024)), whole((ROWS, 512)), whole((ROWS, 512))]
        + [ANY] * (1 + len(after)),
        out_specs=[by_row, by_row, last],
        out_shape=[jax.ShapeDtypeStruct((total, 512), BF)] * 3,
        input_output_aliases={6: 2},
        compiler_params=params(),
        cost_estimate=cost(2 * total * 512 * 1024, total * 4096),
        name="mixed_layer",
    )(*operands)


def input_body(res, p, flags, w, *refs):
    out, rest, carry = refs[-3:]
    step = pl.program_id(0)
    rows = res.shape[0]
    link = flags[...].T[:, LINK - MEL : LINK - MEL + 1].astype(F32)
    both = nt_dot(p[...], w[...])
    past = both[:, 512:1024] * link
    now = res[...].astype(F32) + both[:, 0:512]

    @pl.when(step == 0)
    def _():
        rest[...] = now[rows - ROWS :]
        carry[...] = jnp.zeros_like(carry)

    if rows > ROWS:
        out[0 : rows - ROWS, :] = (now[0 : rows - ROWS] + past[ROWS:]).astype(BF)
    out[rows - ROWS :, :] = (now[rows - ROWS :] + carry[...]).astype(BF)
    carry[...] = past[0:ROWS]


def input_layer(rows, res, p, flags, w, after):
    total = res.shape[0]
    steps = total // rows
    by_row = lambda columns: pl.BlockSpec((rows, columns), lambda i: (steps - 1 - i, 0))
    return pl.pallas_call(
        input_body,
        grid=(steps,),
        in_specs=[
            by_row(512),
            by_row(1024),
            pl.BlockSpec((TILE, rows), lambda i: (0, steps - 1 - i)),
            pl.BlockSpec((1024, 1024), lambda i: (0, 0)),
        ]
        + [ANY] * len(after),
        out_specs=[by_row(512), whole((ROWS, 512))],
        out_shape=[
            jax.ShapeDtypeStruct((total, 512), BF),
            jax.ShapeDtypeStruct((ROWS, 512), F32),
        ],
        scratch_shapes=[pltpu.VMEM((ROWS, 512), F32)],
        compiler_params=params(),
        cost_estimate=cost(4 * total * 512 * 1024, total * 4096),
        name="input_layer",
    )(res, p, flags, w, *after)


def cores_body(keep, got, edge, *outs):
    for n in range(4):
        outs[n][...] = (keep[n].astype(F32) + got[n].astype(F32)).astype(outs[n].dtype)
    outs[4][...] = edge[...]


def add_cores(keep, got, edge):
    spec = pl.BlockSpec((4, 1, PART, LANES), lambda i: (0, i, 0, 0))
    part = pl.BlockSpec((ROWS // 4, 512), lambda i: (i, 0))
    return pl.pallas_call(
        cores_body,
        grid=(4,),
        in_specs=[spec, spec, part],
        out_specs=[pl.BlockSpec((1, PART, LANES), lambda i: (i, 0, 0))] * 4 + [part],
        out_shape=[jax.ShapeDtypeStruct((4, PART, LANES), BF if n else F32) for n in range(4)]
        + [jax.ShapeDtypeStruct(edge.shape, BF)],
        compiler_params=params(),
        cost_estimate=cost(10**6, 8 * 10**6),
        name="add_cores",
    )(keep, got, edge)


def hop_body(keep, g1, g2, g3, *refs):
    outs = refs[-4:]
    for n in range(4):
        total = keep[n] + g1[n].astype(F32) + g2[n].astype(F32) + g3[n].astype(F32)
        outs[n][...] = total.astype(outs[n].dtype)


def add_hop(parts, after):
    return pl.pallas_call(
        hop_body,
        in_specs=[VMEM] * 4 + [ANY] * len(after),
        out_specs=[VMEM] * 4,
        out_shape=[jax.ShapeDtypeStruct((PART, LANES), BF if n else F32) for n in range(4)],
        compiler_params=params(),
        cost_estimate=cost(10**6, 3 * 10**6),
        name="add_hop",
    )(*parts, *after)


def last_body(keep, g1, g2, g3, *refs):
    total, square = refs[-2:]
    total[...] = keep[...] + g1[...].astype(F32) + g2[...].astype(F32) + g3[...].astype(F32)
    square[...] = jnp.full(square.shape, jnp.sum(total[...] * total[...]), F32)


def add_last(parts, devices, after):
    return pl.pallas_call(
        last_body,
        in_specs=[VMEM] * 4 + [ANY] * len(after),
        out_specs=[VMEM] * 2,
        out_shape=[
            jax.ShapeDtypeStruct((PART, LANES), F32),
            jax.ShapeDtypeStruct((devices, LANES), F32),
        ],
        compiler_params=params(),
        cost_estimate=cost(10**6, 10**6),
        name="add_last",
    )(*parts, *after)


def adamw_update(grad, moment, second, weight, factor, decay):
    clipped = grad * factor
    moment_new = beta_one * moment + (1.0 - beta_one) * clipped
    second_new = beta_two * second + (1.0 - beta_two) * clipped * clipped
    mean_hat = moment_new / (1.0 - beta_one**STEP)
    square_hat = second_new / (1.0 - beta_two**STEP)
    weight_new = weight - learn_rate * (
        mean_hat / (jnp.sqrt(square_hat) + epsilon) + decay * weight
    )
    return (moment_new, second_new, weight_new)


def update_body(*refs):
    squares, parts = refs[0], refs[1:5]
    conv, cond, out, bias = refs[5:8], refs[8:11], refs[11:14], refs[14:17]
    norm, new, small = refs[17], refs[18:30], refs[30]
    _, rep, _ = spot()
    grad_norm = jnp.sqrt(jnp.sum(squares[...], 0, keepdims=True))
    norm[...] = grad_norm
    factor = clip_bound / jnp.maximum(grad_norm, clip_bound)

    def step(grad, old, dest, at, decay):
        got = adamw_update(grad, *[ref[at] for ref in old], factor, decay)
        for ref, value in zip(dest, got):
            ref[at] = value

    for k in range(4):
        row = pl.multiple_of((rep ^ k) * TILE, TILE)
        for b in range(8):
            lanes = slice(b * LANES, (b + 1) * LANES)
            for t in range(2):
                base = t * 128 + b * TILE
                step(parts[k][base : base + TILE, :], conv, new[0:3], (pl.ds(row, TILE), t, lanes), weight_decay)
            base = GATE_PART + b * TILE
            step(parts[k][base : base + TILE, :], out, new[6:9], (pl.ds(row, TILE), lanes), weight_decay)
        small[pl.ds(2 * row, 32), :] = parts[k][256:GATE_PART, :]
    step(small[0:MEL, :], cond, new[3:6], (slice(0, MEL), slice(0, LANES)), weight_decay)
    step(small[MEL : MEL + 2, :], bias, new[9:12], (slice(0, 2), slice(0, LANES)), 0.0)


def update(squares, parts, conv, cond, out, bias):
    shapes = [(1, LANES)]
    for group in (conv, cond, out, bias):
        shapes += [group[0].shape] * 3
    return pl.pallas_call(
        update_body,
        in_specs=[VMEM] * 17,
        out_specs=[VMEM] * 13,
        out_shape=[jax.ShapeDtypeStruct(s, F32) for s in shapes],
        scratch_shapes=[pltpu.VMEM((AUX, LANES), F32)],
        compiler_params=params(),
        name="update",
    )(squares, *parts, *conv, *cond, *out, *bias)


def local(
    inputs,
    mel_frames,
    utterance,
    keep_mask,
    res_grad,
    skip_grad,
    conv_weight,
    cond_weight,
    out_weight,
    biases,
    conv_first,
    conv_second,
    cond_first,
    cond_second,
    out_first,
    out_second,
    bias_first,
    bias_second,
):
    rows, width = inputs.shape
    span = DILATION_STEP
    split = lax.axis_size("rep") == 4 and lax.axis_size("seq") == 8
    tile = 1024

    if split:
        own, first = pack_weights(conv_weight, cond_weight, biases.reshape(2, LANES), out_weight)
        stack = jnp.concatenate([swap(first, 0, 2 * j) for j in (1, 2, 3)], 0)
        parts = across_hops(own, stack)
        sums = sum_columns(2 * tile, res_grad, skip_grad, (stack,))
        last = last_rows(inputs, stack)
    else:
        w, o, bias_out = gather_plain(conv_weight, out_weight, cond_weight, biases)
        sums = sum_columns(2 * tile, res_grad, skip_grad, ())
        last = inputs[rows - span :]

    tail = from_behind(last, BOTH, 1)
    tail_ids = from_behind(utterance[rows - span :], BOTH, 1)
    samples = (
        inputs,
        tail,
        mel_frames,
        keep_mask.reshape(1, rows),
        utterance.reshape(1, rows),
        tail_ids.reshape(1, span),
        res_grad,
        skip_grad,
    )
    if split:
        p, hid, flags, edge, w, o, bias_out, keep, send = gates_layer(split, tile, 2, *samples, (sums, *parts))
        got = add_cores(keep, swap(send, 0, 1), edge)
        edge = got[4]
        part = [got[0]] + [swap(got[n], n, 0) for n in (1, 2, 3)]
        after = (got[1],)
    else:
        p, hid, flags, edge, grad, grad_out = gates_layer(split, tile, 2, *samples, (w, o))
        after = ()

    returned = from_behind(edge, BOTH, -1)
    input_grad, rest = input_layer(tile, res_grad, p, flags, w, after)
    if split:
        got = add_hop(part, (rest,))
        part = [got[0]] + [swap(got[n], 0, 2 * n) for n in (1, 2, 3)]
        after = (got[1],)
    residual_out, skip_out, input_grad = mixed_layer(
        tile, inputs, hid, o, bias_out, rest, returned, input_grad, after
    )

    if split:
        total, square = add_last(part, lax.axis_size(BOTH), (skip_out,))
        part = [total] + [swap(total, n, 0) for n in (1, 2, 3)]
        squares = lax.all_to_all(square, BOTH, 0, 0, tiled=True)
        fold = lambda v: v.reshape(2, LANES)
        norm, *new = update(
            squares,
            part,
            (conv_first, conv_second, conv_weight),
            (cond_first, cond_second, cond_weight),
            (out_first, out_second, out_weight),
            (fold(bias_first), fold(bias_second), fold(biases)),
        )
        grad_norm = norm[0, 0]
        new = new[:9] + [v.reshape(-1) for v in new[9:]]
    else:
        grad = mixed_columns(grad)
        grad_conv = jnp.stack([grad[0:512], grad[512:1024]], 1)
        grad_bias = jnp.concatenate([grad[1024 + ONES], sums[0]], 0)
        own = (
            lax.psum_scatter(grad_conv, "seq", scatter_dimension=0, tiled=True),
            lax.psum_scatter(grad[1024 : 1024 + MEL], "seq", scatter_dimension=1, tiled=True),
            lax.psum_scatter(grad_out, "seq", scatter_dimension=0, tiled=True),
            lax.psum_scatter(grad_bias, "seq", scatter_dimension=0, tiled=True),
        )
        own = lax.psum(own, "rep")
        grad_norm = jnp.sqrt(lax.psum(sum(jnp.sum(g * g) for g in own), "seq"))
        factor = clip_bound / jnp.maximum(grad_norm, clip_bound)
        new = [
            *adamw_update(own[0], conv_first, conv_second, conv_weight, factor, weight_decay),
            *adamw_update(own[1], cond_first, cond_second, cond_weight, factor, weight_decay),
            *adamw_update(own[2], out_first, out_second, out_weight, factor, weight_decay),
            *adamw_update(own[3], bias_first, bias_second, biases, factor, 0.0),
        ]
    return (residual_out, skip_out, input_grad, grad_norm, *new)


def solution(mesh):
    rows = P(BOTH, None)
    line = P(BOTH)
    conv = P("seq", None, None)
    cond = P(None, "seq")
    out = P("seq", None)
    bias = P("seq")
    placed = (
        rows,
        P(None, BOTH),
        line,
        line,
        rows,
        rows,
        conv,
        cond,
        out,
        bias,
        conv,
        conv,
        cond,
        cond,
        out,
        out,
        bias,
        bias,
    )
    return jax.shard_map(
        local,
        mesh=mesh,
        in_specs=placed,
        out_specs=(rows, rows, rows, P()) + (conv,) * 3 + (cond,) * 3 + (out,) * 3 + (bias,) * 3,
        check_vma=False,
    )
```

time: 467 us -> 188 us (0.40); the launches traced: 459 us -> 187 us
  matrix products: 165 us -> 0 us
  Pallas kernels: 0 us -> 121 us
  blocking collectives: 86.8 us -> 10 us
  waiting for transfers between devices: 85.7 us -> 14.1 us
  local copies, waits for them, and re-layouts: 50.7 us -> 6.42 us
  other arithmetic: 40.2 us -> 0 us
  starting transfers between devices: 9.27 us -> 34.8 us
  between operations: 20.4 us -> 1.15 us
    dot_general x11 -> x0, matrix products: 165 us -> none  [the longest x3 55.9 us: contract_cols(): lax.dot_general(left, right, (((1,), (1,)), ((), ())), preferred_element_...]
    pallas_call x0 -> x10, Pallas kernels: none -> 121 us  [the longest x1 59.8 us: gates_layer(): pl.pallas_call(functools.partial(gates_body, split, subs), grid=(steps,),...]
    reduce_scatter x2 -> x0, waiting for transfers between devices: 46.5 us -> none  [the longest x1 36.5 us: local(): lax.psum_scatter(grads[2], 'seq', scatter_dimension=0, tiled=True)]
    all_gather x2 -> x0, blocking collectives: 37.7 us -> none  [the longest x1 24.6 us: local(): lax.all_gather(lowered[3], 'seq', axis=0, tiled=True)]
    psum x2 -> x0, blocking collectives: 34.2 us -> none  [the longest x1 17.4 us: local(): owned = lax.psum((parts[0], parts[1], parts[2], parts[3]), 'rep')]
    psum x1 -> x0, waiting for transfers between devices: 32.8 us -> none  [local(): owned = lax.psum((parts[0], parts[1], parts[2], parts[3]), 'rep')]
    ppermute x0 -> x21, starting transfers between devices: none -> 27.8 us  [swap(): return lax.ppermute(x, BOTH, pairs)]
    slice x7 -> x1, local copies, waits for them, and re-layouts: 25.1 us -> 0.69 us  [local(): tail_ids = from_behind(utterance[rows - span:], BOTH, 1)]
  transfers between devices with their start and end apart: 9 -> 24, of which waited for: 4 -> 4; matrix products, arithmetic and copies ran while one was open for 37% -> 0% of each run, Pallas kernels for 0% -> 24%
where the time goes in v2:
time: 188 us; the launch traced here: 187 us
  Pallas kernels  121 us (64%)
  starting transfers between devices  34.8 us (19%)
  waiting for transfers between devices  14.1 us (8%)
  blocking collectives  10 us (5%)
  local copies, waits for them, and re-layouts  6.42 us (3%)
    pallas_call x1, Pallas kernels, gates_layer(): pl.pallas_call(functools.partial(gates_body, split, subs), grid=(steps,),...  59.8 us
    ppermute x21, starting transfers between devices, swap(): return lax.ppermute(x, BOTH, pairs)  27.8 us
    pallas_call x1, Pallas kernels, input_layer(): pl.pallas_call(input_body, grid=(steps,), in_specs=[by_row(512), by_row(1...  20.8 us
    ppermute x21, waiting for transfers between devices, swap(): return lax.ppermute(x, BOTH, pairs)  14.1 us
    pallas_call x1, Pallas kernels, mixed_layer(): pl.pallas_call(mixed_body, grid=(total // rows,), in_specs=[by_row, by_ro...  14.1 us
    all_to_all x1, blocking collectives, local(): squares = lax.all_to_all(square, BOTH, 0, 0, tiled=True)  10 us
    ppermute x3, starting transfers between devices, from_behind(): return lax.ppermute(x, axis, pairs)  7.07 us
    pallas_call x1, Pallas kernels, sum_columns(): pl.pallas_call(sums_body, grid=(total // rows,), in_specs=[by_row, by_row...  6.62 us
  transfers between devices with their start and end apart: 24, of which 4 were waited for; matrix products, arithmetic and copies ran while one was open for 0% of the time, Pallas kernels for 24%

profile of v2, /device:TPU:0, one launch (start us, length us, event | category | flops | bytes accessed | tf_op | source)
XLA Modules:
  0.0 187.3 jit_solution(9661438871391548456)
XLA Ops:
  0.6 2.6 %pack_weights.1 = (bf16[4,416,128]{2,1,0:T(8,128)(2,1)}, bf16[416,128]{1,0:T(8,128)(2,1)}) custom-call(f32[64,2,1024]{2,1,0:T(2,128)} %refs_7_.1, f32[80,128]{1,0:T(8,128)} %refs_10_.1, f32[2,128]{1,0:T(2,128)} %bitcast.17, f32[64,1024]{1,0:T(8,128)} %refs_13_.1), custom_call_target="tpu_custom_call" | custom-call | tf_op jit(solution)/shard_map/pack_weights/pallas_call | solution.py:106
  3.3 3.0 %collective-permute-start = (bf16[416,128]{1,0:T(8,128)(2,1)}, bf16[416,128]{1,0:T(8,128)(2,1)S(1)}, u32[]{:S(2)}, u32[]{:S(2)}) collective-permute-start(bf16[416,128]{1,0:T(8,128)(2,1)} %get-tuple-element.56), channel_id=1, source_target_pairs={{0,2},{1,3},{2,0},{3,1},{4,6},{5,7},{6,4},{7,5},{8,10},{9,11},{10,... | collective-permute-start | bytes 319496 | tf_op jit(solution)/shard_map/ppermute | solution.py:46
  6.3 2.6 %collective-permute-start.1 = (bf16[416,128]{1,0:T(8,128)(2,1)}, bf16[416,128]{1,0:T(8,128)(2,1)S(1)}, u32[]{:S(2)}, u32[]{:S(2)}) collective-permute-start(bf16[416,128]{1,0:T(8,128)(2,1)} %get-tuple-element.56), channel_id=1, source_target_pairs={{0,4},{1,5},{2,6},{3,7},{4,0},{5,1},{6,2},{7,3},{8,12},{9,13},{10,... | collective-permute-start | bytes 319496 | tf_op jit(solution)/shard_map/ppermute | solution.py:46
  8.9 0.6 collective-permute-done
  9.5 8.1 %collective-permute-done.1 = bf16[416,128]{1,0:T(8,128)(2,1)S(1)} collective-permute-done((bf16[416,128]{1,0:T(8,128)(2,1)}, bf16[416,128]{1,0:T(8,128)(2,1)S(1)}, u32[]{:S(2)}, u32[]{:S(2)}) %collective-permute-start.1) | collective-permute-done | bytes 106528 | tf_op jit(solution)/shard_map/ppermute | solution.py:46
  17.6 1.6 collective-permute-start.7
  19.2 1.5 collective-permute-start.8
  20.7 0.5 collective-permute-start.9
  21.2 0.7 slice.6
  21.9 2.4 %collective-permute-start.4 = (s32[512]{0:T(512)S(1)}, s32[512]{0:T(512)S(1)}, u32[]{:S(2)}, u32[]{:S(2)}) collective-permute-start(s32[512]{0:T(512)S(1)} %slice.6), channel_id=1, source_target_pairs={{0,1},{1,2},{2,3},{3,4},{4,5},{5,6},{6,7},{7,8},{8,9},{9,10},{10,1... | collective-permute-start | bytes 6152 | tf_op jit(solution)/shard_map/ppermute | solution.py:36
  24.3 1.9 last_rows.1
  26.2 3.2 %collective-permute-start.3 = (bf16[512,512]{1,0:T(8,128)(2,1)}, bf16[512,512]{1,0:T(8,128)(2,1)S(1)}, u32[]{:S(2)}, u32[]{:S(2)}) collective-permute-start(bf16[512,512]{1,0:T(8,128)(2,1)} %last_rows.1), channel_id=1, source_target_pairs={{0,1},{1,2},{2,3},{3,4},{4,5},{5,6},{6,7},{7,8},{8,9},{9,10},{10,1... | collective-permute-start | bytes 1572872 | tf_op jit(solution)/shard_map/ppermute | solution.py:36
  29.4 1.1 collective-permute-start.5
  30.5 1.9 %collective-permute-done.8.refs_6_ = bf16[1248,128]{1,0:T(8,128)(2,1)S(1)} collective-permute-done((bf16[1248,128]{1,0:T(8,128)(2,1)S(1)}, bf16[1248,128]{1,0:T(8,128)(2,1)S(1)}, u32[]{:S(2)}, u32[]{:S(2)}) %collective-permute-start.8) | collective-permute-done | bytes 319520 | tf_op jit(solution)/shard_map/ppermute | solution.py:46
  32.5 0.5 collective-permute-start.11
  33.1 6.6 %sum_columns.1.refs_0_ = f32[8,1024]{1,0:T(8,128)} custom-call(bf16[6144,512]{1,0:T(8,128)(2,1)} %res.5, bf16[6144,512]{1,0:T(8,128)(2,1)} %skp.3, bf16[1248,128]{1,0:T(8,128)(2,1)} %copy-done), custom_call_target="tpu_custom_call" | custom-call | flops 6291456 | bytes 12582912 | tf_op jit(solution)/shard_map/sum_columns/pallas_call | solution.py:229
  39.9 0.7 copy-done.14
  40.5 0.2 copy-done.11
  40.8 0.1 copy-done.20
  40.9 0.1 copy-done.21
  41.0 59.8 %gates_layer.1 = (bf16[6144,1024]{1,0:T(8,128)(2,1)}, bf16[6144,512]{1,0:T(8,128)(2,1)}, bf16[16,6144]{1,0:T(8,128)(2,1)}, bf16[512,512]{1,0:T(8,128)(2,1)}, bf1...) custom-call(bf16[6144,512]{1,0:T(8,128)(2,1)} %x.5, ...), custom_call_target="tpu_custom_call" | custom-call | flops 43486543872 | bytes 49152000 | tf_op jit(solution)/shard_map/gates_layer/pallas_call | solution.py:408
  100.9 0.4 collective-permute-start.13
  101.3 3.4 %collective-permute-done.13.got = bf16[4,4,416,128]{3,2,1,0:T(8,128)(2,1)S(1)} collective-permute-done((bf16[4,4,416,128]{3,2,1,0:T(8,128)(2,1)}, bf16[4,4,416,128]{3,2,1,0:T(8,128)(2,1)S(1)}, u32[]{:S(2)}, u32[]{:S(2)}) %collective-permute-start.13) | collective-permute-done | bytes 1703968 | tf_op jit(solution)/shard_map/ppermute | solution.py:46
  104.7 1.2 copy-done.1
  105.9 4.1 %add_cores.1 = (f32[4,416,128]{2,1,0:T(8,128)}, bf16[4,416,128]{2,1,0:T(8,128)(2,1)}, bf16[4,416,128]{2,1,0:T(8,128)(2,1)}, bf16[4,416,128]{2,1,0:T(8,128)(2,1)}, bf16[512,512]{1,0:T(8,128)(2,1)}) custom-call(bf16[4,4,416,128]{3,2,1,0:T(8,128)(2,1)} %get-tuple-element.64.keep, bf16[4,4,416,128]{3,2,1,0:T(8,128)(2,1)} %copy-done.1, ...), custom_call_target="tpu_custom_call" | custom-call | flops 1000000 | bytes 8000000 | tf_op jit(solution)/shard_map/add_cores/pallas_call | solution.py:506
  110.1 4.6 %collective-permute-start.15 = (bf16[4,416,128]{2,1,0:T(8,128)(2,1)}, bf16[4,416,128]{2,1,0:T(8,128)(2,1)S(1)}, u32[]{:S(2)}, u32[]{:S(2)}) collective-permute-start(bf16[4,416,128]{2,1,0:T(8,128)(2,1)} %get-tuple-element.67.refs_0_), channel_id=1, source_target_pairs={{0,8},{1,9},{2,10},{3,11},{4,12},{5,13},{6,14},{7,15},{8,0},{9,1},... | collective-permute-start | bytes 1277960 | tf_op jit(solution)/shard_map/ppermute | solution.py:46
  114.7 2.0 %collective-permute-start.16 = (bf16[4,416,128]{2,1,0:T(8,128)(2,1)}, bf16[4,416,128]{2,1,0:T(8,128)(2,1)S(1)}, u32[]{:S(2)}, u32[]{:S(2)}) collective-permute-start(bf16[4,416,128]{2,1,0:T(8,128)(2,1)} %get-tuple-element.72), channel_id=1, source_target_pairs={{0,16},{1,17},{2,18},{3,19},{4,20},{5,21},{6,22},{7,23},{8,24},{9,... | collective-permute-start | bytes 1277960 | tf_op jit(solution)/shard_map/ppermute | solution.py:46
  116.6 1.4 collective-permute-start.17
  118.0 1.5 collective-permute-start.14
  119.5 20.8 %input_layer.1 = (bf16[6144,512]{1,0:T(8,128)(2,1)}, f32[512,512]{1,0:T(8,128)}) custom-call(bf16[6144,512]{1,0:T(8,128)(2,1)} %res.5, bf16[6144,1024]{1,0:T(8,128)(2,1)} %get-tuple-element.61.p, bf16[16,6144]{1,0:T(8,128)(2,1)} %get-tuple-element.62.flags, bf16[1152,1024]{1,0:T(8,128)(2,1)} %get-tuple-element.63.w, ...), custom_call_target="tpu_custom_call" | custom-call | flops 12884901888 | bytes 25165824 | tf_op jit(solution)/shard_map/input_layer/pallas_call | solution.py:475
  140.3 0.7 copy-done.2
  141.0 0.1 copy-done.3
  141.1 0.1 copy-done.4
  141.3 2.4 %add_hop.1 = (f32[416,128]{1,0:T(8,128)}, bf16[416,128]{1,0:T(8,128)(2,1)}, bf16[416,128]{1,0:T(8,128)(2,1)}, bf16[416,128]{1,0:T(8,128)(2,1)}) custom-call(f32[4,416,128]{2,1,0:T(8,128)} %get-tuple-element.71.keep, bf16[4,416,128]{2,1,0:T(8,128)(2,1)} %copy-done.2, bf16[4,416,128]{2,1,0:T(8,128)(2,1)} %copy-done.3, bf16[4,416,128]{2,1,0:T(8,128)(2,1)} %copy-done.4, ...), custom_call_target="tpu_custom_call" | custom-call | flops 1000000 | bytes 3000000 | tf_op jit(solution)/shard_map/add_hop/pallas_call | solution.py:527
  143.6 1.8 collective-permute-start.18
  145.5 0.3 collective-permute-start.19
  145.8 2.3 %collective-permute-start.20 = (bf16[416,128]{1,0:T(8,128)(2,1)}, bf16[416,128]{1,0:T(8,128)(2,1)S(1)}, u32[]{:S(2)}, u32[]{:S(2)}) collective-permute-start(bf16[416,128]{1,0:T(8,128)(2,1)} %get-tuple-element.80), channel_id=1, source_target_pairs={{0,6},{1,7},{2,4},{3,5},{4,2},{5,3},{6,0},{7,1},{8,14},{9,15},{10,... | collective-permute-start | bytes 319496 | tf_op jit(solution)/shard_map/ppermute | solution.py:46
  148.0 0.8 copy-done.12
  148.8 14.1 %mixed_layer.1 = (bf16[6144,512]{1,0:T(8,128)(2,1)}, bf16[6144,512]{1,0:T(8,128)(2,1)}, bf16[6144,512]{1,0:T(8,128)(2,1)}) custom-call(bf16[6144,512]{1,0:T(8,128)(2,1)} %x.5, bf16[6144,512]{1,0:T(8,128)(2,1)} %get-tuple-element.58.hid, bf16[512,1024]{1,0:T(8,128)(2,1)} %get-tuple-element.59.o, ...), custom_call_target="tpu_custom_call", output_to_operand_aliasing={{2}: (6, {})} | custom-call | flops 6442450944 | bytes 25165824 | tf_op jit(solution)/shard_map/mixed_layer/pallas_call | solution.py:437
  163.0 0.6 copy-done.8
  163.6 1.9 %add_last.1 = (f32[416,128]{1,0:T(8,128)}, f32[32,128]{1,0:T(8,128)}) custom-call(f32[416,128]{1,0:T(8,128)} %get-tuple-element.78.keep, bf16[416,128]{1,0:T(8,128)(2,1)} %copy-done.8, bf16[416,128]{1,0:T(8,128)(2,1)} %copy-done.9, bf16[416,128]{1,0:T(8,128)(2,1)} %copy-done.10, bf16[6144,512]{1,0:T(8,128)(2,1)} %get-tuple-element.41.refs_0_), custom_call_target="tpu_custom_call" | custom-call | flops 1000000 | bytes 1000000 | tf_op jit(solution)/shard_map/add_last/pallas_call | solution.py:545
  165.5 1.5 collective-permute-start.21
  167.1 1.2 collective-permute-start.22
  168.3 1.4 collective-permute-start.23
  169.7 10.0 %all_to_all.11 = f32[32,1,128]{2,1,0:T(1,128)} all-to-all(f32[32,1,128]{2,1,0:T(1,128)} %bitcast.16), channel_id=1, replica_groups=mesh['rep'=4,'seq'=8] {'rep','seq'}, dimensions={0} | all-to-all | bytes 32768 | tf_op jit(solution)/shard_map/all_to_all | solution.py:685
  179.7 0.6 copy-done.5
  180.5 0.1 copy-done.7
  180.6 6.6 %update.1 = (f32[1,128]{1,0:T(1,128)}, f32[64,2,1024]{2,1,0:T(2,128)}, f32[64,2,1024]{2,1,0:T(2,128)}, f32[64,2,1024]{2,1,0:T(2,128)}, f32[80,128]{1,0:T(8,128)}...) custom-call(f32[32,128]{1,0:T(8,128)} %bitcast.15, ...), custom_call_target="tpu_custom_call" | custom-call | tf_op jit(solution)/shard_map/update/pallas_call | solution.py:603
  (61 shorter events, 0.5 us)
Async XLA Ops:
  3.3 26.1 %copy-start.13 = (bf16[4,416,128]{2,1,0:T(8,128)(2,1)S(1)}, bf16[4,416,128]{2,1,0:T(8,128)(2,1)}, u32[]{:S(2)}) copy-start(bf16[4,416,128]{2,1,0:T(8,128)(2,1)} %get-tuple-element.57.refs_1_) | copy-start | bytes 1277956
  3.3 6.2 %collective-permute-start = (bf16[416,128]{1,0:T(8,128)(2,1)}, bf16[416,128]{1,0:T(8,128)(2,1)S(1)}, u32[]{:S(2)}, u32[]{:S(2)}) collective-permute-start(bf16[416,128]{1,0:T(8,128)(2,1)} %get-tuple-element.56), channel_id=1, source_target_pairs={{0,2},{1,3},{2,0},{3,1},{4,6},{5,7},{6,4},{7,5},{8,10},{9,11},{10,... | collective-permute-start | bytes 319496 | tf_op jit(solution)/shard_map/ppermute | solution.py:46
  6.3 11.3 %collective-permute-start.1 = (bf16[416,128]{1,0:T(8,128)(2,1)}, bf16[416,128]{1,0:T(8,128)(2,1)S(1)}, u32[]{:S(2)}, u32[]{:S(2)}) collective-permute-start(bf16[416,128]{1,0:T(8,128)(2,1)} %get-tuple-element.56), channel_id=1, source_target_pairs={{0,4},{1,5},{2,6},{3,7},{4,0},{5,1},{6,2},{7,3},{8,12},{9,13},{10,... | collective-permute-start | bytes 319496 | tf_op jit(solution)/shard_map/ppermute | solution.py:46
  8.9 8.7 %collective-permute-start.2 = (bf16[416,128]{1,0:T(8,128)(2,1)}, bf16[416,128]{1,0:T(8,128)(2,1)S(1)}, u32[]{:S(2)}, u32[]{:S(2)}) collective-permute-start(bf16[416,128]{1,0:T(8,128)(2,1)} %get-tuple-element.56), channel_id=1, source_target_pairs={{0,6},{1,7},{2,4},{3,5},{4,2},{5,3},{6,0},{7,1},{8,14},{9,15},{10,... | collective-permute-start | bytes 319496 | tf_op jit(solution)/shard_map/ppermute | solution.py:46
  17.6 6.7 %copy-start = (bf16[1248,128]{1,0:T(8,128)(2,1)}, bf16[1248,128]{1,0:T(8,128)(2,1)S(1)}, u32[]{:S(2)}) copy-start(bf16[1248,128]{1,0:T(8,128)(2,1)S(1)} %constant_dynamic-update-slice_fusion._.refs_0_.refs_3_) | copy-start | bytes 958468
  17.6 11.8 %collective-permute-start.7 = (bf16[1248,128]{1,0:T(8,128)(2,1)S(1)}, bf16[1248,128]{1,0:T(8,128)(2,1)S(1)}, u32[]{:S(2)}, u32[]{:S(2)}) collective-permute-start(bf16[1248,128]{1,0:T(8,128)(2,1)S(1)} %constant_dynamic-update-slice_fusion._.refs_0_.refs_3_), channel_id=1, source_target_pairs={{0,8},{1,9},{2,10},{3,11},{4,12},{5,13},{6,14},{7,15},{8,0},{9,1},... | collective-permute-start | bytes 958472 | tf_op jit(solution)/shard_map/ppermute | solution.py:46
  19.2 13.3 %collective-permute-start.8 = (bf16[1248,128]{1,0:T(8,128)(2,1)S(1)}, bf16[1248,128]{1,0:T(8,128)(2,1)S(1)}, u32[]{:S(2)}, u32[]{:S(2)}) collective-permute-start(bf16[1248,128]{1,0:T(8,128)(2,1)S(1)} %constant_dynamic-update-slice_fusion._.refs_0_.refs_3_), channel_id=1, source_target_pairs={{0,16},{1,17},{2,18},{3,19},{4,20},{5,21},{6,22},{7,23},{8,24},{9,... | collective-permute-start | bytes 958472 | tf_op jit(solution)/shard_map/ppermute | solution.py:46
  20.7 11.8 %collective-permute-start.9 = (bf16[1248,128]{1,0:T(8,128)(2,1)S(1)}, bf16[1248,128]{1,0:T(8,128)(2,1)S(1)}, u32[]{:S(2)}, u32[]{:S(2)}) collective-permute-start(bf16[1248,128]{1,0:T(8,128)(2,1)S(1)} %constant_dynamic-update-slice_fusion._.refs_0_.refs_3_), channel_id=1, source_target_pairs={{0,24},{1,25},{2,26},{3,27},{4,28},{5,29},{6,30},{7,31},{8,16},{9,... | collective-permute-start | bytes 958472 | tf_op jit(solution)/shard_map/ppermute | solution.py:46
  21.2 11.8 %collective-permute-start.6 = (bf16[1248,128]{1,0:T(8,128)(2,1)S(1)}, bf16[1248,128]{1,0:T(8,128)(2,1)S(1)}, u32[]{:S(2)}, u32[]{:S(2)}) collective-permute-start(bf16[1248,128]{1,0:T(8,128)(2,1)S(1)} %constant_dynamic-update-slice_fusion._.refs_0_.refs_3_), channel_id=1, source_target_pairs={{0,1},{1,0},{2,3},{3,2},{4,5},{5,4},{6,7},{7,6},{8,9},{9,8},{10,11... | collective-permute-start | bytes 958472 | tf_op jit(solution)/shard_map/ppermute | solution.py:46
  21.9 4.3 %collective-permute-start.4 = (s32[512]{0:T(512)S(1)}, s32[512]{0:T(512)S(1)}, u32[]{:S(2)}, u32[]{:S(2)}) collective-permute-start(s32[512]{0:T(512)S(1)} %slice.6), channel_id=1, source_target_pairs={{0,1},{1,2},{2,3},{3,4},{4,5},{5,6},{6,7},{7,8},{8,9},{9,10},{10,1... | collective-permute-start | bytes 6152 | tf_op jit(solution)/shard_map/ppermute | solution.py:36
  26.2 13.6 %copy-start.22 = (s32[512]{0:T(512)}, s32[512]{0:T(512)S(1)}, u32[]{:S(2)}) copy-start(s32[512]{0:T(512)S(1)} %collective-permute-done.4) | copy-start | bytes 6148
  26.2 13.6 %collective-permute-start.3 = (bf16[512,512]{1,0:T(8,128)(2,1)}, bf16[512,512]{1,0:T(8,128)(2,1)S(1)}, u32[]{:S(2)}, u32[]{:S(2)}) collective-permute-start(bf16[512,512]{1,0:T(8,128)(2,1)} %last_rows.1), channel_id=1, source_target_pairs={{0,1},{1,2},{2,3},{3,4},{4,5},{5,6},{6,7},{7,8},{8,9},{9,10},{10,1... | collective-permute-start | bytes 1572872 | tf_op jit(solution)/shard_map/ppermute | solution.py:36
  29.4 10.3 %copy-start.15 = (bf16[1248,128]{1,0:T(8,128)(2,1)}, bf16[1248,128]{1,0:T(8,128)(2,1)S(1)}, u32[]{:S(2)}) copy-start(bf16[1248,128]{1,0:T(8,128)(2,1)S(1)} %collective-permute-done.7.refs_5_) | copy-start | bytes 958468
  29.4 10.3 %collective-permute-start.5 = (bf16[4,416,128]{2,1,0:T(8,128)(2,1)S(1)}, bf16[4,416,128]{2,1,0:T(8,128)(2,1)S(1)}, u32[]{:S(2)}, u32[]{:S(2)}) collective-permute-start(bf16[4,416,128]{2,1,0:T(8,128)(2,1)S(1)} %copy-done.13), channel_id=1, source_target_pairs={{0,1},{1,0},{2,3},{3,2},{4,5},{5,4},{6,7},{7,6},{8,9},{9,8},{10,11... | collective-permute-start | bytes 1277960 | tf_op jit(solution)/shard_map/ppermute | solution.py:46
  32.5 7.2 %copy-start.16 = (bf16[1248,128]{1,0:T(8,128)(2,1)}, bf16[1248,128]{1,0:T(8,128)(2,1)S(1)}, u32[]{:S(2)}) copy-start(bf16[1248,128]{1,0:T(8,128)(2,1)S(1)} %collective-permute-done.8.refs_6_) | copy-start | bytes 958468
  32.5 7.3 %collective-permute-start.10 = (bf16[1248,128]{1,0:T(8,128)(2,1)S(1)}, bf16[1248,128]{1,0:T(8,128)(2,1)S(1)}, u32[]{:S(2)}, u32[]{:S(2)}) collective-permute-start(bf16[1248,128]{1,0:T(8,128)(2,1)S(1)} %collective-permute-done.7.refs_5_), channel_id=1, source_target_pairs={{0,1},{1,0},{2,3},{3,2},{4,5},{5,4},{6,7},{7,6},{8,9},{9,8},{10,11... | collective-permute-start | bytes 958472 | tf_op jit(solution)/shard_map/ppermute | solution.py:46
  32.5 7.2 %copy-start.17 = (bf16[1248,128]{1,0:T(8,128)(2,1)}, bf16[1248,128]{1,0:T(8,128)(2,1)S(1)}, u32[]{:S(2)}) copy-start(bf16[1248,128]{1,0:T(8,128)(2,1)S(1)} %collective-permute-done.9.refs_7_) | copy-start | bytes 958468
  32.5 7.3 %collective-permute-start.11 = (bf16[1248,128]{1,0:T(8,128)(2,1)S(1)}, bf16[1248,128]{1,0:T(8,128)(2,1)S(1)}, u32[]{:S(2)}, u32[]{:S(2)}) collective-permute-start(bf16[1248,128]{1,0:T(8,128)(2,1)S(1)} %collective-permute-done.8.refs_6_), channel_id=1, source_target_pairs={{0,1},{1,0},{2,3},{3,2},{4,5},{5,4},{6,7},{7,6},{8,9},{9,8},{10,11... | collective-permute-start | bytes 958472 | tf_op jit(solution)/shard_map/ppermute | solution.py:46
  33.0 6.7 %copy-start.18 = (bf16[1248,128]{1,0:T(8,128)(2,1)}, bf16[1248,128]{1,0:T(8,128)(2,1)S(1)}, u32[]{:S(2)}) copy-start(bf16[1248,128]{1,0:T(8,128)(2,1)S(1)} %collective-permute-done.6.refs_4_) | copy-start | bytes 958468
  33.0 6.8 %collective-permute-start.12 = (bf16[1248,128]{1,0:T(8,128)(2,1)S(1)}, bf16[1248,128]{1,0:T(8,128)(2,1)S(1)}, u32[]{:S(2)}, u32[]{:S(2)}) collective-permute-start(bf16[1248,128]{1,0:T(8,128)(2,1)S(1)} %collective-permute-done.9.refs_7_), channel_id=1, source_target_pairs={{0,1},{1,0},{2,3},{3,2},{4,5},{5,4},{6,7},{7,6},{8,9},{9,8},{10,11... | collective-permute-start | bytes 958472 | tf_op jit(solution)/shard_map/ppermute | solution.py:46
  39.8 0.8 copy-start.14
  39.8 0.9 copy-start.11
  39.8 1.0 copy-start.19
  39.8 1.1 copy-start.20
  39.8 1.2 copy-start.21
  100.9 3.9 %collective-permute-start.13 = (bf16[4,4,416,128]{3,2,1,0:T(8,128)(2,1)}, bf16[4,4,416,128]{3,2,1,0:T(8,128)(2,1)S(1)}, u32[]{:S(2)}, u32[]{:S(2)}) collective-permute-start(bf16[4,4,416,128]{3,2,1,0:T(8,128)(2,1)} %get-tuple-element.65), channel_id=1, source_target_pairs={{0,1},{1,0},{2,3},{3,2},{4,5},{5,4},{6,7},{7,6},{8,9},{9,8},{10,11... | collective-permute-start | bytes 5111816 | tf_op jit(solution)/shard_map/ppermute | solution.py:46
  104.7 1.2 copy-start.1
  110.1 30.2 %collective-permute-start.15 = (bf16[4,416,128]{2,1,0:T(8,128)(2,1)}, bf16[4,416,128]{2,1,0:T(8,128)(2,1)S(1)}, u32[]{:S(2)}, u32[]{:S(2)}) collective-permute-start(bf16[4,416,128]{2,1,0:T(8,128)(2,1)} %get-tuple-element.67.refs_0_), channel_id=1, source_target_pairs={{0,8},{1,9},{2,10},{3,11},{4,12},{5,13},{6,14},{7,15},{8,0},{9,1},... | collective-permute-start | bytes 1277960 | tf_op jit(solution)/shard_map/ppermute | solution.py:46
  114.7 25.6 %collective-permute-start.16 = (bf16[4,416,128]{2,1,0:T(8,128)(2,1)}, bf16[4,416,128]{2,1,0:T(8,128)(2,1)S(1)}, u32[]{:S(2)}, u32[]{:S(2)}) collective-permute-start(bf16[4,416,128]{2,1,0:T(8,128)(2,1)} %get-tuple-element.72), channel_id=1, source_target_pairs={{0,16},{1,17},{2,18},{3,19},{4,20},{5,21},{6,22},{7,23},{8,24},{9,... | collective-permute-start | bytes 1277960 | tf_op jit(solution)/shard_map/ppermute | solution.py:46
  116.6 23.7 %collective-permute-start.17 = (bf16[4,416,128]{2,1,0:T(8,128)(2,1)}, bf16[4,416,128]{2,1,0:T(8,128)(2,1)S(1)}, u32[]{:S(2)}, u32[]{:S(2)}) collective-permute-start(bf16[4,416,128]{2,1,0:T(8,128)(2,1)} %get-tuple-element.73), channel_id=1, source_target_pairs={{0,24},{1,25},{2,26},{3,27},{4,28},{5,29},{6,30},{7,31},{8,16},{9,... | collective-permute-start | bytes 1277960 | tf_op jit(solution)/shard_map/ppermute | solution.py:46
  118.0 30.0 %collective-permute-start.14 = (bf16[512,512]{1,0:T(8,128)(2,1)}, bf16[512,512]{1,0:T(8,128)(2,1)S(1)}, u32[]{:S(2)}, u32[]{:S(2)}) collective-permute-start(bf16[512,512]{1,0:T(8,128)(2,1)} %get-tuple-element.69), channel_id=1, source_target_pairs={{1,0},{2,1},{3,2},{4,3},{5,4},{6,5},{7,6},{8,7},{9,8},{10,9},{11,1... | collective-permute-start | bytes 1572872 | tf_op jit(solution)/shard_map/ppermute | solution.py:36
  140.2 0.8 copy-start.2
  140.3 0.9 copy-start.3
  140.3 1.0 copy-start.4
  143.6 19.3 %collective-permute-start.18 = (bf16[416,128]{1,0:T(8,128)(2,1)}, bf16[416,128]{1,0:T(8,128)(2,1)S(1)}, u32[]{:S(2)}, u32[]{:S(2)}) collective-permute-start(bf16[416,128]{1,0:T(8,128)(2,1)} %get-tuple-element.74.refs_1_), channel_id=1, source_target_pairs={{0,2},{1,3},{2,0},{3,1},{4,6},{5,7},{6,4},{7,5},{8,10},{9,11},{10,... | collective-permute-start | bytes 319496 | tf_op jit(solution)/shard_map/ppermute | solution.py:46
  145.5 17.5 %collective-permute-start.19 = (bf16[416,128]{1,0:T(8,128)(2,1)}, bf16[416,128]{1,0:T(8,128)(2,1)S(1)}, u32[]{:S(2)}, u32[]{:S(2)}) collective-permute-start(bf16[416,128]{1,0:T(8,128)(2,1)} %get-tuple-element.79), channel_id=1, source_target_pairs={{0,4},{1,5},{2,6},{3,7},{4,0},{5,1},{6,2},{7,3},{8,12},{9,13},{10,... | collective-permute-start | bytes 319496 | tf_op jit(solution)/shard_map/ppermute | solution.py:46
  145.8 17.2 %collective-permute-start.20 = (bf16[416,128]{1,0:T(8,128)(2,1)}, bf16[416,128]{1,0:T(8,128)(2,1)S(1)}, u32[]{:S(2)}, u32[]{:S(2)}) collective-permute-start(bf16[416,128]{1,0:T(8,128)(2,1)} %get-tuple-element.80), channel_id=1, source_target_pairs={{0,6},{1,7},{2,4},{3,5},{4,2},{5,3},{6,0},{7,1},{8,14},{9,15},{10,... | collective-permute-start | bytes 319496 | tf_op jit(solution)/shard_map/ppermute | solution.py:46
  148.0 0.8 copy-start.12
  162.9 0.6 copy-start.8
  162.9 0.7 copy-start.9
  162.9 0.7 copy-start.10
  165.5 14.2 %collective-permute-start.21 = (f32[416,128]{1,0:T(8,128)}, f32[416,128]{1,0:T(8,128)S(1)}, u32[]{:S(2)}, u32[]{:S(2)}) collective-permute-start(f32[416,128]{1,0:T(8,128)} %get-tuple-element.82.refs_1_), channel_id=1, source_target_pairs={{0,8},{1,9},{2,10},{3,11},{4,12},{5,13},{6,14},{7,15},{8,0},{9,1},... | collective-permute-start | bytes 638984 | tf_op jit(solution)/shard_map/ppermute | solution.py:46
  167.1 12.6 %collective-permute-start.22 = (f32[416,128]{1,0:T(8,128)}, f32[416,128]{1,0:T(8,128)S(1)}, u32[]{:S(2)}, u32[]{:S(2)}) collective-permute-start(f32[416,128]{1,0:T(8,128)} %get-tuple-element.82.refs_1_), channel_id=1, source_target_pairs={{0,16},{1,17},{2,18},{3,19},{4,20},{5,21},{6,22},{7,23},{8,24},{9,... | collective-permute-start | bytes 638984 | tf_op jit(solution)/shard_map/ppermute | solution.py:46
  168.3 11.4 %collective-permute-start.23 = (f32[416,128]{1,0:T(8,128)}, f32[416,128]{1,0:T(8,128)S(1)}, u32[]{:S(2)}, u32[]{:S(2)}) collective-permute-start(f32[416,128]{1,0:T(8,128)} %get-tuple-element.82.refs_1_), channel_id=1, source_target_pairs={{0,24},{1,25},{2,26},{3,27},{4,28},{5,29},{6,30},{7,31},{8,16},{9,... | collective-permute-start | bytes 638984 | tf_op jit(solution)/shard_map/ppermute | solution.py:46
  179.7 0.7 copy-start.5
  179.7 0.8 copy-start.6
  179.7 0.8 copy-start.7

commit v3 on v2

--- a/solution.py
+++ b/solution.py
@@ -25,6 +25,8 @@
 KEEP = 81
 LINK = 82
 ROWS = 512
+GATES_MIB = 52
+ARRIVE = 10**10
 BF = jnp.bfloat16
 F32 = jnp.float32
 BOTH = ("rep", "seq")
@@ -62,8 +64,11 @@
     return jnp.dot(left, right, preferred_element_type=F32)
 
 
-def params(**more):
-    return pltpu.CompilerParams(vmem_limit_bytes=58 * 2**20, **more)
+TOKEN = jax.ShapeDtypeStruct((8, LANES), F32)
+
+
+def params(mib=24):
+    return pltpu.CompilerParams(vmem_limit_bytes=mib * 2**20)
 
 
 def cost(flops, moved):
@@ -112,7 +117,7 @@
             jax.ShapeDtypeStruct((PART, LANES), BF),
         ],
         scratch_shapes=[pltpu.VMEM((AUX, LANES), BF)],
-        compiler_params=params(),
+        compiler_params=params(58),
         name="pack_weights",
     )(conv, cond, bias, out)
 
@@ -128,9 +133,25 @@
         in_specs=[pl.BlockSpec((ROWS, x.shape[1]), lambda i: (x.shape[0] // ROWS - 1, 0)), ANY],
         out_specs=whole((ROWS, x.shape[1])),
         out_shape=jax.ShapeDtypeStruct((ROWS, x.shape[1]), x.dtype),
-        compiler_params=params(),
+        compiler_params=params(63),
         name="last_rows",
     )(x, after)
+
+
+def arrive_body(_, token):
+    token[...] = jnp.zeros_like(token)
+
+
+def arrived_by(array):
+    return pl.pallas_call(
+        arrive_body,
+        in_specs=[ANY],
+        out_specs=VMEM,
+        out_shape=TOKEN,
+        compiler_params=params(63),
+        cost_estimate=cost(ARRIVE, 4096),
+        name="arrived_by",
+    )(array)
 
 
 def mixed_block(block):
@@ -211,33 +232,6 @@
     return mixed_columns(w), out_all, bias_out
 
 
-def sums_body(res, skp, *refs):
-    sums = refs[-1]
-
-    @pl.when(pl.program_id(0) == 0)
-    def _():
-        sums[...] = jnp.zeros_like(sums)
-
-    for n, part in enumerate((res, skp)):
-        total = jnp.sum(part[...].astype(F32), 0, keepdims=True)
-        sums[:, n * 512 : (n + 1) * 512] += jnp.broadcast_to(total, (8, 512))
-
-
-def sum_columns(rows, res, skp, after):
-    total = res.shape[0]
-    by_row = pl.BlockSpec((rows, 512), lambda i: (i, 0))
-    return pl.pallas_call(
-        sums_body,
-        grid=(total // rows,),
-        in_specs=[by_row, by_row] + [ANY] * len(after),
-        out_specs=whole((8, 1024)),
-        out_shape=jax.ShapeDtypeStruct((8, 1024), F32),
-        compiler_params=params(),
-        cost_estimate=cost(total * 1024, total * 2048),
-        name="sum_columns",
-    )(res, skp, *after)
-
-
 def emit_pieces(outs, write):
     core, rep, z = spot()
     for c, dest in enumerate(outs):
@@ -259,11 +253,11 @@
 
 def gates_body(split, subs, x, tail, mel, keep, ids, tail_ids, res, skp, *refs):
     if split:
-        sums, parts, refs = refs[0], refs[1:11], refs[11:]
+        parts, refs = refs[0:10], refs[11:]
         p, hid, flags, edge, w, o, bias_out, keep_out, send_out = refs[:9]
-        xe, carry, carry_ids, acc, acc_out, small, small_low = refs[9:]
+        xe, carry, carry_ids, acc, acc_out, sums, small, small_low, arrived, *held = refs[9:]
     else:
-        w, o, p, hid, flags, edge, grad, grad_out, xe, carry, carry_ids, acc, acc_out = refs
+        w, o, p, hid, flags, edge, grad, grad_out, sums, xe, carry, carry_ids, acc, acc_out = refs
     step, last = pl.program_id(0), pl.num_programs(0) - 1
     rows, half = x.shape[0], p.shape[1] // 4
 
@@ -273,8 +267,17 @@
         carry_ids[...] = jnp.where(lax.axis_index(BOTH) > 0, tail_ids[...], -1)
         acc[...] = jnp.zeros_like(acc)
         acc_out[...] = jnp.zeros_like(acc_out)
+        sums[...] = jnp.zeros_like(sums)
         if split:
-            unpack(parts, w, o, bias_out, small_low)
+            copies = [
+                pltpu.make_async_copy(part, here, arrived.at[n])
+                for n, (part, here) in enumerate(zip(parts, held))
+            ]
+            for copy in copies:
+                copy.start()
+            for copy in copies:
+                copy.wait()
+            unpack(held, w, o, bias_out, small_low)
 
     ids_now = ids[...]
     ids_past = carry_ids[...]
@@ -320,6 +323,9 @@
     acc[...] += tn_dot(xe[...], p[...])
     acc_out[:, 0:512] += tn_dot(hid[...], res[...])
     acc_out[:, 512:1024] += tn_dot(hid[...], skp[...])
+    for n, part in enumerate((res, skp)):
+        total = jnp.sum(part[...].astype(F32), 0, keepdims=True)
+        sums[:, n * 512 : (n + 1) * 512] += jnp.broadcast_to(total, (8, 512))
 
     @pl.when(step == 0)
     def _():
@@ -370,7 +376,7 @@
         whole((1, ROWS)),
         by_row(512),
         by_row(512),
-    ] + [whole(e.shape) for e in extra]
+    ] + [ANY if split else whole(e.shape) for e in extra]
     out_specs = [
         by_row(1024),
         by_row(512),
@@ -392,7 +398,7 @@
             ((4, 4, PART, LANES), BF),
         ]
     else:
-        more = [((1024 + AUX, 1024), F32), ((512, 1024), F32)]
+        more = [((1024 + AUX, 1024), F32), ((512, 1024), F32), ((8, 1024), F32)]
     for shape, dtype in more:
         out_specs.append(whole(shape))
         out_shape.append(jax.ShapeDtypeStruct(shape, dtype))
@@ -404,7 +410,13 @@
         pltpu.VMEM((512, 1024), F32),
     ]
     if split:
-        scratch += [pltpu.VMEM((8, AUX, LANES), F32), pltpu.VMEM((8, AUX, LANES), BF)]
+        scratch += [
+            pltpu.VMEM((8, 1024), F32),
+            pltpu.VMEM((8, AUX, LANES), F32),
+            pltpu.VMEM((8, AUX, LANES), BF),
+            pltpu.SemaphoreType.DMA((10,)),
+        ]
+        scratch += [pltpu.VMEM(e.shape, e.dtype) for e in extra[:10]]
     return pl.pallas_call(
         functools.partial(gates_body, split, subs),
         grid=(steps,),
@@ -412,14 +424,14 @@
         out_specs=out_specs,
         out_shape=out_shape,
         scratch_shapes=scratch,
-        compiler_params=params(),
+        compiler_params=params(GATES_MIB),
         cost_estimate=cost(6.75 * 2 * total * 512 * 1024, total * 8000),
         name="gates_layer",
     )(x, tail, mel, keep, ids, tail_ids, res, skp, *extra)
 
 
 def mixed_body(x, hid, o, bias, rest, edge, *refs):
-    residual, skip, patch = refs[-3:]
+    residual, skip, patch, token = refs[-4:]
     mixed = dot(hid[...], o[...]) + bias[0:1, :]
     residual[...] = (x[...].astype(F32) + mixed[:, 0:512]).astype(BF)
     skip[...] = mixed[:, 512:1024].astype(BF)
@@ -427,6 +439,7 @@
     @pl.when(pl.program_id(0) == 0)
     def _():
         patch[...] = (rest[...] + edge[...].astype(F32)).astype(BF)
+        token[...] = jnp.zeros_like(token)
 
 
 def mixed_layer(rows, x, hid, o, bias, rest, edge, input_grad, after):
@@ -439,17 +452,17 @@
         grid=(total // rows,),
         in_specs=[by_row, by_row, whole((512, 1024)), whole((8, 1024)), whole((ROWS, 512)), whole((ROWS, 512))]
         + [ANY] * (1 + len(after)),
-        out_specs=[by_row, by_row, last],
-        out_shape=[jax.ShapeDtypeStruct((total, 512), BF)] * 3,
+        out_specs=[by_row, by_row, last, whole(TOKEN.shape)],
+        out_shape=[jax.ShapeDtypeStruct((total, 512), BF)] * 3 + [TOKEN],
         input_output_aliases={6: 2},
-        compiler_params=params(),
+        compiler_params=params(58),
         cost_estimate=cost(2 * total * 512 * 1024, total * 4096),
         name="mixed_layer",
     )(*operands)
 
 
 def input_body(res, p, flags, w, *refs):
-    out, rest, carry = refs[-3:]
+    out, rest, token, carry = refs[-4:]
     step = pl.program_id(0)
     rows = res.shape[0]
     link = flags[...].T[:, LINK - MEL : LINK - MEL + 1].astype(F32)
@@ -461,6 +474,7 @@
     def _():
         rest[...] = now[rows - ROWS :]
         carry[...] = jnp.zeros_like(carry)
+        token[...] = jnp.zeros_like(token)
 
     if rows > ROWS:
         out[0 : rows - ROWS, :] = (now[0 : rows - ROWS] + past[ROWS:]).astype(BF)
@@ -482,42 +496,42 @@
             pl.BlockSpec((1024, 1024), lambda i: (0, 0)),
         ]
         + [ANY] * len(after),
-        out_specs=[by_row(512), whole((ROWS, 512))],
+        out_specs=[by_row(512), whole((ROWS, 512)), whole(TOKEN.shape)],
         out_shape=[
             jax.ShapeDtypeStruct((total, 512), BF),
             jax.ShapeDtypeStruct((ROWS, 512), F32),
+            TOKEN,
         ],
         scratch_shapes=[pltpu.VMEM((ROWS, 512), F32)],
-        compiler_params=params(),
+        compiler_params=params(58),
         cost_estimate=cost(4 * total * 512 * 1024, total * 4096),
         name="input_layer",
     )(res, p, flags, w, *after)
 
 
-def cores_body(keep, got, edge, *outs):
+def cores_body(keep, got, *outs):
+    outs[4][...] = jnp.zeros_like(outs[4])
     for n in range(4):
         outs[n][...] = (keep[n].astype(F32) + got[n].astype(F32)).astype(outs[n].dtype)
-    outs[4][...] = edge[...]
-
-
-def add_cores(keep, got, edge):
+
+
+def add_cores(keep, got):
     spec = pl.BlockSpec((4, 1, PART, LANES), lambda i: (0, i, 0, 0))
-    part = pl.BlockSpec((ROWS // 4, 512), lambda i: (i, 0))
     return pl.pallas_call(
         cores_body,
         grid=(4,),
-        in_specs=[spec, spec, part],
-        out_specs=[pl.BlockSpec((1, PART, LANES), lambda i: (i, 0, 0))] * 4 + [part],
-        out_shape=[jax.ShapeDtypeStruct((4, PART, LANES), BF if n else F32) for n in range(4)]
-        + [jax.ShapeDtypeStruct(edge.shape, BF)],
+        in_specs=[spec, spec],
+        out_specs=[pl.BlockSpec((1, PART, LANES), lambda i: (i, 0, 0))] * 4 + [whole(TOKEN.shape)],
+        out_shape=[jax.ShapeDtypeStruct((4, PART, LANES), BF if n else F32) for n in range(4)] + [TOKEN],
         compiler_params=params(),
         cost_estimate=cost(10**6, 8 * 10**6),
         name="add_cores",
-    )(keep, got, edge)
+    )(keep, got)
 
 
 def hop_body(keep, g1, g2, g3, *refs):
-    outs = refs[-4:]
+    outs = refs[-5:]
+    outs[4][...] = jnp.zeros_like(outs[4])
     for n in range(4):
         total = keep[n] + g1[n].astype(F32) + g2[n].astype(F32) + g3[n].astype(F32)
         outs[n][...] = total.astype(outs[n].dtype)
@@ -527,8 +541,8 @@
     return pl.pallas_call(
         hop_body,
         in_specs=[VMEM] * 4 + [ANY] * len(after),
-        out_specs=[VMEM] * 4,
-        out_shape=[jax.ShapeDtypeStruct((PART, LANES), BF if n else F32) for n in range(4)],
+        out_specs=[VMEM] * 5,
+        out_shape=[jax.ShapeDtypeStruct((PART, LANES), BF if n else F32) for n in range(4)] + [TOKEN],
         compiler_params=params(),
         cost_estimate=cost(10**6, 3 * 10**6),
         name="add_hop",
@@ -638,16 +652,16 @@
 
     if split:
         own, first = pack_weights(conv_weight, cond_weight, biases.reshape(2, LANES), out_weight)
-        stack = jnp.concatenate([swap(first, 0, 2 * j) for j in (1, 2, 3)], 0)
+        along = [swap(first, 0, 2 * j) for j in (1, 2, 3)]
+        tail = from_behind(last_rows(inputs, along[0]), BOTH, 1)
+        stack = jnp.concatenate(along, 0)
+        here = (arrived_by(tail),)
         parts = across_hops(own, stack)
-        sums = sum_columns(2 * tile, res_grad, skip_grad, (stack,))
-        last = last_rows(inputs, stack)
     else:
         w, o, bias_out = gather_plain(conv_weight, out_weight, cond_weight, biases)
-        sums = sum_columns(2 * tile, res_grad, skip_grad, ())
-        last = inputs[rows - span :]
-
-    tail = from_behind(last, BOTH, 1)
+        tail = from_behind(inputs[rows - span :], BOTH, 1)
+        here = ()
+
     tail_ids = from_behind(utterance[rows - span :], BOTH, 1)
     samples = (
         inputs,
@@ -660,27 +674,26 @@
         skip_grad,
     )
     if split:
-        p, hid, flags, edge, w, o, bias_out, keep, send = gates_layer(split, tile, 2, *samples, (sums, *parts))
-        got = add_cores(keep, swap(send, 0, 1), edge)
-        edge = got[4]
+        p, hid, flags, edge, w, o, bias_out, keep, send = gates_layer(split, tile, 2, *samples, (*parts, *here))
+        got = add_cores(keep, swap(send, 0, 1))
         part = [got[0]] + [swap(got[n], n, 0) for n in (1, 2, 3)]
-        after = (got[1],)
+        after = (got[4],)
     else:
-        p, hid, flags, edge, grad, grad_out = gates_layer(split, tile, 2, *samples, (w, o))
+        p, hid, flags, edge, grad, grad_out, sums = gates_layer(split, tile, 2, *samples, (w, o))
         after = ()
 
     returned = from_behind(edge, BOTH, -1)
-    input_grad, rest = input_layer(tile, res_grad, p, flags, w, after)
+    input_grad, rest, token = input_layer(tile, res_grad, p, flags, w, after)
     if split:
-        got = add_hop(part, (rest,))
+        got = add_hop(part, (token,))
         part = [got[0]] + [swap(got[n], 0, 2 * n) for n in (1, 2, 3)]
-        after = (got[1],)
-    residual_out, skip_out, input_grad = mixed_layer(
+        after = (got[4],)
+    residual_out, skip_out, input_grad, token = mixed_layer(
         tile, inputs, hid, o, bias_out, rest, returned, input_grad, after
     )
 
     if split:
-        total, square = add_last(part, lax.axis_size(BOTH), (skip_out,))
+        total, square = add_last(part, lax.axis_size(BOTH), (token,))
         part = [total] + [swap(total, n, 0) for n in (1, 2, 3)]
         squares = lax.all_to_all(square, BOTH, 0, 0, tiled=True)
         fold = lambda v: v.reshape(2, LANES)

time: 188 us -> 177 us (0.941)
  Pallas kernels: 121 us -> 107 us
  waiting for transfers between devices: 14.1 us -> 23.5 us
  starting transfers between devices: 34.8 us -> 26.8 us
  local copies, waits for them, and re-layouts: 6.42 us -> 8.55 us
    pallas_call x2, Pallas kernels: 10.7 us -> 1.29 us  [the longest x1 0.7 us: add_cores(): pl.pallas_call(cores_body, grid=(4,), in_specs=[spec, spec], out_specs=[p...]
    ppermute x21, waiting for transfers between devices: 14.1 us -> 22.7 us  [swap(): return lax.ppermute(x, BOTH, pairs)]
    ppermute x21, starting transfers between devices: 27.8 us -> 21.9 us  [swap(): return lax.ppermute(x, BOTH, pairs)]
    unnamed x48 -> x54, local copies, waits for them, and re-layouts: 5.71 us -> 8.53 us
    ppermute x3, starting transfers between devices: 7.07 us -> 4.81 us  [from_behind(): return lax.ppermute(x, axis, pairs)]
    pallas_call x1, Pallas kernels: 2.35 us -> 0.2 us  [add_hop(): pl.pallas_call(hop_body, in_specs=[VMEM] * 4 + [ANY] * len(after), out_sp...]
    pallas_call x1, Pallas kernels: 6.55 us -> 4.63 us  [update(): pl.pallas_call(update_body, in_specs=[VMEM] * 17, out_specs=[VMEM] * 13,...]
  transfers between devices with their start and end apart: 24 -> 24, of which waited for: 4 -> 9; matrix products, arithmetic and copies ran while one was open for 0% -> 1% of each run, Pallas kernels for 24% -> 22%
where the time goes in v3:
time: 177 us; the launch traced here: 176 us
  Pallas kernels  107 us (60%)
  starting transfers between devices  26.8 us (15%)
  waiting for transfers between devices  23.5 us (13%)
  blocking collectives  9.09 us (5%)
  local copies, waits for them, and re-layouts  8.55 us (5%)
    pallas_call x1, Pallas kernels, gates_layer(): pl.pallas_call(functools.partial(gates_body, split, subs), grid=(steps,),...  61.2 us
    ppermute x21, waiting for transfers between devices, swap(): return lax.ppermute(x, BOTH, pairs)  22.7 us
    ppermute x21, starting transfers between devices, swap(): return lax.ppermute(x, BOTH, pairs)  21.9 us
    pallas_call x1, Pallas kernels, input_layer(): pl.pallas_call(input_body, grid=(steps,), in_specs=[by_row(512), by_row(1...  20.8 us
    pallas_call x1, Pallas kernels, mixed_layer(): pl.pallas_call(mixed_body, grid=(total // rows,), in_specs=[by_row, by_ro...  14.2 us
    all_to_all x1, blocking collectives, local(): squares = lax.all_to_all(square, BOTH, 0, 0, tiled=True)  9.09 us
    unnamed x54, local copies, waits for them, and re-layouts  8.53 us
    ppermute x3, starting transfers between devices, from_behind(): return lax.ppermute(x, axis, pairs)  4.81 us
  transfers between devices with their start and end apart: 24, of which 9 were waited for; matrix products, arithmetic and copies ran while one was open for 1% of the time, Pallas kernels for 22%

profile of v3, /device:TPU:0, one launch (start us, length us, event | category | flops | bytes accessed | tf_op | source)
XLA Modules:
  0.0 176.1 jit_solution(3059553317448945502)
XLA Ops:
  0.7 2.6 %pack_weights.1 = (bf16[4,416,128]{2,1,0:T(8,128)(2,1)}, bf16[416,128]{1,0:T(8,128)(2,1)}) custom-call(f32[64,2,1024]{2,1,0:T(2,128)} %refs_7_.1, f32[80,128]{1,0:T(8,128)} %refs_10_.1, f32[2,128]{1,0:T(2,128)} %bitcast.17, f32[64,1024]{1,0:T(8,128)} %refs_13_.1), custom_call_target="tpu_custom_call" | custom-call | tf_op jit(solution)/shard_map/pack_weights/pallas_call | solution.py:111
  3.3 3.0 %collective-permute-start = (bf16[416,128]{1,0:T(8,128)(2,1)}, bf16[416,128]{1,0:T(8,128)(2,1)S(1)}, u32[]{:S(2)}, u32[]{:S(2)}) collective-permute-start(bf16[416,128]{1,0:T(8,128)(2,1)} %get-tuple-element.59), channel_id=1, source_target_pairs={{0,2},{1,3},{2,0},{3,1},{4,6},{5,7},{6,4},{7,5},{8,10},{9,11},{10,... | collective-permute-start | bytes 319496 | tf_op jit(solution)/shard_map/ppermute | solution.py:48
  6.3 2.5 %collective-permute-start.5 = (bf16[416,128]{1,0:T(8,128)(2,1)}, bf16[416,128]{1,0:T(8,128)(2,1)S(1)}, u32[]{:S(2)}, u32[]{:S(2)}) collective-permute-start(bf16[416,128]{1,0:T(8,128)(2,1)} %get-tuple-element.59), channel_id=1, source_target_pairs={{0,6},{1,7},{2,4},{3,5},{4,2},{5,3},{6,0},{7,1},{8,14},{9,15},{10,... | collective-permute-start | bytes 319496 | tf_op jit(solution)/shard_map/ppermute | solution.py:48
  8.9 0.6 collective-permute-done._
  9.5 0.6 copy-done.24
  10.1 1.9 %last_rows.1 = bf16[512,512]{1,0:T(8,128)(2,1)} custom-call(bf16[6144,512]{1,0:T(8,128)(2,1)} %x.5, bf16[416,128]{1,0:T(8,128)(2,1)} %copy-done.24), custom_call_target="tpu_custom_call" | custom-call | tf_op jit(solution)/shard_map/last_rows/pallas_call | solution.py:130
  12.0 2.1 %collective-permute-start.1 = (bf16[512,512]{1,0:T(8,128)(2,1)}, bf16[512,512]{1,0:T(8,128)(2,1)}, u32[]{:S(2)}, u32[]{:S(2)}) collective-permute-start(bf16[512,512]{1,0:T(8,128)(2,1)} %last_rows.1), channel_id=1, source_target_pairs={{0,1},{1,2},{2,3},{3,4},{4,5},{5,6},{6,7},{7,8},{8,9},{9,10},{10,1... | collective-permute-start | bytes 1572872 | tf_op jit(solution)/shard_map/ppermute | solution.py:38
  14.1 0.9 constant_dynamic-update-slice_fusion.2
  15.0 3.7 %collective-permute-done.4 = bf16[416,128]{1,0:T(8,128)(2,1)S(1)} collective-permute-done((bf16[416,128]{1,0:T(8,128)(2,1)}, bf16[416,128]{1,0:T(8,128)(2,1)S(1)}, u32[]{:S(2)}, u32[]{:S(2)}) %collective-permute-start.4) | collective-permute-done | bytes 106528 | tf_op jit(solution)/shard_map/ppermute | solution.py:48
  18.7 2.5 %collective-permute-start.9 = (bf16[1248,128]{1,0:T(8,128)(2,1)S(1)}, bf16[1248,128]{1,0:T(8,128)(2,1)S(1)}, u32[]{:S(2)}, u32[]{:S(2)}) collective-permute-start(bf16[1248,128]{1,0:T(8,128)(2,1)S(1)} %constant_dynamic-update-slice_fusion.refs_2_), channel_id=1, source_target_pairs={{0,24},{1,25},{2,26},{3,27},{4,28},{5,29},{6,30},{7,31},{8,16},{9,... | collective-permute-start | bytes 958472 | tf_op jit(solution)/shard_map/ppermute | solution.py:48
  21.2 0.5 collective-permute-start.8
  21.7 0.5 collective-permute-start.7
  22.3 1.3 collective-permute-start.2
  23.6 0.8 collective-permute-done.2
  24.4 0.6 copy-done.19
  24.9 0.5 collective-permute-start.3
  25.5 6.1 %collective-permute-done.9.refs_6_ = bf16[1248,128]{1,0:T(8,128)(2,1)S(1)} collective-permute-done((bf16[1248,128]{1,0:T(8,128)(2,1)S(1)}, bf16[1248,128]{1,0:T(8,128)(2,1)S(1)}, u32[]{:S(2)}, u32[]{:S(2)}) %collective-permute-start.9) | collective-permute-done | bytes 319520 | tf_op jit(solution)/shard_map/ppermute | solution.py:48
  31.6 7.6 %collective-permute-done.8.refs_5_ = bf16[1248,128]{1,0:T(8,128)(2,1)S(1)} collective-permute-done((bf16[1248,128]{1,0:T(8,128)(2,1)S(1)}, bf16[1248,128]{1,0:T(8,128)(2,1)S(1)}, u32[]{:S(2)}, u32[]{:S(2)}) %collective-permute-start.8) | collective-permute-done | bytes 319520 | tf_op jit(solution)/shard_map/ppermute | solution.py:48
  39.2 1.1 collective-permute-done.7.refs_4_
  40.4 0.5 collective-permute-start.10
  40.9 0.6 arrived_by.1.refs_10_
  41.5 0.9 collective-permute-done.11.refs_8_
  42.4 0.4 collective-permute-done.10.refs_7_
  42.8 0.7 copy-done.16
  43.5 0.7 copy-done.20
  44.2 0.7 copy-done.23
  44.9 61.2 %gates_layer.1 = (bf16[6144,1024]{1,0:T(8,128)(2,1)}, bf16[6144,512]{1,0:T(8,128)(2,1)}, bf16[16,6144]{1,0:T(8,128)(2,1)S(1)}, bf16[512,512]{1,0:T(8,128)(2,1)},...) custom-call(bf16[6144,512]{1,0:T(8,128)(2,1)} %x.5, ...), custom_call_target="tpu_custom_call" | custom-call | flops 43486543872 | bytes 49152000 | tf_op jit(solution)/shard_map/gates_layer/pallas_call | solution.py:420
  106.3 1.5 collective-permute-start.14
  107.8 2.2 %collective-permute-done.13.got = bf16[4,4,416,128]{3,2,1,0:T(8,128)(2,1)S(1)} collective-permute-done((bf16[4,4,416,128]{3,2,1,0:T(8,128)(2,1)}, bf16[4,4,416,128]{3,2,1,0:T(8,128)(2,1)S(1)}, u32[]{:S(2)}, u32[]{:S(2)}) %collective-permute-start.13) | collective-permute-done | bytes 1703968 | tf_op jit(solution)/shard_map/ppermute | solution.py:48
  110.0 1.5 copy-done.1
  111.5 0.7 add_cores.1
  112.2 0.6 copy-done.18
  112.8 0.5 collective-permute-start.15
  113.3 1.5 collective-permute-start.16
  114.8 1.4 collective-permute-start.17
  116.3 20.8 %input_layer.1 = (bf16[6144,512]{1,0:T(8,128)(2,1)}, f32[512,512]{1,0:T(8,128)}, f32[8,128]{1,0:T(8,128)}) custom-call(bf16[6144,512]{1,0:T(8,128)(2,1)} %res.3, bf16[6144,1024]{1,0:T(8,128)(2,1)} %get-tuple-element.64.p, bf16[16,6144]{1,0:T(8,128)(2,1)} %copy-done.22, bf16[1152,1024]{1,0:T(8,128)(2,1)} %get-tuple-element.66.w, f32[8,128]{1,0:T(8,128)} %copy-done.18), custom_call_target="tpu_custom_call" | custom-call | flops 12884901888 | bytes 25165824 | tf_op jit(solution)/shard_map/input_layer/pallas_call | solution.py:489
  137.1 0.7 copy-done.11
  138.0 0.5 collective-permute-start.18
  138.5 1.1 collective-permute-start.19
  139.6 2.8 %collective-permute-start.20 = (bf16[416,128]{1,0:T(8,128)(2,1)S(1)}, bf16[416,128]{1,0:T(8,128)(2,1)S(1)}, u32[]{:S(2)}, u32[]{:S(2)}) collective-permute-start(bf16[416,128]{1,0:T(8,128)(2,1)S(1)} %get-tuple-element.85), channel_id=1, source_target_pairs={{0,6},{1,7},{2,4},{3,5},{4,2},{5,3},{6,0},{7,1},{8,14},{9,15},{10,... | collective-permute-start | bytes 319496 | tf_op jit(solution)/shard_map/ppermute | solution.py:48
  142.4 0.8 copy-done.25
  143.3 14.2 %mixed_layer.1 = (bf16[6144,512]{1,0:T(8,128)(2,1)}, bf16[6144,512]{1,0:T(8,128)(2,1)}, bf16[6144,512]{1,0:T(8,128)(2,1)}, f32[8,128]{1,0:T(8,128)}) custom-call(bf16[6144,512]{1,0:T(8,128)(2,1)} %x.5, bf16[6144,512]{1,0:T(8,128)(2,1)} %get-tuple-element.61.hid, bf16[512,1024]{1,0:T(8,128)(2,1)} %get-tuple-element.62.o, ...), custom_call_target="tpu_custom_call", output_to_operand_aliasing={{2}: (6, {})} | custom-call | flops 6442450944 | bytes 25165824 | tf_op jit(solution)/shard_map/mixed_layer/pallas_call | solution.py:450
  157.6 0.7 copy-done.10
  158.5 1.6 collective-permute-start.23
  160.1 0.5 collective-permute-start.22
  160.6 1.5 collective-permute-start.21
  162.1 9.1 %all_to_all.11 = f32[32,1,128]{2,1,0:T(1,128)S(1)} all-to-all(f32[32,1,128]{2,1,0:T(1,128)S(1)} %bitcast.16), channel_id=1, replica_groups=mesh['rep'=4,'seq'=8] {'rep','seq'}, dimensions={0} | all-to-all | bytes 32768 | tf_op jit(solution)/shard_map/all_to_all | solution.py:698
  171.3 4.6 %update.1 = (f32[1,128]{1,0:T(1,128)}, f32[64,2,1024]{2,1,0:T(2,128)}, f32[64,2,1024]{2,1,0:T(2,128)}, f32[64,2,1024]{2,1,0:T(2,128)}, f32[80,128]{1,0:T(8,128)}...) custom-call(f32[32,128]{1,0:T(8,128)S(1)} %bitcast.15, ...), custom_call_target="tpu_custom_call" | custom-call | tf_op jit(solution)/shard_map/update/pallas_call | solution.py:617
  (67 shorter events, 1.0 us)
Async XLA Ops:
  0.6 21.6 %copy-start.15 = (s32[6144]{0:T(1024)S(1)}, s32[6144]{0:T(1024)}, u32[]{:S(2)}) copy-start(s32[6144]{0:T(1024)} %param.20) | copy-start | bytes 73732
  3.3 6.2 %collective-permute-start = (bf16[416,128]{1,0:T(8,128)(2,1)}, bf16[416,128]{1,0:T(8,128)(2,1)S(1)}, u32[]{:S(2)}, u32[]{:S(2)}) collective-permute-start(bf16[416,128]{1,0:T(8,128)(2,1)} %get-tuple-element.59), channel_id=1, source_target_pairs={{0,2},{1,3},{2,0},{3,1},{4,6},{5,7},{6,4},{7,5},{8,10},{9,11},{10,... | collective-permute-start | bytes 319496 | tf_op jit(solution)/shard_map/ppermute | solution.py:48
  6.3 12.4 %collective-permute-start.5 = (bf16[416,128]{1,0:T(8,128)(2,1)}, bf16[416,128]{1,0:T(8,128)(2,1)S(1)}, u32[]{:S(2)}, u32[]{:S(2)}) collective-permute-start(bf16[416,128]{1,0:T(8,128)(2,1)} %get-tuple-element.59), channel_id=1, source_target_pairs={{0,6},{1,7},{2,4},{3,5},{4,2},{5,3},{6,0},{7,1},{8,14},{9,15},{10,... | collective-permute-start | bytes 319496 | tf_op jit(solution)/shard_map/ppermute | solution.py:48
  8.8 9.9 %collective-permute-start.4 = (bf16[416,128]{1,0:T(8,128)(2,1)}, bf16[416,128]{1,0:T(8,128)(2,1)S(1)}, u32[]{:S(2)}, u32[]{:S(2)}) collective-permute-start(bf16[416,128]{1,0:T(8,128)(2,1)} %get-tuple-element.59), channel_id=1, source_target_pairs={{0,4},{1,5},{2,6},{3,7},{4,0},{5,1},{6,2},{7,3},{8,12},{9,13},{10,... | collective-permute-start | bytes 319496 | tf_op jit(solution)/shard_map/ppermute | solution.py:48
  9.5 0.6 copy-start.24
  12.0 28.4 %collective-permute-start.1 = (bf16[512,512]{1,0:T(8,128)(2,1)}, bf16[512,512]{1,0:T(8,128)(2,1)}, u32[]{:S(2)}, u32[]{:S(2)}) collective-permute-start(bf16[512,512]{1,0:T(8,128)(2,1)} %last_rows.1), channel_id=1, source_target_pairs={{0,1},{1,2},{2,3},{3,4},{4,5},{5,6},{6,7},{7,8},{8,9},{9,10},{10,1... | collective-permute-start | bytes 1572872 | tf_op jit(solution)/shard_map/ppermute | solution.py:38
  18.7 12.9 %collective-permute-start.9 = (bf16[1248,128]{1,0:T(8,128)(2,1)S(1)}, bf16[1248,128]{1,0:T(8,128)(2,1)S(1)}, u32[]{:S(2)}, u32[]{:S(2)}) collective-permute-start(bf16[1248,128]{1,0:T(8,128)(2,1)S(1)} %constant_dynamic-update-slice_fusion.refs_2_), channel_id=1, source_target_pairs={{0,24},{1,25},{2,26},{3,27},{4,28},{5,29},{6,30},{7,31},{8,16},{9,... | collective-permute-start | bytes 958472 | tf_op jit(solution)/shard_map/ppermute | solution.py:48
  21.2 18.0 %collective-permute-start.8 = (bf16[1248,128]{1,0:T(8,128)(2,1)S(1)}, bf16[1248,128]{1,0:T(8,128)(2,1)S(1)}, u32[]{:S(2)}, u32[]{:S(2)}) collective-permute-start(bf16[1248,128]{1,0:T(8,128)(2,1)S(1)} %constant_dynamic-update-slice_fusion.refs_2_), channel_id=1, source_target_pairs={{0,16},{1,17},{2,18},{3,19},{4,20},{5,21},{6,22},{7,23},{8,24},{9,... | collective-permute-start | bytes 958472 | tf_op jit(solution)/shard_map/ppermute | solution.py:48
  21.7 18.6 %collective-permute-start.7 = (bf16[1248,128]{1,0:T(8,128)(2,1)S(1)}, bf16[1248,128]{1,0:T(8,128)(2,1)}, u32[]{:S(2)}, u32[]{:S(2)}) collective-permute-start(bf16[1248,128]{1,0:T(8,128)(2,1)S(1)} %constant_dynamic-update-slice_fusion.refs_2_), channel_id=1, source_target_pairs={{0,8},{1,9},{2,10},{3,11},{4,12},{5,13},{6,14},{7,15},{8,0},{9,1},... | collective-permute-start | bytes 958472 | tf_op jit(solution)/shard_map/ppermute | solution.py:48
  22.3 2.1 %collective-permute-start.2 = (s32[512]{0:T(512)S(1)}, s32[512]{0:T(512)S(1)}, u32[]{:S(2)}, u32[]{:S(2)}) collective-permute-start(s32[512]{0:T(512)S(1)} %slice.6), channel_id=1, source_target_pairs={{0,1},{1,2},{2,3},{3,4},{4,5},{5,6},{6,7},{7,8},{8,9},{9,10},{10,1... | collective-permute-start | bytes 6152 | tf_op jit(solution)/shard_map/ppermute | solution.py:38
  24.9 16.5 %collective-permute-start.3 = (bf16[4,416,128]{2,1,0:T(8,128)(2,1)}, bf16[4,416,128]{2,1,0:T(8,128)(2,1)}, u32[]{:S(2)}, u32[]{:S(2)}) collective-permute-start(bf16[4,416,128]{2,1,0:T(8,128)(2,1)} %get-tuple-element.60.refs_0_), channel_id=1, source_target_pairs={{0,1},{1,0},{2,3},{3,2},{4,5},{5,4},{6,7},{7,6},{8,9},{9,8},{10,11... | collective-permute-start | bytes 1277960 | tf_op jit(solution)/shard_map/ppermute | solution.py:48
  31.6 9.9 %collective-permute-start.6 = (bf16[1248,128]{1,0:T(8,128)(2,1)S(1)}, bf16[1248,128]{1,0:T(8,128)(2,1)}, u32[]{:S(2)}, u32[]{:S(2)}) collective-permute-start(bf16[1248,128]{1,0:T(8,128)(2,1)S(1)} %constant_dynamic-update-slice_fusion.refs_2_), channel_id=1, source_target_pairs={{0,1},{1,0},{2,3},{3,2},{4,5},{5,4},{6,7},{7,6},{8,9},{9,8},{10,11... | collective-permute-start | bytes 958472 | tf_op jit(solution)/shard_map/ppermute | solution.py:48
  39.2 2.3 %collective-permute-start.12 = (bf16[1248,128]{1,0:T(8,128)(2,1)S(1)}, bf16[1248,128]{1,0:T(8,128)(2,1)}, u32[]{:S(2)}, u32[]{:S(2)}) collective-permute-start(bf16[1248,128]{1,0:T(8,128)(2,1)S(1)} %collective-permute-done.9.refs_6_), channel_id=1, source_target_pairs={{0,1},{1,0},{2,3},{3,2},{4,5},{5,4},{6,7},{7,6},{8,9},{9,8},{10,11... | collective-permute-start | bytes 958472 | tf_op jit(solution)/shard_map/ppermute | solution.py:48
  40.4 2.0 %collective-permute-start.11 = (bf16[1248,128]{1,0:T(8,128)(2,1)S(1)}, bf16[1248,128]{1,0:T(8,128)(2,1)}, u32[]{:S(2)}, u32[]{:S(2)}) collective-permute-start(bf16[1248,128]{1,0:T(8,128)(2,1)S(1)} %collective-permute-done.8.refs_5_), channel_id=1, source_target_pairs={{0,1},{1,0},{2,3},{3,2},{4,5},{5,4},{6,7},{7,6},{8,9},{9,8},{10,11... | collective-permute-start | bytes 958472 | tf_op jit(solution)/shard_map/ppermute | solution.py:48
  40.4 2.4 %collective-permute-start.10 = (bf16[1248,128]{1,0:T(8,128)(2,1)}, bf16[1248,128]{1,0:T(8,128)(2,1)}, u32[]{:S(2)}, u32[]{:S(2)}) collective-permute-start(bf16[1248,128]{1,0:T(8,128)(2,1)} %collective-permute-done.7.refs_4_), channel_id=1, source_target_pairs={{0,1},{1,0},{2,3},{3,2},{4,5},{5,4},{6,7},{7,6},{8,9},{9,8},{10,11... | collective-permute-start | bytes 958472 | tf_op jit(solution)/shard_map/ppermute | solution.py:48
  42.8 0.7 copy-start.16
  43.5 0.7 copy-start.20
  44.2 0.7 copy-start.23
  106.1 10.1 %copy-start.21 = (f32[8,1024]{1,0:T(8,128)}, f32[8,1024]{1,0:T(8,128)S(1)}, u32[]{:S(2)}) copy-start(f32[8,1024]{1,0:T(8,128)S(1)} %get-tuple-element.63.bias) | copy-start | bytes 98308
  106.1 10.1 %copy-start.22 = (bf16[16,6144]{1,0:T(8,128)(2,1)}, bf16[16,6144]{1,0:T(8,128)(2,1)S(1)}, u32[]{:S(2)}) copy-start(bf16[16,6144]{1,0:T(8,128)(2,1)S(1)} %get-tuple-element.65.flags) | copy-start | bytes 589828
  106.1 3.9 %collective-permute-start.13 = (bf16[4,4,416,128]{3,2,1,0:T(8,128)(2,1)}, bf16[4,4,416,128]{3,2,1,0:T(8,128)(2,1)S(1)}, u32[]{:S(2)}, u32[]{:S(2)}) collective-permute-start(bf16[4,4,416,128]{3,2,1,0:T(8,128)(2,1)} %get-tuple-element.68), channel_id=1, source_target_pairs={{0,1},{1,0},{2,3},{3,2},{4,5},{5,4},{6,7},{7,6},{8,9},{9,8},{10,11... | collective-permute-start | bytes 5111816 | tf_op jit(solution)/shard_map/ppermute | solution.py:48
  106.3 36.1 %collective-permute-start.14 = (bf16[512,512]{1,0:T(8,128)(2,1)}, bf16[512,512]{1,0:T(8,128)(2,1)S(1)}, u32[]{:S(2)}, u32[]{:S(2)}) collective-permute-start(bf16[512,512]{1,0:T(8,128)(2,1)} %get-tuple-element.71), channel_id=1, source_target_pairs={{1,0},{2,1},{3,2},{4,3},{5,4},{6,5},{7,6},{8,7},{9,8},{10,9},{11,1... | collective-permute-start | bytes 1572872 | tf_op jit(solution)/shard_map/ppermute | solution.py:38
  110.0 1.5 copy-start.1
  112.8 24.3 %collective-permute-start.15 = (bf16[4,416,128]{2,1,0:T(8,128)(2,1)S(1)}, bf16[4,416,128]{2,1,0:T(8,128)(2,1)S(1)}, u32[]{:S(2)}, u32[]{:S(2)}) collective-permute-start(bf16[4,416,128]{2,1,0:T(8,128)(2,1)S(1)} %get-tuple-element.74), channel_id=1, source_target_pairs={{0,8},{1,9},{2,10},{3,11},{4,12},{5,13},{6,14},{7,15},{8,0},{9,1},... | collective-permute-start | bytes 1277960 | tf_op jit(solution)/shard_map/ppermute | solution.py:48
  113.3 23.7 %collective-permute-start.16 = (bf16[4,416,128]{2,1,0:T(8,128)(2,1)S(1)}, bf16[4,416,128]{2,1,0:T(8,128)(2,1)S(1)}, u32[]{:S(2)}, u32[]{:S(2)}) collective-permute-start(bf16[4,416,128]{2,1,0:T(8,128)(2,1)S(1)} %get-tuple-element.75), channel_id=1, source_target_pairs={{0,16},{1,17},{2,18},{3,19},{4,20},{5,21},{6,22},{7,23},{8,24},{9,... | collective-permute-start | bytes 1277960 | tf_op jit(solution)/shard_map/ppermute | solution.py:48
  114.8 22.2 %collective-permute-start.17 = (bf16[4,416,128]{2,1,0:T(8,128)(2,1)S(1)}, bf16[4,416,128]{2,1,0:T(8,128)(2,1)S(1)}, u32[]{:S(2)}, u32[]{:S(2)}) collective-permute-start(bf16[4,416,128]{2,1,0:T(8,128)(2,1)S(1)} %get-tuple-element.76), channel_id=1, source_target_pairs={{0,24},{1,25},{2,26},{3,27},{4,28},{5,29},{6,30},{7,31},{8,16},{9,... | collective-permute-start | bytes 1277960 | tf_op jit(solution)/shard_map/ppermute | solution.py:48
  137.1 0.7 copy-start.11
  138.0 4.5 %copy-start.17 = (f32[8,128]{1,0:T(8,128)}, f32[8,128]{1,0:T(8,128)S(1)}, u32[]{:S(2)}) copy-start(f32[8,128]{1,0:T(8,128)S(1)} %get-tuple-element.78.refs_1_) | copy-start | bytes 12292
  138.0 19.6 %collective-permute-start.18 = (bf16[416,128]{1,0:T(8,128)(2,1)S(1)}, bf16[416,128]{1,0:T(8,128)(2,1)S(1)}, u32[]{:S(2)}, u32[]{:S(2)}) collective-permute-start(bf16[416,128]{1,0:T(8,128)(2,1)S(1)} %get-tuple-element.83), channel_id=1, source_target_pairs={{0,2},{1,3},{2,0},{3,1},{4,6},{5,7},{6,4},{7,5},{8,10},{9,11},{10,... | collective-permute-start | bytes 319496 | tf_op jit(solution)/shard_map/ppermute | solution.py:48
  138.5 19.1 %collective-permute-start.19 = (bf16[416,128]{1,0:T(8,128)(2,1)S(1)}, bf16[416,128]{1,0:T(8,128)(2,1)S(1)}, u32[]{:S(2)}, u32[]{:S(2)}) collective-permute-start(bf16[416,128]{1,0:T(8,128)(2,1)S(1)} %get-tuple-element.84), channel_id=1, source_target_pairs={{0,4},{1,5},{2,6},{3,7},{4,0},{5,1},{6,2},{7,3},{8,12},{9,13},{10,... | collective-permute-start | bytes 319496 | tf_op jit(solution)/shard_map/ppermute | solution.py:48
  139.6 18.0 %collective-permute-start.20 = (bf16[416,128]{1,0:T(8,128)(2,1)S(1)}, bf16[416,128]{1,0:T(8,128)(2,1)S(1)}, u32[]{:S(2)}, u32[]{:S(2)}) collective-permute-start(bf16[416,128]{1,0:T(8,128)(2,1)S(1)} %get-tuple-element.85), channel_id=1, source_target_pairs={{0,6},{1,7},{2,4},{3,5},{4,2},{5,3},{6,0},{7,1},{8,14},{9,15},{10,... | collective-permute-start | bytes 319496 | tf_op jit(solution)/shard_map/ppermute | solution.py:48
  142.4 0.8 copy-start.25
  143.2 28.0 %copy-start = (f32[64,2,1024]{2,1,0:T(2,128)S(1)}, f32[64,2,1024]{2,1,0:T(2,128)}, u32[]{:S(2)}) copy-start(f32[64,2,1024]{2,1,0:T(2,128)} %refs_7_.1) | copy-start | bytes 1572868
  143.2 28.0 %copy-start.2 = (f32[64,1024]{1,0:T(8,128)S(1)}, f32[64,1024]{1,0:T(8,128)}, u32[]{:S(2)}) copy-start(f32[64,1024]{1,0:T(8,128)} %refs_13_.1) | copy-start | bytes 786436
  143.2 28.0 %copy-start.3 = (f32[64,2,1024]{2,1,0:T(2,128)S(1)}, f32[64,2,1024]{2,1,0:T(2,128)}, u32[]{:S(2)}) copy-start(f32[64,2,1024]{2,1,0:T(2,128)} %refs_5_.1) | copy-start | bytes 1572868
  143.2 28.0 %copy-start.4 = (f32[64,2,1024]{2,1,0:T(2,128)S(1)}, f32[64,2,1024]{2,1,0:T(2,128)}, u32[]{:S(2)}) copy-start(f32[64,2,1024]{2,1,0:T(2,128)} %refs_6_.1) | copy-start | bytes 1572868
  143.2 28.0 %copy-start.5 = (f32[64,1024]{1,0:T(8,128)S(1)}, f32[64,1024]{1,0:T(8,128)}, u32[]{:S(2)}) copy-start(f32[64,1024]{1,0:T(8,128)} %refs_11_.1) | copy-start | bytes 786436
  143.2 28.0 %copy-start.6 = (f32[64,1024]{1,0:T(8,128)S(1)}, f32[64,1024]{1,0:T(8,128)}, u32[]{:S(2)}) copy-start(f32[64,1024]{1,0:T(8,128)} %refs_12_.1) | copy-start | bytes 786436
  143.3 28.0 %copy-start.7 = (f32[80,128]{1,0:T(8,128)S(1)}, f32[80,128]{1,0:T(8,128)}, u32[]{:S(2)}) copy-start(f32[80,128]{1,0:T(8,128)} %refs_10_.1) | copy-start | bytes 122884
  143.3 28.0 %copy-start.8 = (f32[80,128]{1,0:T(8,128)S(1)}, f32[80,128]{1,0:T(8,128)}, u32[]{:S(2)}) copy-start(f32[80,128]{1,0:T(8,128)} %refs_8_.1) | copy-start | bytes 122884
  143.3 28.0 %copy-start.9 = (f32[80,128]{1,0:T(8,128)S(1)}, f32[80,128]{1,0:T(8,128)}, u32[]{:S(2)}) copy-start(f32[80,128]{1,0:T(8,128)} %refs_9_.1) | copy-start | bytes 122884
  143.3 28.0 %copy-start.12 = (f32[256]{0:T(256)S(1)}, f32[256]{0:T(256)}, u32[]{:S(2)}) copy-start(f32[256]{0:T(256)} %param.27) | copy-start | bytes 3076
  143.3 28.0 %copy-start.13 = (f32[256]{0:T(256)S(1)}, f32[256]{0:T(256)}, u32[]{:S(2)}) copy-start(f32[256]{0:T(256)} %param.34) | copy-start | bytes 3076
  143.3 28.0 %copy-start.14 = (f32[256]{0:T(256)S(1)}, f32[256]{0:T(256)}, u32[]{:S(2)}) copy-start(f32[256]{0:T(256)} %param.35) | copy-start | bytes 3076
  157.6 0.7 copy-start.10
  158.5 12.6 %collective-permute-start.23 = (f32[416,128]{1,0:T(8,128)S(1)}, f32[416,128]{1,0:T(8,128)S(1)}, u32[]{:S(2)}, u32[]{:S(2)}) collective-permute-start(f32[416,128]{1,0:T(8,128)S(1)} %get-tuple-element.88.refs_1_), channel_id=1, source_target_pairs={{0,24},{1,25},{2,26},{3,27},{4,28},{5,29},{6,30},{7,31},{8,16},{9,... | collective-permute-start | bytes 638984 | tf_op jit(solution)/shard_map/ppermute | solution.py:48
  160.1 11.1 %collective-permute-start.22 = (f32[416,128]{1,0:T(8,128)S(1)}, f32[416,128]{1,0:T(8,128)S(1)}, u32[]{:S(2)}, u32[]{:S(2)}) collective-permute-start(f32[416,128]{1,0:T(8,128)S(1)} %get-tuple-element.88.refs_1_), channel_id=1, source_target_pairs={{0,16},{1,17},{2,18},{3,19},{4,20},{5,21},{6,22},{7,23},{8,24},{9,... | collective-permute-start | bytes 638984 | tf_op jit(solution)/shard_map/ppermute | solution.py:48
  160.6 10.6 %collective-permute-start.21 = (f32[416,128]{1,0:T(8,128)S(1)}, f32[416,128]{1,0:T(8,128)S(1)}, u32[]{:S(2)}, u32[]{:S(2)}) collective-permute-start(f32[416,128]{1,0:T(8,128)S(1)} %get-tuple-element.88.refs_1_), channel_id=1, source_target_pairs={{0,8},{1,9},{2,10},{3,11},{4,12},{5,13},{6,14},{7,15},{8,0},{9,1},... | collective-permute-start | bytes 638984 | tf_op jit(solution)/shard_map/ppermute | solution.py:48
  (2 other events, 1.2 us)

commit v4 on v3

--- a/solution.py
+++ b/solution.py
@@ -133,25 +133,30 @@
         in_specs=[pl.BlockSpec((ROWS, x.shape[1]), lambda i: (x.shape[0] // ROWS - 1, 0)), ANY],
         out_specs=whole((ROWS, x.shape[1])),
         out_shape=jax.ShapeDtypeStruct((ROWS, x.shape[1]), x.dtype),
-        compiler_params=params(63),
+        compiler_params=params(58),
         name="last_rows",
     )(x, after)
 
 
-def arrive_body(_, token):
-    token[...] = jnp.zeros_like(token)
-
-
-def arrived_by(array):
-    return pl.pallas_call(
-        arrive_body,
-        in_specs=[ANY],
+def flags_body(keep, ids, tail_ids, _, flags):
+    first = jnp.where(lax.axis_index(BOTH) > 0, tail_ids[...], -1)
+    past = jnp.concatenate([first, ids[:, 0 : ids.shape[1] - ROWS]], 1)
+    place = lax.broadcasted_iota(jnp.int32, flags.shape, 0)
+    link = jnp.where(place == LINK - ONES, (ids[...] == past).astype(F32), 0.0)
+    kept = jnp.where(place == KEEP - ONES, keep[...].astype(F32), link)
+    flags[...] = jnp.where(place == 0, 1.0, kept).astype(BF)
+
+
+def flag_rows(keep, ids, tail_ids, after):
+    return pl.pallas_call(
+        flags_body,
+        in_specs=[VMEM] * 3 + [ANY],
         out_specs=VMEM,
-        out_shape=TOKEN,
-        compiler_params=params(63),
+        out_shape=jax.ShapeDtypeStruct((TILE, keep.shape[1]), BF),
+        compiler_params=params(),
         cost_estimate=cost(ARRIVE, 4096),
-        name="arrived_by",
-    )(array)
+        name="flag_rows",
+    )(keep, ids, tail_ids, after)
 
 
 def mixed_block(block):
@@ -251,20 +256,19 @@
         dest[base + b * TILE : base + (b + 1) * TILE, :] = value[:, lane : lane + LANES]
 
 
-def gates_body(split, subs, x, tail, mel, keep, ids, tail_ids, res, skp, *refs):
+def gates_body(split, subs, x, tail, mel, flags, res, skp, *refs):
     if split:
-        parts, refs = refs[0:10], refs[11:]
-        p, hid, flags, edge, w, o, bias_out, keep_out, send_out = refs[:9]
-        xe, carry, carry_ids, acc, acc_out, sums, small, small_low, arrived, *held = refs[9:]
+        parts, refs = refs[0:10], refs[10:]
+        p, hid, edge, w, o, bias_out, keep_out, send_out = refs[:8]
+        xe, carry, acc, acc_out, sums, small, small_low, arrived, *held = refs[8:]
     else:
-        w, o, p, hid, flags, edge, grad, grad_out, sums, xe, carry, carry_ids, acc, acc_out = refs
+        w, o, p, hid, edge, grad, grad_out, sums, xe, carry, acc, acc_out = refs
     step, last = pl.program_id(0), pl.num_programs(0) - 1
     rows, half = x.shape[0], p.shape[1] // 4
 
     @pl.when(step == 0)
     def _():
         carry[...] = tail[...]
-        carry_ids[...] = jnp.where(lax.axis_index(BOTH) > 0, tail_ids[...], -1)
         acc[...] = jnp.zeros_like(acc)
         acc_out[...] = jnp.zeros_like(acc_out)
         sums[...] = jnp.zeros_like(sums)
@@ -279,22 +283,7 @@
                 copy.wait()
             unpack(held, w, o, bias_out, small_low)
 
-    ids_now = ids[...]
-    ids_past = carry_ids[...]
-    if rows > ROWS:
-        ids_past = jnp.concatenate([ids_past, ids_now[:, 0 : rows - ROWS]], 1)
-    place = lax.broadcasted_iota(jnp.int32, (TILE, rows), 0)
-    mark = jnp.where(
-        place == 0,
-        1.0,
-        jnp.where(
-            place == KEEP - ONES,
-            keep[...].astype(F32),
-            jnp.where(place == LINK - ONES, (ids_now == ids_past).astype(F32), 0.0),
-        ),
-    ).astype(BF)
-    flags[...] = mark
-    side = jnp.concatenate([mel[...], mark, jnp.zeros((32, rows), BF)], 0).T
+    side = jnp.concatenate([mel[...], flags[...], jnp.zeros((32, rows), BF)], 0).T
     link = side[:, LINK : LINK + 1]
     kept_rows = side[:, KEEP : KEEP + 1].astype(F32)
     xe[:, 0:512] = x[...]
@@ -303,7 +292,6 @@
         xe[ROWS:, 512:1024] = x[0 : rows - ROWS, :] * link[ROWS:]
     xe[:, 1024:1152] = side
     carry[...] = x[rows - ROWS :, :]
-    carry_ids[...] = ids_now[:, rows - ROWS :]
 
     size = rows // subs
     for s in range(subs):
@@ -321,11 +309,10 @@
             p[at, base : base + half] = (up * kept * (1.0 - filt * filt)).astype(BF)
             p[at, base + half : base + 2 * half] = (up * hidden * (1.0 - gate)).astype(BF)
     acc[...] += tn_dot(xe[...], p[...])
-    acc_out[:, 0:512] += tn_dot(hid[...], res[...])
-    acc_out[:, 512:1024] += tn_dot(hid[...], skp[...])
-    for n, part in enumerate((res, skp)):
-        total = jnp.sum(part[...].astype(F32), 0, keepdims=True)
-        sums[:, n * 512 : (n + 1) * 512] += jnp.broadcast_to(total, (8, 512))
+    left = jnp.concatenate([hid[...], side[:, MEL : MEL + TILE]], 1)
+    got = tn_dot(left, jnp.concatenate([res[...], skp[...]], 1))
+    acc_out[...] += got[0:512]
+    sums[...] += got[512:520]
 
     @pl.when(step == 0)
     def _():
@@ -362,7 +349,7 @@
         emit_pieces((keep_out, send_out), write)
 
 
-def gates_layer(split, rows, subs, x, tail, mel, keep, ids, tail_ids, res, skp, extra):
+def gates_layer(split, rows, subs, x, tail, mel, flags, res, skp, extra):
     total = x.shape[0]
     steps = total // rows
     by_row = lambda columns: pl.BlockSpec((rows, columns), lambda i: (i, 0))
@@ -371,22 +358,18 @@
         by_row(512),
         whole((ROWS, 512)),
         by_lane(MEL),
-        by_lane(1),
-        by_lane(1),
-        whole((1, ROWS)),
+        by_lane(TILE),
         by_row(512),
         by_row(512),
     ] + [ANY if split else whole(e.shape) for e in extra]
     out_specs = [
         by_row(1024),
         by_row(512),
-        by_lane(TILE),
         whole((ROWS, 512)),
     ]
     out_shape = [
         jax.ShapeDtypeStruct((total, 1024), BF),
         jax.ShapeDtypeStruct((total, 512), BF),
-        jax.ShapeDtypeStruct((TILE, total), BF),
         jax.ShapeDtypeStruct((ROWS, 512), BF),
     ]
     if split:
@@ -405,7 +388,6 @@
     scratch = [
         pltpu.VMEM((rows, 1024 + AUX), BF),
         pltpu.VMEM((ROWS, 512), BF),
-        pltpu.VMEM((1, ROWS), jnp.int32),
         pltpu.VMEM((1024 + AUX, 1024), F32),
         pltpu.VMEM((512, 1024), F32),
     ]
@@ -416,7 +398,7 @@
             pltpu.VMEM((8, AUX, LANES), BF),
             pltpu.SemaphoreType.DMA((10,)),
         ]
-        scratch += [pltpu.VMEM(e.shape, e.dtype) for e in extra[:10]]
+        scratch += [pltpu.VMEM(e.shape, e.dtype) for e in extra]
     return pl.pallas_call(
         functools.partial(gates_body, split, subs),
         grid=(steps,),
@@ -427,38 +409,58 @@
         compiler_params=params(GATES_MIB),
         cost_estimate=cost(6.75 * 2 * total * 512 * 1024, total * 8000),
         name="gates_layer",
-    )(x, tail, mel, keep, ids, tail_ids, res, skp, *extra)
-
-
-def mixed_body(x, hid, o, bias, rest, edge, *refs):
-    residual, skip, patch, token = refs[-4:]
+    )(x, tail, mel, flags, res, skp, *extra)
+
+
+def mixed_body(x, hid, o, bias, *refs):
+    residual, skip, token = refs[-3:]
     mixed = dot(hid[...], o[...]) + bias[0:1, :]
     residual[...] = (x[...].astype(F32) + mixed[:, 0:512]).astype(BF)
     skip[...] = mixed[:, 512:1024].astype(BF)
 
     @pl.when(pl.program_id(0) == 0)
     def _():
+        token[...] = jnp.zeros_like(token)
+
+
+def patch_body(x, hid, o, bias, rest, edge, *refs):
+    residual, skip, patch, token = refs[-4:]
+    mixed_body(x, hid, o, bias, residual, skip, token)
+
+    @pl.when(pl.program_id(0) == 0)
+    def _():
         patch[...] = (rest[...] + edge[...].astype(F32)).astype(BF)
-        token[...] = jnp.zeros_like(token)
-
-
-def mixed_layer(rows, x, hid, o, bias, rest, edge, input_grad, after):
+
+
+def mixed_layer(rows, first, steps, x, hid, o, bias, patched, partial, after):
     total = x.shape[0]
-    by_row = pl.BlockSpec((rows, 512), lambda i: (i, 0))
+    by_row = pl.BlockSpec((rows, 512), lambda i: (first + i, 0))
     last = pl.BlockSpec((ROWS, 512), lambda i: (total // ROWS - 1, 0))
-    operands = (x, hid, o, bias, rest, edge, input_grad, *after)
-    return pl.pallas_call(
-        mixed_body,
-        grid=(total // rows,),
-        in_specs=[by_row, by_row, whole((512, 1024)), whole((8, 1024)), whole((ROWS, 512)), whole((ROWS, 512))]
-        + [ANY] * (1 + len(after)),
-        out_specs=[by_row, by_row, last, whole(TOKEN.shape)],
-        out_shape=[jax.ShapeDtypeStruct((total, 512), BF)] * 3 + [TOKEN],
-        input_output_aliases={6: 2},
+    operands = [x, hid, o, bias]
+    in_specs = [by_row, by_row, whole((512, 1024)), whole((8, 1024))]
+    out_specs = [by_row, by_row]
+    aliases = {}
+    if patched:
+        rest, edge, input_grad = patched
+        operands += [rest, edge, input_grad]
+        in_specs += [whole((ROWS, 512)), whole((ROWS, 512)), ANY]
+        out_specs.append(last)
+        aliases[6] = 2
+    for n, array in enumerate(partial):
+        aliases[len(operands)] = n
+        operands.append(array)
+        in_specs.append(ANY)
+    return pl.pallas_call(
+        patch_body if patched else mixed_body,
+        grid=(steps,),
+        in_specs=in_specs + [ANY] * len(after),
+        out_specs=out_specs + [whole(TOKEN.shape)],
+        out_shape=[jax.ShapeDtypeStruct((total, 512), BF)] * len(out_specs) + [TOKEN],
+        input_output_aliases=aliases,
         compiler_params=params(58),
-        cost_estimate=cost(2 * total * 512 * 1024, total * 4096),
-        name="mixed_layer",
-    )(*operands)
+        cost_estimate=cost(2 * rows * steps * 512 * 1024, rows * steps * 4096),
+        name="mixed_layer_%d" % first,
+    )(*operands, *after)
 
 
 def input_body(res, p, flags, w, *refs):
@@ -510,7 +512,6 @@
 
 
 def cores_body(keep, got, *outs):
-    outs[4][...] = jnp.zeros_like(outs[4])
     for n in range(4):
         outs[n][...] = (keep[n].astype(F32) + got[n].astype(F32)).astype(outs[n].dtype)
 
@@ -521,8 +522,8 @@
         cores_body,
         grid=(4,),
         in_specs=[spec, spec],
-        out_specs=[pl.BlockSpec((1, PART, LANES), lambda i: (i, 0, 0))] * 4 + [whole(TOKEN.shape)],
-        out_shape=[jax.ShapeDtypeStruct((4, PART, LANES), BF if n else F32) for n in range(4)] + [TOKEN],
+        out_specs=[pl.BlockSpec((1, PART, LANES), lambda i: (i, 0, 0))] * 4,
+        out_shape=[jax.ShapeDtypeStruct((4, PART, LANES), BF if n else F32) for n in range(4)],
         compiler_params=params(),
         cost_estimate=cost(10**6, 8 * 10**6),
         name="add_cores",
@@ -655,31 +656,23 @@
         along = [swap(first, 0, 2 * j) for j in (1, 2, 3)]
         tail = from_behind(last_rows(inputs, along[0]), BOTH, 1)
         stack = jnp.concatenate(along, 0)
-        here = (arrived_by(tail),)
         parts = across_hops(own, stack)
     else:
         w, o, bias_out = gather_plain(conv_weight, out_weight, cond_weight, biases)
         tail = from_behind(inputs[rows - span :], BOTH, 1)
-        here = ()
 
     tail_ids = from_behind(utterance[rows - span :], BOTH, 1)
-    samples = (
-        inputs,
-        tail,
-        mel_frames,
-        keep_mask.reshape(1, rows),
-        utterance.reshape(1, rows),
-        tail_ids.reshape(1, span),
-        res_grad,
-        skip_grad,
+    flags = flag_rows(
+        keep_mask.reshape(1, rows), utterance.reshape(1, rows), tail_ids.reshape(1, span), tail
     )
+    samples = (inputs, tail, mel_frames, flags, res_grad, skip_grad)
     if split:
-        p, hid, flags, edge, w, o, bias_out, keep, send = gates_layer(split, tile, 2, *samples, (*parts, *here))
+        p, hid, edge, w, o, bias_out, keep, send = gates_layer(split, tile, 2, *samples, parts)
         got = add_cores(keep, swap(send, 0, 1))
         part = [got[0]] + [swap(got[n], n, 0) for n in (1, 2, 3)]
-        after = (got[4],)
+        after = (got[1],)
     else:
-        p, hid, flags, edge, grad, grad_out, sums = gates_layer(split, tile, 2, *samples, (w, o))
+        p, hid, edge, grad, grad_out, sums = gates_layer(split, tile, 2, *samples, (w, o))
         after = ()
 
     returned = from_behind(edge, BOTH, -1)
@@ -688,12 +681,18 @@
         got = add_hop(part, (token,))
         part = [got[0]] + [swap(got[n], 0, 2 * n) for n in (1, 2, 3)]
         after = (got[4],)
-    residual_out, skip_out, input_grad, token = mixed_layer(
-        tile, inputs, hid, o, bias_out, rest, returned, input_grad, after
-    )
-
+    steps = rows // tile
+    cut = steps * 4 // 6
+    mixed = functools.partial(mixed_layer, tile)
+    *sample_outs, token = mixed(0, cut, inputs, hid, o, bias_out, (), (), after)
     if split:
         total, square = add_last(part, lax.axis_size(BOTH), (token,))
+        after = (square,)
+    residual_out, skip_out, input_grad, _ = mixed(
+        cut, steps - cut, inputs, hid, o, bias_out, (rest, returned, input_grad), sample_outs, after
+    )
+
+    if split:
         part = [total] + [swap(total, n, 0) for n in (1, 2, 3)]
         squares = lax.all_to_all(square, BOTH, 0, 0, tiled=True)
         fold = lambda v: v.reshape(2, LANES)

time: 177 us -> 169 us (0.955)
  blocking collectives: 9.09 us -> 0 us
  starting transfers between devices: 26.8 us -> 28.9 us
  local copies, waits for them, and re-layouts: 8.55 us -> 6.53 us
    all_to_all x1 -> x0, blocking collectives: 9.09 us -> none  [local(): squares = lax.all_to_all(square, BOTH, 0, 0, tiled=True)]
    all_to_all x0 -> x1, starting transfers between devices: none -> 2.94 us  [local(): squares = lax.all_to_all(square, BOTH, 0, 0, tiled=True)]
    unnamed x54 -> x60, local copies, waits for them, and re-layouts: 8.53 us -> 6.51 us
    pallas_call x1, Pallas kernels: 61.2 us -> 59.2 us  [gates_layer(): pl.pallas_call(functools.partial(gates_body, split, subs), grid=(steps,),...]
    pallas_call x2 -> x3, Pallas kernels: 14.8 us -> 16.2 us  [the longest x2 16.2 us: mixed_layer(): pl.pallas_call(patch_body if patched else mixed_body, grid=(steps,), in_s...]
  transfers between devices with their start and end apart: 24 -> 25, of which waited for: 9 -> 9; matrix products, arithmetic and copies ran while one was open for 1% -> 1% of each run, Pallas kernels for 22% -> 24%
where the time goes in v4:
time: 169 us; the launch traced here: 168 us
  Pallas kernels  107 us (63%)
  starting transfers between devices  28.9 us (17%)
  waiting for transfers between devices  24.6 us (15%)
  local copies, waits for them, and re-layouts  6.53 us (4%)
    pallas_call x1, Pallas kernels, gates_layer(): pl.pallas_call(functools.partial(gates_body, split, subs), grid=(steps,),...  59.2 us
    ppermute x21, waiting for transfers between devices, swap(): return lax.ppermute(x, BOTH, pairs)  23.8 us
    ppermute x21, starting transfers between devices, swap(): return lax.ppermute(x, BOTH, pairs)  21.9 us
    pallas_call x1, Pallas kernels, input_layer(): pl.pallas_call(input_body, grid=(steps,), in_specs=[by_row(512), by_row(1...  20.8 us
    pallas_call x2, Pallas kernels, mixed_layer(): pl.pallas_call(patch_body if patched else mixed_body, grid=(steps,), in_s...  16.2 us
    unnamed x60, local copies, waits for them, and re-layouts  6.51 us
    pallas_call x1, Pallas kernels, update(): pl.pallas_call(update_body, in_specs=[VMEM] * 17, out_specs=[VMEM] * 13,...  4.63 us
    ppermute x3, starting transfers between devices, from_behind(): return lax.ppermute(x, axis, pairs)  4.05 us
  transfers between devices with their start and end apart: 25, of which 9 were waited for; matrix products, arithmetic and copies ran while one was open for 1% of the time, Pallas kernels for 24%

profile of v4, /device:TPU:0, one launch (start us, length us, event | category | flops | bytes accessed | tf_op | source)
XLA Modules:
  0.0 168.4 jit_solution(1407940524776693217)
XLA Ops:
  0.7 2.6 %pack_weights.1 = (bf16[4,416,128]{2,1,0:T(8,128)(2,1)}, bf16[416,128]{1,0:T(8,128)(2,1)}) custom-call(f32[64,2,1024]{2,1,0:T(2,128)} %refs_7_.1, f32[80,128]{1,0:T(8,128)} %refs_10_.1, f32[2,128]{1,0:T(2,128)} %bitcast.16, f32[64,1024]{1,0:T(8,128)} %refs_13_.1), custom_call_target="tpu_custom_call" | custom-call | tf_op jit(solution)/shard_map/pack_weights/pallas_call | solution.py:111
  3.3 3.0 %collective-permute-start = (bf16[416,128]{1,0:T(8,128)(2,1)}, bf16[416,128]{1,0:T(8,128)(2,1)S(1)}, u32[]{:S(2)}, u32[]{:S(2)}) collective-permute-start(bf16[416,128]{1,0:T(8,128)(2,1)} %get-tuple-element.59), channel_id=1, source_target_pairs={{0,2},{1,3},{2,0},{3,1},{4,6},{5,7},{6,4},{7,5},{8,10},{9,11},{10,... | collective-permute-start | bytes 319496 | tf_op jit(solution)/shard_map/ppermute | solution.py:48
  6.3 2.5 %collective-permute-start.5 = (bf16[416,128]{1,0:T(8,128)(2,1)}, bf16[416,128]{1,0:T(8,128)(2,1)S(1)}, u32[]{:S(2)}, u32[]{:S(2)}) collective-permute-start(bf16[416,128]{1,0:T(8,128)(2,1)} %get-tuple-element.59), channel_id=1, source_target_pairs={{0,6},{1,7},{2,4},{3,5},{4,2},{5,3},{6,0},{7,1},{8,14},{9,15},{10,... | collective-permute-start | bytes 319496 | tf_op jit(solution)/shard_map/ppermute | solution.py:48
  8.9 0.6 collective-permute-done._
  9.5 0.6 copy-done.23
  10.1 1.9 %last_rows.1 = bf16[512,512]{1,0:T(8,128)(2,1)} custom-call(bf16[6144,512]{1,0:T(8,128)(2,1)} %x.7, bf16[416,128]{1,0:T(8,128)(2,1)} %copy-done.23), custom_call_target="tpu_custom_call" | custom-call | tf_op jit(solution)/shard_map/last_rows/pallas_call | solution.py:130
  12.0 1.3 collective-permute-start.1
  13.3 0.9 constant_dynamic-update-slice_fusion.2
  14.2 4.5 %collective-permute-done.4 = bf16[416,128]{1,0:T(8,128)(2,1)S(1)} collective-permute-done((bf16[416,128]{1,0:T(8,128)(2,1)}, bf16[416,128]{1,0:T(8,128)(2,1)S(1)}, u32[]{:S(2)}, u32[]{:S(2)}) %collective-permute-start.4) | collective-permute-done | bytes 106528 | tf_op jit(solution)/shard_map/ppermute | solution.py:48
  18.7 2.5 %collective-permute-start.9 = (bf16[1248,128]{1,0:T(8,128)(2,1)S(1)}, bf16[1248,128]{1,0:T(8,128)(2,1)S(1)}, u32[]{:S(2)}, u32[]{:S(2)}) collective-permute-start(bf16[1248,128]{1,0:T(8,128)(2,1)S(1)} %constant_dynamic-update-slice_fusion.refs_2_), channel_id=1, source_target_pairs={{0,24},{1,25},{2,26},{3,27},{4,28},{5,29},{6,30},{7,31},{8,16},{9,... | collective-permute-start | bytes 958472 | tf_op jit(solution)/shard_map/ppermute | solution.py:48
  21.3 0.5 collective-permute-start.8
  21.8 0.5 collective-permute-start.7
  22.3 1.3 collective-permute-start.2
  23.6 0.8 collective-permute-done.2
  24.4 0.5 collective-permute-start.3
  24.9 6.7 %collective-permute-done.9.refs_6_ = bf16[1248,128]{1,0:T(8,128)(2,1)S(1)} collective-permute-done((bf16[1248,128]{1,0:T(8,128)(2,1)S(1)}, bf16[1248,128]{1,0:T(8,128)(2,1)S(1)}, u32[]{:S(2)}, u32[]{:S(2)}) %collective-permute-start.9) | collective-permute-done | bytes 319520 | tf_op jit(solution)/shard_map/ppermute | solution.py:48
  31.6 7.6 %collective-permute-done.8.refs_5_ = bf16[1248,128]{1,0:T(8,128)(2,1)S(1)} collective-permute-done((bf16[1248,128]{1,0:T(8,128)(2,1)S(1)}, bf16[1248,128]{1,0:T(8,128)(2,1)S(1)}, u32[]{:S(2)}, u32[]{:S(2)}) %collective-permute-start.8) | collective-permute-done | bytes 319520 | tf_op jit(solution)/shard_map/ppermute | solution.py:48
  39.2 1.0 collective-permute-done.7.refs_4_
  40.3 0.5 collective-permute-start.10
  40.9 0.2 copy-done.17
  41.1 0.8 collective-permute-done.11.refs_8_
  41.9 0.5 collective-permute-done.10.refs_7_
  42.4 0.3 copy-done.27
  42.6 0.7 copy-done.28
  43.4 59.2 %gates_layer.1 = (bf16[6144,1024]{1,0:T(8,128)(2,1)}, bf16[6144,512]{1,0:T(8,128)(2,1)}, bf16[512,512]{1,0:T(8,128)(2,1)}, bf16[1152,1024]{1,0:T(8,128)(2,1)}, b...) custom-call(bf16[6144,512]{1,0:T(8,128)(2,1)} %x.7, ...), custom_call_target="tpu_custom_call" | custom-call | flops 43486543872 | bytes 49152000 | tf_op jit(solution)/shard_map/gates_layer/pallas_call | solution.py:402
  102.6 0.2 collective-permute-start.13
  102.8 1.5 collective-permute-start.14
  104.3 2.2 %collective-permute-done.13.got = bf16[4,4,416,128]{3,2,1,0:T(8,128)(2,1)S(1)} collective-permute-done((bf16[4,4,416,128]{3,2,1,0:T(8,128)(2,1)}, bf16[4,4,416,128]{3,2,1,0:T(8,128)(2,1)S(1)}, u32[]{:S(2)}, u32[]{:S(2)}) %collective-permute-start.13) | collective-permute-done | bytes 1703968 | tf_op jit(solution)/shard_map/ppermute | solution.py:48
  106.5 1.5 copy-done.1
  108.0 0.7 add_cores.1
  108.7 1.9 %collective-permute-start.16 = (bf16[4,416,128]{2,1,0:T(8,128)(2,1)S(1)}, bf16[4,416,128]{2,1,0:T(8,128)(2,1)S(1)}, u32[]{:S(2)}, u32[]{:S(2)}) collective-permute-start(bf16[4,416,128]{2,1,0:T(8,128)(2,1)S(1)} %get-tuple-element.73), channel_id=1, source_target_pairs={{0,16},{1,17},{2,18},{3,19},{4,20},{5,21},{6,22},{7,23},{8,24},{9,... | collective-permute-start | bytes 1277960 | tf_op jit(solution)/shard_map/ppermute | solution.py:48
  110.8 1.5 collective-permute-start.15
  112.2 20.8 %input_layer.1 = (bf16[6144,512]{1,0:T(8,128)(2,1)}, f32[512,512]{1,0:T(8,128)}, f32[8,128]{1,0:T(8,128)}) custom-call(bf16[6144,512]{1,0:T(8,128)(2,1)} %res.3, bf16[6144,1024]{1,0:T(8,128)(2,1)} %get-tuple-element.64.p, bf16[16,6144]{1,0:T(8,128)(2,1)} %copy-done.21, bf16[1152,1024]{1,0:T(8,128)(2,1)} %get-tuple-element.65.w, bf16[4,416,128]{2,1,0:T(8,128)(2,1)} %copy-done.18), custom_call_target="tpu_custom_call" | custom-call | flops 12884901888 | bytes 25165824 | tf_op jit(solution)/shard_map/input_layer/pallas_call | solution.py:491
  133.1 0.7 copy-done.11
  133.7 0.2 add_hop.1
  133.9 0.5 collective-permute-start.18
  134.4 1.3 collective-permute-start.19
  135.7 2.7 %collective-permute-start.20 = (bf16[416,128]{1,0:T(8,128)(2,1)S(1)}, bf16[416,128]{1,0:T(8,128)(2,1)S(1)}, u32[]{:S(2)}, u32[]{:S(2)}) collective-permute-start(bf16[416,128]{1,0:T(8,128)(2,1)S(1)} %get-tuple-element.82), channel_id=1, source_target_pairs={{0,6},{1,7},{2,4},{3,5},{4,2},{5,3},{6,0},{7,1},{8,14},{9,15},{10,... | collective-permute-start | bytes 319496 | tf_op jit(solution)/shard_map/ppermute | solution.py:48
  138.4 9.6 %mixed_layer_0.1 = (bf16[6144,512]{1,0:T(8,128)(2,1)}, bf16[6144,512]{1,0:T(8,128)(2,1)}, f32[8,128]{1,0:T(8,128)}) custom-call(bf16[6144,512]{1,0:T(8,128)(2,1)} %x.7, bf16[6144,512]{1,0:T(8,128)(2,1)} %get-tuple-element.61.hid, bf16[512,1024]{1,0:T(8,128)(2,1)} %get-tuple-element.62.o, f32[8,1024]{1,0:T(8,128)} %copy-done.10, f32[8,128]{1,0:T(8,128)} %copy-done.20), custom_call_target="tpu_custom_call" | custom-call | flops 4294967296 | bytes 16777216 | tf_op jit(solution)/shard_map/mixed_layer_0/pallas_call | solution.py:453
  148.0 0.7 copy-done.12
  148.7 0.8 add_last.1
  149.5 1.5 collective-permute-start.23
  151.0 0.5 collective-permute-start.22
  151.5 1.5 collective-permute-start.21
  153.0 2.9 %all-to-all-start = ((f32[32,1,128]{2,1,0:T(1,128)}), f32[32,1,128]{2,1,0:T(1,128)S(1)}, u32[]{:S(2)}, u32[]{:S(2)}) async-start(f32[32,1,128]{2,1,0:T(1,128)} %bitcast.5), calls=%async_computation | async-start | bytes 32768 | tf_op jit(solution)/shard_map/all_to_all | solution.py:697
  156.0 0.8 copy-done.22
  156.9 6.6 %mixed_layer_4.1 = (bf16[6144,512]{1,0:T(8,128)(2,1)}, bf16[6144,512]{1,0:T(8,128)(2,1)}, bf16[6144,512]{1,0:T(8,128)(2,1)}, f32[8,128]{1,0:T(8,128)}) custom-call(bf16[6144,512]{1,0:T(8,128)(2,1)} %x.7, bf16[6144,512]{1,0:T(8,128)(2,1)} %get-tuple-element.61.hid, ...), custom_call_target="tpu_custom_call", output_to_operand_aliasing={{2}: (6, {}), {0}: (7, {}), {1}: (8, {})} | custom-call | flops 2147483648 | bytes 8388608 | tf_op jit(solution)/shard_map/mixed_layer_4/pallas_call | solution.py:453
  163.6 4.6 %update.1 = (f32[1,128]{1,0:T(1,128)}, f32[64,2,1024]{2,1,0:T(2,128)}, f32[64,2,1024]{2,1,0:T(2,128)}, f32[64,2,1024]{2,1,0:T(2,128)}, f32[80,128]{1,0:T(8,128)}...) custom-call(f32[32,128]{1,0:T(8,128)S(1)} %bitcast.15, ...), custom_call_target="tpu_custom_call" | custom-call | tf_op jit(solution)/shard_map/update/pallas_call | solution.py:618
  (75 shorter events, 0.5 us)
Async XLA Ops:
  0.6 21.7 %copy-start.16 = (s32[6144]{0:T(1024)S(1)}, s32[6144]{0:T(1024)}, u32[]{:S(2)}) copy-start(s32[6144]{0:T(1024)} %param.20) | copy-start | bytes 73732
  0.7 40.1 %copy-start.19 = (s32[6144]{0:T(1024)S(1)}, s32[6144]{0:T(1024)}, u32[]{:S(2)}) copy-start(s32[6144]{0:T(1024)} %param.21) | copy-start | bytes 73732
  3.3 21.1 %copy-start.24 = (bf16[4,416,128]{2,1,0:T(8,128)(2,1)S(1)}, bf16[4,416,128]{2,1,0:T(8,128)(2,1)}, u32[]{:S(2)}) copy-start(bf16[4,416,128]{2,1,0:T(8,128)(2,1)} %get-tuple-element.60.refs_0_) | copy-start | bytes 1277956
  3.3 6.2 %collective-permute-start = (bf16[416,128]{1,0:T(8,128)(2,1)}, bf16[416,128]{1,0:T(8,128)(2,1)S(1)}, u32[]{:S(2)}, u32[]{:S(2)}) collective-permute-start(bf16[416,128]{1,0:T(8,128)(2,1)} %get-tuple-element.59), channel_id=1, source_target_pairs={{0,2},{1,3},{2,0},{3,1},{4,6},{5,7},{6,4},{7,5},{8,10},{9,11},{10,... | collective-permute-start | bytes 319496 | tf_op jit(solution)/shard_map/ppermute | solution.py:48
  6.3 12.4 %collective-permute-start.5 = (bf16[416,128]{1,0:T(8,128)(2,1)}, bf16[416,128]{1,0:T(8,128)(2,1)S(1)}, u32[]{:S(2)}, u32[]{:S(2)}) collective-permute-start(bf16[416,128]{1,0:T(8,128)(2,1)} %get-tuple-element.59), channel_id=1, source_target_pairs={{0,6},{1,7},{2,4},{3,5},{4,2},{5,3},{6,0},{7,1},{8,14},{9,15},{10,... | collective-permute-start | bytes 319496 | tf_op jit(solution)/shard_map/ppermute | solution.py:48
  8.8 9.9 %collective-permute-start.4 = (bf16[416,128]{1,0:T(8,128)(2,1)}, bf16[416,128]{1,0:T(8,128)(2,1)S(1)}, u32[]{:S(2)}, u32[]{:S(2)}) collective-permute-start(bf16[416,128]{1,0:T(8,128)(2,1)} %get-tuple-element.59), channel_id=1, source_target_pairs={{0,4},{1,5},{2,6},{3,7},{4,0},{5,1},{6,2},{7,3},{8,12},{9,13},{10,... | collective-permute-start | bytes 319496 | tf_op jit(solution)/shard_map/ppermute | solution.py:48
  12.0 28.3 %collective-permute-start.1 = (bf16[512,512]{1,0:T(8,128)(2,1)}, bf16[512,512]{1,0:T(8,128)(2,1)S(1)}, u32[]{:S(2)}, u32[]{:S(2)}) collective-permute-start(bf16[512,512]{1,0:T(8,128)(2,1)} %last_rows.1), channel_id=1, source_target_pairs={{0,1},{1,2},{2,3},{3,4},{4,5},{5,6},{6,7},{7,8},{8,9},{9,10},{10,1... | collective-permute-start | bytes 1572872 | tf_op jit(solution)/shard_map/ppermute | solution.py:38
  18.7 12.9 %collective-permute-start.9 = (bf16[1248,128]{1,0:T(8,128)(2,1)S(1)}, bf16[1248,128]{1,0:T(8,128)(2,1)S(1)}, u32[]{:S(2)}, u32[]{:S(2)}) collective-permute-start(bf16[1248,128]{1,0:T(8,128)(2,1)S(1)} %constant_dynamic-update-slice_fusion.refs_2_), channel_id=1, source_target_pairs={{0,24},{1,25},{2,26},{3,27},{4,28},{5,29},{6,30},{7,31},{8,16},{9,... | collective-permute-start | bytes 958472 | tf_op jit(solution)/shard_map/ppermute | solution.py:48
  21.3 18.0 %collective-permute-start.8 = (bf16[1248,128]{1,0:T(8,128)(2,1)S(1)}, bf16[1248,128]{1,0:T(8,128)(2,1)S(1)}, u32[]{:S(2)}, u32[]{:S(2)}) collective-permute-start(bf16[1248,128]{1,0:T(8,128)(2,1)S(1)} %constant_dynamic-update-slice_fusion.refs_2_), channel_id=1, source_target_pairs={{0,16},{1,17},{2,18},{3,19},{4,20},{5,21},{6,22},{7,23},{8,24},{9,... | collective-permute-start | bytes 958472 | tf_op jit(solution)/shard_map/ppermute | solution.py:48
  21.8 18.5 %collective-permute-start.7 = (bf16[1248,128]{1,0:T(8,128)(2,1)S(1)}, bf16[1248,128]{1,0:T(8,128)(2,1)S(1)}, u32[]{:S(2)}, u32[]{:S(2)}) collective-permute-start(bf16[1248,128]{1,0:T(8,128)(2,1)S(1)} %constant_dynamic-update-slice_fusion.refs_2_), channel_id=1, source_target_pairs={{0,8},{1,9},{2,10},{3,11},{4,12},{5,13},{6,14},{7,15},{8,0},{9,1},... | collective-permute-start | bytes 958472 | tf_op jit(solution)/shard_map/ppermute | solution.py:48
  22.3 2.1 %collective-permute-start.2 = (s32[512]{0:T(512)S(1)}, s32[512]{0:T(512)S(1)}, u32[]{:S(2)}, u32[]{:S(2)}) collective-permute-start(s32[512]{0:T(512)S(1)} %slice.6), channel_id=1, source_target_pairs={{0,1},{1,2},{2,3},{3,4},{4,5},{5,6},{6,7},{7,8},{8,9},{9,10},{10,1... | collective-permute-start | bytes 6152 | tf_op jit(solution)/shard_map/ppermute | solution.py:38
  24.4 16.7 %collective-permute-start.3 = (bf16[4,416,128]{2,1,0:T(8,128)(2,1)S(1)}, bf16[4,416,128]{2,1,0:T(8,128)(2,1)S(1)}, u32[]{:S(2)}, u32[]{:S(2)}) collective-permute-start(bf16[4,416,128]{2,1,0:T(8,128)(2,1)S(1)} %copy-done.24), channel_id=1, source_target_pairs={{0,1},{1,0},{2,3},{3,2},{4,5},{5,4},{6,7},{7,6},{8,9},{9,8},{10,11... | collective-permute-start | bytes 1277960 | tf_op jit(solution)/shard_map/ppermute | solution.py:48
  31.6 9.5 %collective-permute-start.6 = (bf16[1248,128]{1,0:T(8,128)(2,1)S(1)}, bf16[1248,128]{1,0:T(8,128)(2,1)S(1)}, u32[]{:S(2)}, u32[]{:S(2)}) collective-permute-start(bf16[1248,128]{1,0:T(8,128)(2,1)S(1)} %constant_dynamic-update-slice_fusion.refs_2_), channel_id=1, source_target_pairs={{0,1},{1,0},{2,3},{3,2},{4,5},{5,4},{6,7},{7,6},{8,9},{9,8},{10,11... | collective-permute-start | bytes 958472 | tf_op jit(solution)/shard_map/ppermute | solution.py:48
  39.2 1.9 %collective-permute-start.12 = (bf16[1248,128]{1,0:T(8,128)(2,1)S(1)}, bf16[1248,128]{1,0:T(8,128)(2,1)S(1)}, u32[]{:S(2)}, u32[]{:S(2)}) collective-permute-start(bf16[1248,128]{1,0:T(8,128)(2,1)S(1)} %collective-permute-done.9.refs_6_), channel_id=1, source_target_pairs={{0,1},{1,0},{2,3},{3,2},{4,5},{5,4},{6,7},{7,6},{8,9},{9,8},{10,11... | collective-permute-start | bytes 958472 | tf_op jit(solution)/shard_map/ppermute | solution.py:48
  40.3 1.6 collective-permute-start.11
  40.3 2.1 %collective-permute-start.10 = (bf16[1248,128]{1,0:T(8,128)(2,1)S(1)}, bf16[1248,128]{1,0:T(8,128)(2,1)S(1)}, u32[]{:S(2)}, u32[]{:S(2)}) collective-permute-start(bf16[1248,128]{1,0:T(8,128)(2,1)S(1)} %collective-permute-done.7.refs_4_), channel_id=1, source_target_pairs={{0,1},{1,0},{2,3},{3,2},{4,5},{5,4},{6,7},{7,6},{8,9},{9,8},{10,11... | collective-permute-start | bytes 958472 | tf_op jit(solution)/shard_map/ppermute | solution.py:48
  41.1 61.5 %copy-start.21 = (bf16[16,6144]{1,0:T(8,128)(2,1)}, bf16[16,6144]{1,0:T(8,128)(2,1)S(1)}, u32[]{:S(2)}) copy-start(bf16[16,6144]{1,0:T(8,128)(2,1)S(1)} %flag_rows.1.flags) | copy-start | bytes 589828
  41.1 1.3 copy-start.25
  41.1 1.2 copy-start.26
  102.6 8.1 %copy-start.10 = (f32[8,1024]{1,0:T(8,128)}, f32[8,1024]{1,0:T(8,128)S(1)}, u32[]{:S(2)}) copy-start(f32[8,1024]{1,0:T(8,128)S(1)} %get-tuple-element.63.bias) | copy-start | bytes 98308
  102.6 3.9 %collective-permute-start.13 = (bf16[4,4,416,128]{3,2,1,0:T(8,128)(2,1)}, bf16[4,4,416,128]{3,2,1,0:T(8,128)(2,1)S(1)}, u32[]{:S(2)}, u32[]{:S(2)}) collective-permute-start(bf16[4,4,416,128]{3,2,1,0:T(8,128)(2,1)} %get-tuple-element.67), channel_id=1, source_target_pairs={{0,1},{1,0},{2,3},{3,2},{4,5},{5,4},{6,7},{7,6},{8,9},{9,8},{10,11... | collective-permute-start | bytes 5111816 | tf_op jit(solution)/shard_map/ppermute | solution.py:48
  102.8 53.1 %collective-permute-start.14 = (bf16[512,512]{1,0:T(8,128)(2,1)}, bf16[512,512]{1,0:T(8,128)(2,1)S(1)}, u32[]{:S(2)}, u32[]{:S(2)}) collective-permute-start(bf16[512,512]{1,0:T(8,128)(2,1)} %get-tuple-element.70), channel_id=1, source_target_pairs={{1,0},{2,1},{3,2},{4,3},{5,4},{6,5},{7,6},{8,7},{9,8},{10,9},{11,1... | collective-permute-start | bytes 1572872 | tf_op jit(solution)/shard_map/ppermute | solution.py:38
  106.5 1.5 copy-start.1
  108.7 3.6 %copy-start.18 = (bf16[4,416,128]{2,1,0:T(8,128)(2,1)}, bf16[4,416,128]{2,1,0:T(8,128)(2,1)S(1)}, u32[]{:S(2)}) copy-start(bf16[4,416,128]{2,1,0:T(8,128)(2,1)S(1)} %get-tuple-element.68.refs_0_) | copy-start | bytes 1277956
  108.7 24.3 %collective-permute-start.16 = (bf16[4,416,128]{2,1,0:T(8,128)(2,1)S(1)}, bf16[4,416,128]{2,1,0:T(8,128)(2,1)S(1)}, u32[]{:S(2)}, u32[]{:S(2)}) collective-permute-start(bf16[4,416,128]{2,1,0:T(8,128)(2,1)S(1)} %get-tuple-element.73), channel_id=1, source_target_pairs={{0,16},{1,17},{2,18},{3,19},{4,20},{5,21},{6,22},{7,23},{8,24},{9,... | collective-permute-start | bytes 1277960 | tf_op jit(solution)/shard_map/ppermute | solution.py:48
  110.6 22.4 %collective-permute-start.17 = (bf16[4,416,128]{2,1,0:T(8,128)(2,1)S(1)}, bf16[4,416,128]{2,1,0:T(8,128)(2,1)S(1)}, u32[]{:S(2)}, u32[]{:S(2)}) collective-permute-start(bf16[4,416,128]{2,1,0:T(8,128)(2,1)S(1)} %get-tuple-element.74), channel_id=1, source_target_pairs={{0,24},{1,25},{2,26},{3,27},{4,28},{5,29},{6,30},{7,31},{8,16},{9,... | collective-permute-start | bytes 1277960 | tf_op jit(solution)/shard_map/ppermute | solution.py:48
  110.8 22.3 %collective-permute-start.15 = (bf16[4,416,128]{2,1,0:T(8,128)(2,1)S(1)}, bf16[4,416,128]{2,1,0:T(8,128)(2,1)S(1)}, u32[]{:S(2)}, u32[]{:S(2)}) collective-permute-start(bf16[4,416,128]{2,1,0:T(8,128)(2,1)S(1)} %get-tuple-element.68.refs_0_), channel_id=1, source_target_pairs={{0,8},{1,9},{2,10},{3,11},{4,12},{5,13},{6,14},{7,15},{8,0},{9,1},... | collective-permute-start | bytes 1277960 | tf_op jit(solution)/shard_map/ppermute | solution.py:48
  133.9 4.5 %copy-start.20 = (f32[8,128]{1,0:T(8,128)}, f32[8,128]{1,0:T(8,128)S(1)}, u32[]{:S(2)}) copy-start(f32[8,128]{1,0:T(8,128)S(1)} %get-tuple-element.76.refs_0_) | copy-start | bytes 12292
  133.9 14.0 %collective-permute-start.18 = (bf16[416,128]{1,0:T(8,128)(2,1)S(1)}, bf16[416,128]{1,0:T(8,128)(2,1)S(1)}, u32[]{:S(2)}, u32[]{:S(2)}) collective-permute-start(bf16[416,128]{1,0:T(8,128)(2,1)S(1)} %get-tuple-element.80), channel_id=1, source_target_pairs={{0,2},{1,3},{2,0},{3,1},{4,6},{5,7},{6,4},{7,5},{8,10},{9,11},{10,... | collective-permute-start | bytes 319496 | tf_op jit(solution)/shard_map/ppermute | solution.py:48
  134.4 13.5 %collective-permute-start.19 = (bf16[416,128]{1,0:T(8,128)(2,1)S(1)}, bf16[416,128]{1,0:T(8,128)(2,1)S(1)}, u32[]{:S(2)}, u32[]{:S(2)}) collective-permute-start(bf16[416,128]{1,0:T(8,128)(2,1)S(1)} %get-tuple-element.81), channel_id=1, source_target_pairs={{0,4},{1,5},{2,6},{3,7},{4,0},{5,1},{6,2},{7,3},{8,12},{9,13},{10,... | collective-permute-start | bytes 319496 | tf_op jit(solution)/shard_map/ppermute | solution.py:48
  135.7 12.3 %collective-permute-start.20 = (bf16[416,128]{1,0:T(8,128)(2,1)S(1)}, bf16[416,128]{1,0:T(8,128)(2,1)S(1)}, u32[]{:S(2)}, u32[]{:S(2)}) collective-permute-start(bf16[416,128]{1,0:T(8,128)(2,1)S(1)} %get-tuple-element.82), channel_id=1, source_target_pairs={{0,6},{1,7},{2,4},{3,5},{4,2},{5,3},{6,0},{7,1},{8,14},{9,15},{10,... | collective-permute-start | bytes 319496 | tf_op jit(solution)/shard_map/ppermute | solution.py:48
  149.5 14.0 %collective-permute-start.23 = (f32[416,128]{1,0:T(8,128)S(1)}, f32[416,128]{1,0:T(8,128)S(1)}, u32[]{:S(2)}, u32[]{:S(2)}) collective-permute-start(f32[416,128]{1,0:T(8,128)S(1)} %get-tuple-element.88.refs_1_), channel_id=1, source_target_pairs={{0,24},{1,25},{2,26},{3,27},{4,28},{5,29},{6,30},{7,31},{8,16},{9,... | collective-permute-start | bytes 638984 | tf_op jit(solution)/shard_map/ppermute | solution.py:48
  151.0 12.5 %collective-permute-start.22 = (f32[416,128]{1,0:T(8,128)S(1)}, f32[416,128]{1,0:T(8,128)S(1)}, u32[]{:S(2)}, u32[]{:S(2)}) collective-permute-start(f32[416,128]{1,0:T(8,128)S(1)} %get-tuple-element.88.refs_1_), channel_id=1, source_target_pairs={{0,16},{1,17},{2,18},{3,19},{4,20},{5,21},{6,22},{7,23},{8,24},{9,... | collective-permute-start | bytes 638984 | tf_op jit(solution)/shard_map/ppermute | solution.py:48
  151.5 12.0 %collective-permute-start.21 = (f32[416,128]{1,0:T(8,128)S(1)}, f32[416,128]{1,0:T(8,128)S(1)}, u32[]{:S(2)}, u32[]{:S(2)}) collective-permute-start(f32[416,128]{1,0:T(8,128)S(1)} %get-tuple-element.88.refs_1_), channel_id=1, source_target_pairs={{0,8},{1,9},{2,10},{3,11},{4,12},{5,13},{6,14},{7,15},{8,0},{9,1},... | collective-permute-start | bytes 638984 | tf_op jit(solution)/shard_map/ppermute | solution.py:48
  153.0 10.5 %all-to-all-start = ((f32[32,1,128]{2,1,0:T(1,128)}), f32[32,1,128]{2,1,0:T(1,128)S(1)}, u32[]{:S(2)}, u32[]{:S(2)}) async-start(f32[32,1,128]{2,1,0:T(1,128)} %bitcast.5), calls=%async_computation | async-start | bytes 32768 | tf_op jit(solution)/shard_map/all_to_all | solution.py:697
  156.0 0.8 copy-start.22
  156.8 6.8 %copy-start = (f32[64,2,1024]{2,1,0:T(2,128)S(1)}, f32[64,2,1024]{2,1,0:T(2,128)}, u32[]{:S(2)}) copy-start(f32[64,2,1024]{2,1,0:T(2,128)} %refs_7_.1) | copy-start | bytes 1572868
  156.8 6.8 %copy-start.2 = (f32[64,1024]{1,0:T(8,128)S(1)}, f32[64,1024]{1,0:T(8,128)}, u32[]{:S(2)}) copy-start(f32[64,1024]{1,0:T(8,128)} %refs_13_.1) | copy-start | bytes 786436
  156.8 6.8 %copy-start.3 = (f32[64,2,1024]{2,1,0:T(2,128)S(1)}, f32[64,2,1024]{2,1,0:T(2,128)}, u32[]{:S(2)}) copy-start(f32[64,2,1024]{2,1,0:T(2,128)} %refs_5_.1) | copy-start | bytes 1572868
  156.8 6.8 %copy-start.4 = (f32[64,2,1024]{2,1,0:T(2,128)S(1)}, f32[64,2,1024]{2,1,0:T(2,128)}, u32[]{:S(2)}) copy-start(f32[64,2,1024]{2,1,0:T(2,128)} %refs_6_.1) | copy-start | bytes 1572868
  156.8 6.8 %copy-start.5 = (f32[64,1024]{1,0:T(8,128)S(1)}, f32[64,1024]{1,0:T(8,128)}, u32[]{:S(2)}) copy-start(f32[64,1024]{1,0:T(8,128)} %refs_11_.1) | copy-start | bytes 786436
  156.8 6.8 %copy-start.6 = (f32[64,1024]{1,0:T(8,128)S(1)}, f32[64,1024]{1,0:T(8,128)}, u32[]{:S(2)}) copy-start(f32[64,1024]{1,0:T(8,128)} %refs_12_.1) | copy-start | bytes 786436
  156.8 6.8 %copy-start.7 = (f32[80,128]{1,0:T(8,128)S(1)}, f32[80,128]{1,0:T(8,128)}, u32[]{:S(2)}) copy-start(f32[80,128]{1,0:T(8,128)} %refs_10_.1) | copy-start | bytes 122884
  156.8 6.8 %copy-start.8 = (f32[80,128]{1,0:T(8,128)S(1)}, f32[80,128]{1,0:T(8,128)}, u32[]{:S(2)}) copy-start(f32[80,128]{1,0:T(8,128)} %refs_8_.1) | copy-start | bytes 122884
  156.8 6.8 %copy-start.9 = (f32[80,128]{1,0:T(8,128)S(1)}, f32[80,128]{1,0:T(8,128)}, u32[]{:S(2)}) copy-start(f32[80,128]{1,0:T(8,128)} %refs_9_.1) | copy-start | bytes 122884
  156.8 6.8 %copy-start.13 = (f32[256]{0:T(256)S(1)}, f32[256]{0:T(256)}, u32[]{:S(2)}) copy-start(f32[256]{0:T(256)} %param.27) | copy-start | bytes 3076
  156.8 6.8 %copy-start.14 = (f32[256]{0:T(256)S(1)}, f32[256]{0:T(256)}, u32[]{:S(2)}) copy-start(f32[256]{0:T(256)} %param.34) | copy-start | bytes 3076
  156.8 6.8 %copy-start.15 = (f32[256]{0:T(256)S(1)}, f32[256]{0:T(256)}, u32[]{:S(2)}) copy-start(f32[256]{0:T(256)} %param.35) | copy-start | bytes 3076
  (6 other events, 4.3 us)

commit v5 on v4

--- a/solution.py
+++ b/solution.py
@@ -25,7 +25,7 @@
 KEEP = 81
 LINK = 82
 ROWS = 512
-GATES_MIB = 52
+GATES_MIB = 45
 ARRIVE = 10**10
 BF = jnp.bfloat16
 F32 = jnp.float32

time: 169 us -> 165 us (0.976)
  local copies, waits for them, and re-layouts: 6.53 us -> 3.85 us
    unnamed x60 -> x52, local copies, waits for them, and re-layouts: 6.51 us -> 3.83 us
  transfers between devices with their start and end apart: 25 -> 25, of which waited for: 9 -> 9; matrix products, arithmetic and copies ran while one was open for 1% -> 1% of each run, Pallas kernels for 24% -> 25%
where the time goes in v5:
time: 165 us
  Pallas kernels  106 us (64%)
  starting transfers between devices  29 us (18%)
  waiting for transfers between devices  24.8 us (15%)
  local copies, waits for them, and re-layouts  3.85 us (2%)
    pallas_call x1, Pallas kernels, gates_layer(): pl.pallas_call(functools.partial(gates_body, split, subs), grid=(steps,),...  58 us
    ppermute x21, waiting for transfers between devices, swap(): return lax.ppermute(x, BOTH, pairs)  24 us
    ppermute x21, starting transfers between devices, swap(): return lax.ppermute(x, BOTH, pairs)  22 us
    pallas_call x1, Pallas kernels, input_layer(): pl.pallas_call(input_body, grid=(steps,), in_specs=[by_row(512), by_row(1...  20.8 us
    pallas_call x2, Pallas kernels, mixed_layer(): pl.pallas_call(patch_body if patched else mixed_body, grid=(steps,), in_s...  16.2 us
    pallas_call x1, Pallas kernels, update(): pl.pallas_call(update_body, in_specs=[VMEM] * 17, out_specs=[VMEM] * 13,...  4.63 us
    ppermute x3, starting transfers between devices, from_behind(): return lax.ppermute(x, axis, pairs)  4.05 us
    unnamed x52, local copies, waits for them, and re-layouts  3.83 us
  transfers between devices with their start and end apart: 25, of which 9 were waited for; matrix products, arithmetic and copies ran while one was open for 1% of the time, Pallas kernels for 25%

profile of v5, /device:TPU:0, one launch (start us, length us, event | category | flops | bytes accessed | tf_op | source)
XLA Modules:
  0.0 164.8 jit_solution(12514748673958940998)
XLA Ops:
  0.7 2.6 %pack_weights.1 = (bf16[4,416,128]{2,1,0:T(8,128)(2,1)}, bf16[416,128]{1,0:T(8,128)(2,1)}) custom-call(f32[64,2,1024]{2,1,0:T(2,128)} %refs_7_.1, f32[80,128]{1,0:T(8,128)} %refs_10_.1, f32[2,128]{1,0:T(2,128)} %bitcast.16, f32[64,1024]{1,0:T(8,128)} %refs_13_.1), custom_call_target="tpu_custom_call" | custom-call | tf_op jit(solution)/shard_map/pack_weights/pallas_call | solution.py:111
  3.3 3.0 %collective-permute-start = (bf16[416,128]{1,0:T(8,128)(2,1)}, bf16[416,128]{1,0:T(8,128)(2,1)S(1)}, u32[]{:S(2)}, u32[]{:S(2)}) collective-permute-start(bf16[416,128]{1,0:T(8,128)(2,1)} %get-tuple-element.59), channel_id=1, source_target_pairs={{0,2},{1,3},{2,0},{3,1},{4,6},{5,7},{6,4},{7,5},{8,10},{9,11},{10,... | collective-permute-start | bytes 319496 | tf_op jit(solution)/shard_map/ppermute | solution.py:48
  6.3 2.5 %collective-permute-start.5 = (bf16[416,128]{1,0:T(8,128)(2,1)}, bf16[416,128]{1,0:T(8,128)(2,1)S(1)}, u32[]{:S(2)}, u32[]{:S(2)}) collective-permute-start(bf16[416,128]{1,0:T(8,128)(2,1)} %get-tuple-element.59), channel_id=1, source_target_pairs={{0,6},{1,7},{2,4},{3,5},{4,2},{5,3},{6,0},{7,1},{8,14},{9,15},{10,... | collective-permute-start | bytes 319496 | tf_op jit(solution)/shard_map/ppermute | solution.py:48
  8.8 0.1 collective-permute-start.4
  8.9 0.6 collective-permute-done._
  9.5 0.6 copy-done.24
  10.1 1.9 %last_rows.1 = bf16[512,512]{1,0:T(8,128)(2,1)} custom-call(bf16[6144,512]{1,0:T(8,128)(2,1)} %x.7, bf16[416,128]{1,0:T(8,128)(2,1)} %copy-done.24), custom_call_target="tpu_custom_call" | custom-call | tf_op jit(solution)/shard_map/last_rows/pallas_call | solution.py:130
  12.0 1.3 collective-permute-start.1
  13.3 0.9 constant_dynamic-update-slice_fusion.2
  14.2 4.5 %collective-permute-done.4 = bf16[416,128]{1,0:T(8,128)(2,1)S(1)} collective-permute-done((bf16[416,128]{1,0:T(8,128)(2,1)}, bf16[416,128]{1,0:T(8,128)(2,1)S(1)}, u32[]{:S(2)}, u32[]{:S(2)}) %collective-permute-start.4) | collective-permute-done | bytes 106528 | tf_op jit(solution)/shard_map/ppermute | solution.py:48
  18.7 2.5 %collective-permute-start.9 = (bf16[1248,128]{1,0:T(8,128)(2,1)S(1)}, bf16[1248,128]{1,0:T(8,128)(2,1)S(1)}, u32[]{:S(2)}, u32[]{:S(2)}) collective-permute-start(bf16[1248,128]{1,0:T(8,128)(2,1)S(1)} %constant_dynamic-update-slice_fusion.refs_2_), channel_id=1, source_target_pairs={{0,24},{1,25},{2,26},{3,27},{4,28},{5,29},{6,30},{7,31},{8,16},{9,... | collective-permute-start | bytes 958472 | tf_op jit(solution)/shard_map/ppermute | solution.py:48
  21.3 0.5 collective-permute-start.8
  21.8 0.5 collective-permute-start.7
  22.3 1.3 collective-permute-start.2
  23.6 0.8 collective-permute-done.2
  24.4 0.5 collective-permute-start.3
  24.9 6.7 %collective-permute-done.9.refs_6_ = bf16[1248,128]{1,0:T(8,128)(2,1)S(1)} collective-permute-done((bf16[1248,128]{1,0:T(8,128)(2,1)S(1)}, bf16[1248,128]{1,0:T(8,128)(2,1)S(1)}, u32[]{:S(2)}, u32[]{:S(2)}) %collective-permute-start.9) | collective-permute-done | bytes 319520 | tf_op jit(solution)/shard_map/ppermute | solution.py:48
  31.6 7.6 %collective-permute-done.8.refs_5_ = bf16[1248,128]{1,0:T(8,128)(2,1)S(1)} collective-permute-done((bf16[1248,128]{1,0:T(8,128)(2,1)S(1)}, bf16[1248,128]{1,0:T(8,128)(2,1)S(1)}, u32[]{:S(2)}, u32[]{:S(2)}) %collective-permute-start.8) | collective-permute-done | bytes 319520 | tf_op jit(solution)/shard_map/ppermute | solution.py:48
  39.2 0.0 collective-permute-start.12
  39.2 1.0 collective-permute-done.7.refs_4_
  40.3 0.5 collective-permute-start.10
  40.8 0.1 flag_rows.1.flags
  40.9 1.0 collective-permute-done.11.refs_8_
  41.9 0.5 collective-permute-done.10.refs_7_
  42.4 58.0 %gates_layer.1 = (bf16[6144,1024]{1,0:T(8,128)(2,1)}, bf16[6144,512]{1,0:T(8,128)(2,1)}, bf16[512,512]{1,0:T(8,128)(2,1)S(1)}, bf16[1152,1024]{1,0:T(8,128)(2,1)...) custom-call(bf16[6144,512]{1,0:T(8,128)(2,1)} %x.7, ...), custom_call_target="tpu_custom_call" | custom-call | flops 43486543872 | bytes 49152000 | tf_op jit(solution)/shard_map/gates_layer/pallas_call | solution.py:402
  100.4 0.2 collective-permute-start.13
  100.6 1.5 collective-permute-start.14
  102.1 2.2 %collective-permute-done.13.got = bf16[4,4,416,128]{3,2,1,0:T(8,128)(2,1)S(1)} collective-permute-done((bf16[4,4,416,128]{3,2,1,0:T(8,128)(2,1)}, bf16[4,4,416,128]{3,2,1,0:T(8,128)(2,1)S(1)}, u32[]{:S(2)}, u32[]{:S(2)}) %collective-permute-start.13) | collective-permute-done | bytes 1703968 | tf_op jit(solution)/shard_map/ppermute | solution.py:48
  104.3 0.7 add_cores.1
  105.0 2.0 %collective-permute-start.16 = (bf16[4,416,128]{2,1,0:T(8,128)(2,1)S(1)}, bf16[4,416,128]{2,1,0:T(8,128)(2,1)S(1)}, u32[]{:S(2)}, u32[]{:S(2)}) collective-permute-start(bf16[4,416,128]{2,1,0:T(8,128)(2,1)S(1)} %get-tuple-element.73), channel_id=1, source_target_pairs={{0,16},{1,17},{2,18},{3,19},{4,20},{5,21},{6,22},{7,23},{8,24},{9,... | collective-permute-start | bytes 1277960 | tf_op jit(solution)/shard_map/ppermute | solution.py:48
  107.0 0.1 collective-permute-start.17
  107.1 1.5 collective-permute-start.15
  108.6 20.8 %input_layer.1 = (bf16[6144,512]{1,0:T(8,128)(2,1)}, f32[512,512]{1,0:T(8,128)}, f32[8,128]{1,0:T(8,128)}) custom-call(bf16[6144,512]{1,0:T(8,128)(2,1)} %res.3, bf16[6144,1024]{1,0:T(8,128)(2,1)} %get-tuple-element.64.p, bf16[16,6144]{1,0:T(8,128)(2,1)} %copy-done.22, bf16[1152,1024]{1,0:T(8,128)(2,1)} %get-tuple-element.65.w, bf16[4,416,128]{2,1,0:T(8,128)(2,1)} %copy-done.19), custom_call_target="tpu_custom_call" | custom-call | flops 12884901888 | bytes 25165824 | tf_op jit(solution)/shard_map/input_layer/pallas_call | solution.py:491
  129.4 0.7 copy-done.11
  130.0 0.2 add_hop.1
  130.2 0.5 collective-permute-start.18
  130.8 1.6 collective-permute-start.19
  132.3 2.4 %collective-permute-start.20 = (bf16[416,128]{1,0:T(8,128)(2,1)S(1)}, bf16[416,128]{1,0:T(8,128)(2,1)S(1)}, u32[]{:S(2)}, u32[]{:S(2)}) collective-permute-start(bf16[416,128]{1,0:T(8,128)(2,1)S(1)} %get-tuple-element.82), channel_id=1, source_target_pairs={{0,6},{1,7},{2,4},{3,5},{4,2},{5,3},{6,0},{7,1},{8,14},{9,15},{10,... | collective-permute-start | bytes 319496 | tf_op jit(solution)/shard_map/ppermute | solution.py:48
  134.7 9.6 %mixed_layer_0.1 = (bf16[6144,512]{1,0:T(8,128)(2,1)}, bf16[6144,512]{1,0:T(8,128)(2,1)}, f32[8,128]{1,0:T(8,128)}) custom-call(bf16[6144,512]{1,0:T(8,128)(2,1)} %x.7, bf16[6144,512]{1,0:T(8,128)(2,1)} %get-tuple-element.61.hid, bf16[512,1024]{1,0:T(8,128)(2,1)} %copy-done.1, f32[8,1024]{1,0:T(8,128)} %copy-done.10, f32[8,128]{1,0:T(8,128)} %copy-done.21), custom_call_target="tpu_custom_call" | custom-call | flops 4294967296 | bytes 16777216 | tf_op jit(solution)/shard_map/mixed_layer_0/pallas_call | solution.py:453
  144.3 0.7 copy-done.12
  145.0 0.8 add_last.1
  145.8 1.5 collective-permute-start.23
  147.4 0.5 collective-permute-start.22
  147.8 1.5 collective-permute-start.21
  149.3 3.0 %all-to-all-start = ((f32[32,1,128]{2,1,0:T(1,128)}), f32[32,1,128]{2,1,0:T(1,128)S(1)}, u32[]{:S(2)}, u32[]{:S(2)}) async-start(f32[32,1,128]{2,1,0:T(1,128)} %bitcast.5), calls=%async_computation | async-start | bytes 32768 | tf_op jit(solution)/shard_map/all_to_all | solution.py:697
  152.3 0.8 copy-done.23
  153.2 6.6 %mixed_layer_4.1 = (bf16[6144,512]{1,0:T(8,128)(2,1)}, bf16[6144,512]{1,0:T(8,128)(2,1)}, bf16[6144,512]{1,0:T(8,128)(2,1)}, f32[8,128]{1,0:T(8,128)}) custom-call(bf16[6144,512]{1,0:T(8,128)(2,1)} %x.7, bf16[6144,512]{1,0:T(8,128)(2,1)} %get-tuple-element.61.hid, ...), custom_call_target="tpu_custom_call", output_to_operand_aliasing={{2}: (6, {}), {0}: (7, {}), {1}: (8, {})} | custom-call | flops 2147483648 | bytes 8388608 | tf_op jit(solution)/shard_map/mixed_layer_4/pallas_call | solution.py:453
  160.0 4.6 %update.1 = (f32[1,128]{1,0:T(1,128)}, f32[64,2,1024]{2,1,0:T(2,128)}, f32[64,2,1024]{2,1,0:T(2,128)}, f32[64,2,1024]{2,1,0:T(2,128)}, f32[80,128]{1,0:T(8,128)}...) custom-call(f32[32,128]{1,0:T(8,128)S(1)} %bitcast.15, ...), custom_call_target="tpu_custom_call" | custom-call | tf_op jit(solution)/shard_map/update/pallas_call | solution.py:618
  (67 shorter events, 0.2 us)
Async XLA Ops:
  0.6 21.7 %copy-start.16 = (s32[6144]{0:T(1024)S(1)}, s32[6144]{0:T(1024)}, u32[]{:S(2)}) copy-start(s32[6144]{0:T(1024)} %param.20) | copy-start | bytes 73732
  0.7 40.1 %copy-start.20 = (s32[6144]{0:T(1024)S(1)}, s32[6144]{0:T(1024)}, u32[]{:S(2)}) copy-start(s32[6144]{0:T(1024)} %param.21) | copy-start | bytes 73732
  3.3 21.1 %copy-start.18 = (bf16[4,416,128]{2,1,0:T(8,128)(2,1)S(1)}, bf16[4,416,128]{2,1,0:T(8,128)(2,1)}, u32[]{:S(2)}) copy-start(bf16[4,416,128]{2,1,0:T(8,128)(2,1)} %get-tuple-element.60.refs_0_) | copy-start | bytes 1277956
  3.3 6.2 %collective-permute-start = (bf16[416,128]{1,0:T(8,128)(2,1)}, bf16[416,128]{1,0:T(8,128)(2,1)S(1)}, u32[]{:S(2)}, u32[]{:S(2)}) collective-permute-start(bf16[416,128]{1,0:T(8,128)(2,1)} %get-tuple-element.59), channel_id=1, source_target_pairs={{0,2},{1,3},{2,0},{3,1},{4,6},{5,7},{6,4},{7,5},{8,10},{9,11},{10,... | collective-permute-start | bytes 319496 | tf_op jit(solution)/shard_map/ppermute | solution.py:48
  6.3 12.4 %collective-permute-start.5 = (bf16[416,128]{1,0:T(8,128)(2,1)}, bf16[416,128]{1,0:T(8,128)(2,1)S(1)}, u32[]{:S(2)}, u32[]{:S(2)}) collective-permute-start(bf16[416,128]{1,0:T(8,128)(2,1)} %get-tuple-element.59), channel_id=1, source_target_pairs={{0,6},{1,7},{2,4},{3,5},{4,2},{5,3},{6,0},{7,1},{8,14},{9,15},{10,... | collective-permute-start | bytes 319496 | tf_op jit(solution)/shard_map/ppermute | solution.py:48
  8.8 9.9 %collective-permute-start.4 = (bf16[416,128]{1,0:T(8,128)(2,1)}, bf16[416,128]{1,0:T(8,128)(2,1)S(1)}, u32[]{:S(2)}, u32[]{:S(2)}) collective-permute-start(bf16[416,128]{1,0:T(8,128)(2,1)} %get-tuple-element.59), channel_id=1, source_target_pairs={{0,4},{1,5},{2,6},{3,7},{4,0},{5,1},{6,2},{7,3},{8,12},{9,13},{10,... | collective-permute-start | bytes 319496 | tf_op jit(solution)/shard_map/ppermute | solution.py:48
  12.0 28.3 %collective-permute-start.1 = (bf16[512,512]{1,0:T(8,128)(2,1)}, bf16[512,512]{1,0:T(8,128)(2,1)S(1)}, u32[]{:S(2)}, u32[]{:S(2)}) collective-permute-start(bf16[512,512]{1,0:T(8,128)(2,1)} %last_rows.1), channel_id=1, source_target_pairs={{0,1},{1,2},{2,3},{3,4},{4,5},{5,6},{6,7},{7,8},{8,9},{9,10},{10,1... | collective-permute-start | bytes 1572872 | tf_op jit(solution)/shard_map/ppermute | solution.py:38
  18.7 12.9 %collective-permute-start.9 = (bf16[1248,128]{1,0:T(8,128)(2,1)S(1)}, bf16[1248,128]{1,0:T(8,128)(2,1)S(1)}, u32[]{:S(2)}, u32[]{:S(2)}) collective-permute-start(bf16[1248,128]{1,0:T(8,128)(2,1)S(1)} %constant_dynamic-update-slice_fusion.refs_2_), channel_id=1, source_target_pairs={{0,24},{1,25},{2,26},{3,27},{4,28},{5,29},{6,30},{7,31},{8,16},{9,... | collective-permute-start | bytes 958472 | tf_op jit(solution)/shard_map/ppermute | solution.py:48
  21.3 18.0 %collective-permute-start.8 = (bf16[1248,128]{1,0:T(8,128)(2,1)S(1)}, bf16[1248,128]{1,0:T(8,128)(2,1)S(1)}, u32[]{:S(2)}, u32[]{:S(2)}) collective-permute-start(bf16[1248,128]{1,0:T(8,128)(2,1)S(1)} %constant_dynamic-update-slice_fusion.refs_2_), channel_id=1, source_target_pairs={{0,16},{1,17},{2,18},{3,19},{4,20},{5,21},{6,22},{7,23},{8,24},{9,... | collective-permute-start | bytes 958472 | tf_op jit(solution)/shard_map/ppermute | solution.py:48
  21.8 18.5 %collective-permute-start.7 = (bf16[1248,128]{1,0:T(8,128)(2,1)S(1)}, bf16[1248,128]{1,0:T(8,128)(2,1)S(1)}, u32[]{:S(2)}, u32[]{:S(2)}) collective-permute-start(bf16[1248,128]{1,0:T(8,128)(2,1)S(1)} %constant_dynamic-update-slice_fusion.refs_2_), channel_id=1, source_target_pairs={{0,8},{1,9},{2,10},{3,11},{4,12},{5,13},{6,14},{7,15},{8,0},{9,1},... | collective-permute-start | bytes 958472 | tf_op jit(solution)/shard_map/ppermute | solution.py:48
  22.3 2.1 %collective-permute-start.2 = (s32[512]{0:T(512)S(1)}, s32[512]{0:T(512)S(1)}, u32[]{:S(2)}, u32[]{:S(2)}) collective-permute-start(s32[512]{0:T(512)S(1)} %slice.6), channel_id=1, source_target_pairs={{0,1},{1,2},{2,3},{3,4},{4,5},{5,6},{6,7},{7,8},{8,9},{9,10},{10,1... | collective-permute-start | bytes 6152 | tf_op jit(solution)/shard_map/ppermute | solution.py:38
  24.4 16.5 %collective-permute-start.3 = (bf16[4,416,128]{2,1,0:T(8,128)(2,1)S(1)}, bf16[4,416,128]{2,1,0:T(8,128)(2,1)S(1)}, u32[]{:S(2)}, u32[]{:S(2)}) collective-permute-start(bf16[4,416,128]{2,1,0:T(8,128)(2,1)S(1)} %copy-done.18), channel_id=1, source_target_pairs={{0,1},{1,0},{2,3},{3,2},{4,5},{5,4},{6,7},{7,6},{8,9},{9,8},{10,11... | collective-permute-start | bytes 1277960 | tf_op jit(solution)/shard_map/ppermute | solution.py:48
  31.6 9.3 %collective-permute-start.6 = (bf16[1248,128]{1,0:T(8,128)(2,1)S(1)}, bf16[1248,128]{1,0:T(8,128)(2,1)S(1)}, u32[]{:S(2)}, u32[]{:S(2)}) collective-permute-start(bf16[1248,128]{1,0:T(8,128)(2,1)S(1)} %constant_dynamic-update-slice_fusion.refs_2_), channel_id=1, source_target_pairs={{0,1},{1,0},{2,3},{3,2},{4,5},{5,4},{6,7},{7,6},{8,9},{9,8},{10,11... | collective-permute-start | bytes 958472 | tf_op jit(solution)/shard_map/ppermute | solution.py:48
  39.2 1.7 %collective-permute-start.12 = (bf16[1248,128]{1,0:T(8,128)(2,1)S(1)}, bf16[1248,128]{1,0:T(8,128)(2,1)S(1)}, u32[]{:S(2)}, u32[]{:S(2)}) collective-permute-start(bf16[1248,128]{1,0:T(8,128)(2,1)S(1)} %collective-permute-done.9.refs_6_), channel_id=1, source_target_pairs={{0,1},{1,0},{2,3},{3,2},{4,5},{5,4},{6,7},{7,6},{8,9},{9,8},{10,11... | collective-permute-start | bytes 958472 | tf_op jit(solution)/shard_map/ppermute | solution.py:48
  40.3 1.6 collective-permute-start.11
  40.3 2.1 %collective-permute-start.10 = (bf16[1248,128]{1,0:T(8,128)(2,1)S(1)}, bf16[1248,128]{1,0:T(8,128)(2,1)S(1)}, u32[]{:S(2)}, u32[]{:S(2)}) collective-permute-start(bf16[1248,128]{1,0:T(8,128)(2,1)S(1)} %collective-permute-done.7.refs_4_), channel_id=1, source_target_pairs={{0,1},{1,0},{2,3},{3,2},{4,5},{5,4},{6,7},{7,6},{8,9},{9,8},{10,11... | collective-permute-start | bytes 958472 | tf_op jit(solution)/shard_map/ppermute | solution.py:48
  40.8 1.6 copy-start.17
  40.9 59.5 %copy-start.22 = (bf16[16,6144]{1,0:T(8,128)(2,1)}, bf16[16,6144]{1,0:T(8,128)(2,1)S(1)}, u32[]{:S(2)}) copy-start(bf16[16,6144]{1,0:T(8,128)(2,1)S(1)} %flag_rows.1.flags) | copy-start | bytes 589828
  100.4 4.6 %copy-start.1 = (bf16[512,1024]{1,0:T(8,128)(2,1)}, bf16[512,1024]{1,0:T(8,128)(2,1)S(1)}, u32[]{:S(2)}) copy-start(bf16[512,1024]{1,0:T(8,128)(2,1)S(1)} %get-tuple-element.62.o) | copy-start | bytes 3145732
  100.4 6.7 %copy-start.10 = (f32[8,1024]{1,0:T(8,128)}, f32[8,1024]{1,0:T(8,128)S(1)}, u32[]{:S(2)}) copy-start(f32[8,1024]{1,0:T(8,128)S(1)} %get-tuple-element.63.bias) | copy-start | bytes 98308
  100.4 3.9 %collective-permute-start.13 = (bf16[4,4,416,128]{3,2,1,0:T(8,128)(2,1)}, bf16[4,4,416,128]{3,2,1,0:T(8,128)(2,1)S(1)}, u32[]{:S(2)}, u32[]{:S(2)}) collective-permute-start(bf16[4,4,416,128]{3,2,1,0:T(8,128)(2,1)} %get-tuple-element.67), channel_id=1, source_target_pairs={{0,1},{1,0},{2,3},{3,2},{4,5},{5,4},{6,7},{7,6},{8,9},{9,8},{10,11... | collective-permute-start | bytes 5111816 | tf_op jit(solution)/shard_map/ppermute | solution.py:48
  100.6 51.7 %collective-permute-start.14 = (bf16[512,512]{1,0:T(8,128)(2,1)S(1)}, bf16[512,512]{1,0:T(8,128)(2,1)S(1)}, u32[]{:S(2)}, u32[]{:S(2)}) collective-permute-start(bf16[512,512]{1,0:T(8,128)(2,1)S(1)} %get-tuple-element.70), channel_id=1, source_target_pairs={{1,0},{2,1},{3,2},{4,3},{5,4},{6,5},{7,6},{8,7},{9,8},{10,9},{11,1... | collective-permute-start | bytes 1572872 | tf_op jit(solution)/shard_map/ppermute | solution.py:38
  105.0 3.6 %copy-start.19 = (bf16[4,416,128]{2,1,0:T(8,128)(2,1)}, bf16[4,416,128]{2,1,0:T(8,128)(2,1)S(1)}, u32[]{:S(2)}) copy-start(bf16[4,416,128]{2,1,0:T(8,128)(2,1)S(1)} %get-tuple-element.68.refs_0_) | copy-start | bytes 1277956
  105.0 24.3 %collective-permute-start.16 = (bf16[4,416,128]{2,1,0:T(8,128)(2,1)S(1)}, bf16[4,416,128]{2,1,0:T(8,128)(2,1)S(1)}, u32[]{:S(2)}, u32[]{:S(2)}) collective-permute-start(bf16[4,416,128]{2,1,0:T(8,128)(2,1)S(1)} %get-tuple-element.73), channel_id=1, source_target_pairs={{0,16},{1,17},{2,18},{3,19},{4,20},{5,21},{6,22},{7,23},{8,24},{9,... | collective-permute-start | bytes 1277960 | tf_op jit(solution)/shard_map/ppermute | solution.py:48
  107.0 22.4 %collective-permute-start.17 = (bf16[4,416,128]{2,1,0:T(8,128)(2,1)S(1)}, bf16[4,416,128]{2,1,0:T(8,128)(2,1)S(1)}, u32[]{:S(2)}, u32[]{:S(2)}) collective-permute-start(bf16[4,416,128]{2,1,0:T(8,128)(2,1)S(1)} %get-tuple-element.74), channel_id=1, source_target_pairs={{0,24},{1,25},{2,26},{3,27},{4,28},{5,29},{6,30},{7,31},{8,16},{9,... | collective-permute-start | bytes 1277960 | tf_op jit(solution)/shard_map/ppermute | solution.py:48
  107.1 22.3 %collective-permute-start.15 = (bf16[4,416,128]{2,1,0:T(8,128)(2,1)S(1)}, bf16[4,416,128]{2,1,0:T(8,128)(2,1)S(1)}, u32[]{:S(2)}, u32[]{:S(2)}) collective-permute-start(bf16[4,416,128]{2,1,0:T(8,128)(2,1)S(1)} %get-tuple-element.68.refs_0_), channel_id=1, source_target_pairs={{0,8},{1,9},{2,10},{3,11},{4,12},{5,13},{6,14},{7,15},{8,0},{9,1},... | collective-permute-start | bytes 1277960 | tf_op jit(solution)/shard_map/ppermute | solution.py:48
  129.4 0.7 copy-start.11
  130.2 4.5 %copy-start.21 = (f32[8,128]{1,0:T(8,128)}, f32[8,128]{1,0:T(8,128)S(1)}, u32[]{:S(2)}) copy-start(f32[8,128]{1,0:T(8,128)S(1)} %get-tuple-element.76.refs_0_) | copy-start | bytes 12292
  130.2 14.0 %collective-permute-start.18 = (bf16[416,128]{1,0:T(8,128)(2,1)S(1)}, bf16[416,128]{1,0:T(8,128)(2,1)S(1)}, u32[]{:S(2)}, u32[]{:S(2)}) collective-permute-start(bf16[416,128]{1,0:T(8,128)(2,1)S(1)} %get-tuple-element.80), channel_id=1, source_target_pairs={{0,2},{1,3},{2,0},{3,1},{4,6},{5,7},{6,4},{7,5},{8,10},{9,11},{10,... | collective-permute-start | bytes 319496 | tf_op jit(solution)/shard_map/ppermute | solution.py:48
  130.8 13.5 %collective-permute-start.19 = (bf16[416,128]{1,0:T(8,128)(2,1)S(1)}, bf16[416,128]{1,0:T(8,128)(2,1)S(1)}, u32[]{:S(2)}, u32[]{:S(2)}) collective-permute-start(bf16[416,128]{1,0:T(8,128)(2,1)S(1)} %get-tuple-element.81), channel_id=1, source_target_pairs={{0,4},{1,5},{2,6},{3,7},{4,0},{5,1},{6,2},{7,3},{8,12},{9,13},{10,... | collective-permute-start | bytes 319496 | tf_op jit(solution)/shard_map/ppermute | solution.py:48
  132.3 12.0 %collective-permute-start.20 = (bf16[416,128]{1,0:T(8,128)(2,1)S(1)}, bf16[416,128]{1,0:T(8,128)(2,1)S(1)}, u32[]{:S(2)}, u32[]{:S(2)}) collective-permute-start(bf16[416,128]{1,0:T(8,128)(2,1)S(1)} %get-tuple-element.82), channel_id=1, source_target_pairs={{0,6},{1,7},{2,4},{3,5},{4,2},{5,3},{6,0},{7,1},{8,14},{9,15},{10,... | collective-permute-start | bytes 319496 | tf_op jit(solution)/shard_map/ppermute | solution.py:48
  145.8 14.0 %collective-permute-start.23 = (f32[416,128]{1,0:T(8,128)S(1)}, f32[416,128]{1,0:T(8,128)S(1)}, u32[]{:S(2)}, u32[]{:S(2)}) collective-permute-start(f32[416,128]{1,0:T(8,128)S(1)} %get-tuple-element.88.refs_1_), channel_id=1, source_target_pairs={{0,24},{1,25},{2,26},{3,27},{4,28},{5,29},{6,30},{7,31},{8,16},{9,... | collective-permute-start | bytes 638984 | tf_op jit(solution)/shard_map/ppermute | solution.py:48
  147.4 12.5 %collective-permute-start.22 = (f32[416,128]{1,0:T(8,128)S(1)}, f32[416,128]{1,0:T(8,128)S(1)}, u32[]{:S(2)}, u32[]{:S(2)}) collective-permute-start(f32[416,128]{1,0:T(8,128)S(1)} %get-tuple-element.88.refs_1_), channel_id=1, source_target_pairs={{0,16},{1,17},{2,18},{3,19},{4,20},{5,21},{6,22},{7,23},{8,24},{9,... | collective-permute-start | bytes 638984 | tf_op jit(solution)/shard_map/ppermute | solution.py:48
  147.8 12.0 %collective-permute-start.21 = (f32[416,128]{1,0:T(8,128)S(1)}, f32[416,128]{1,0:T(8,128)S(1)}, u32[]{:S(2)}, u32[]{:S(2)}) collective-permute-start(f32[416,128]{1,0:T(8,128)S(1)} %get-tuple-element.88.refs_1_), channel_id=1, source_target_pairs={{0,8},{1,9},{2,10},{3,11},{4,12},{5,13},{6,14},{7,15},{8,0},{9,1},... | collective-permute-start | bytes 638984 | tf_op jit(solution)/shard_map/ppermute | solution.py:48
  149.3 10.5 %all-to-all-start = ((f32[32,1,128]{2,1,0:T(1,128)}), f32[32,1,128]{2,1,0:T(1,128)S(1)}, u32[]{:S(2)}, u32[]{:S(2)}) async-start(f32[32,1,128]{2,1,0:T(1,128)} %bitcast.5), calls=%async_computation | async-start | bytes 32768 | tf_op jit(solution)/shard_map/all_to_all | solution.py:697
  152.3 0.8 copy-start.23
  153.1 6.8 %copy-start = (f32[64,2,1024]{2,1,0:T(2,128)S(1)}, f32[64,2,1024]{2,1,0:T(2,128)}, u32[]{:S(2)}) copy-start(f32[64,2,1024]{2,1,0:T(2,128)} %refs_7_.1) | copy-start | bytes 1572868
  153.1 6.8 %copy-start.2 = (f32[64,1024]{1,0:T(8,128)S(1)}, f32[64,1024]{1,0:T(8,128)}, u32[]{:S(2)}) copy-start(f32[64,1024]{1,0:T(8,128)} %refs_13_.1) | copy-start | bytes 786436
  153.1 6.8 %copy-start.3 = (f32[64,2,1024]{2,1,0:T(2,128)S(1)}, f32[64,2,1024]{2,1,0:T(2,128)}, u32[]{:S(2)}) copy-start(f32[64,2,1024]{2,1,0:T(2,128)} %refs_5_.1) | copy-start | bytes 1572868
  153.1 6.8 %copy-start.4 = (f32[64,2,1024]{2,1,0:T(2,128)S(1)}, f32[64,2,1024]{2,1,0:T(2,128)}, u32[]{:S(2)}) copy-start(f32[64,2,1024]{2,1,0:T(2,128)} %refs_6_.1) | copy-start | bytes 1572868
  153.1 6.8 %copy-start.5 = (f32[64,1024]{1,0:T(8,128)S(1)}, f32[64,1024]{1,0:T(8,128)}, u32[]{:S(2)}) copy-start(f32[64,1024]{1,0:T(8,128)} %refs_11_.1) | copy-start | bytes 786436
  153.1 6.8 %copy-start.6 = (f32[64,1024]{1,0:T(8,128)S(1)}, f32[64,1024]{1,0:T(8,128)}, u32[]{:S(2)}) copy-start(f32[64,1024]{1,0:T(8,128)} %refs_12_.1) | copy-start | bytes 786436
  153.1 6.8 %copy-start.7 = (f32[80,128]{1,0:T(8,128)S(1)}, f32[80,128]{1,0:T(8,128)}, u32[]{:S(2)}) copy-start(f32[80,128]{1,0:T(8,128)} %refs_10_.1) | copy-start | bytes 122884
  153.1 6.8 %copy-start.8 = (f32[80,128]{1,0:T(8,128)S(1)}, f32[80,128]{1,0:T(8,128)}, u32[]{:S(2)}) copy-start(f32[80,128]{1,0:T(8,128)} %refs_8_.1) | copy-start | bytes 122884
  153.1 6.8 %copy-start.9 = (f32[80,128]{1,0:T(8,128)S(1)}, f32[80,128]{1,0:T(8,128)}, u32[]{:S(2)}) copy-start(f32[80,128]{1,0:T(8,128)} %refs_9_.1) | copy-start | bytes 122884
  153.2 6.8 %copy-start.13 = (f32[256]{0:T(256)S(1)}, f32[256]{0:T(256)}, u32[]{:S(2)}) copy-start(f32[256]{0:T(256)} %param.27) | copy-start | bytes 3076
  153.2 6.8 %copy-start.14 = (f32[256]{0:T(256)S(1)}, f32[256]{0:T(256)}, u32[]{:S(2)}) copy-start(f32[256]{0:T(256)} %param.34) | copy-start | bytes 3076
  153.2 6.8 %copy-start.15 = (f32[256]{0:T(256)S(1)}, f32[256]{0:T(256)}, u32[]{:S(2)}) copy-start(f32[256]{0:T(256)} %param.35) | copy-start | bytes 3076
  (2 other events, 1.3 us)

commit v6 on v5

--- a/solution.py
+++ b/solution.py
@@ -259,8 +259,12 @@
 def gates_body(split, subs, x, tail, mel, flags, res, skp, *refs):
     if split:
         parts, refs = refs[0:10], refs[10:]
-        p, hid, edge, w, o, bias_out, keep_out, send_out = refs[:8]
-        xe, carry, acc, acc_out, sums, small, small_low, arrived, *held = refs[8:]
+        p, hid, edge, w_out, o_out, bias_out, keep_out, send_out = refs[:8]
+        xe, carry, acc, acc_out, sums, small, small_low, w, o, arrived, *held = refs[8:]
+        passed = [
+            pltpu.make_async_copy(w, w_out, arrived.at[10]),
+            pltpu.make_async_copy(o, o_out, arrived.at[11]),
+        ]
     else:
         w, o, p, hid, edge, grad, grad_out, sums, xe, carry, acc, acc_out = refs
     step, last = pl.program_id(0), pl.num_programs(0) - 1
@@ -282,6 +286,8 @@
             for copy in copies:
                 copy.wait()
             unpack(held, w, o, bias_out, small_low)
+            for copy in passed:
+                copy.start()
 
     side = jnp.concatenate([mel[...], flags[...], jnp.zeros((32, rows), BF)], 0).T
     link = side[:, LINK : LINK + 1]
@@ -325,6 +331,8 @@
             grad[...] = acc[...]
             grad_out[...] = acc_out[...]
             return
+        for copy in passed:
+            copy.wait()
         small[...] = jnp.zeros_like(small)
         for s in range(8):
             lane = mixed_block(s) * LANES
@@ -374,14 +382,16 @@
     ]
     if split:
         more = [
-            ((1024 + AUX, 1024), BF),
-            ((512, 1024), BF),
             ((8, 1024), F32),
             ((4, 4, PART, LANES), BF),
             ((4, 4, PART, LANES), BF),
         ]
     else:
         more = [((1024 + AUX, 1024), F32), ((512, 1024), F32), ((8, 1024), F32)]
+    if split:
+        for shape in ((1024 + AUX, 1024), (512, 1024)):
+            out_specs.append(ANY)
+            out_shape.append(jax.ShapeDtypeStruct(shape, BF))
     for shape, dtype in more:
         out_specs.append(whole(shape))
         out_shape.append(jax.ShapeDtypeStruct(shape, dtype))
@@ -396,7 +406,9 @@
             pltpu.VMEM((8, 1024), F32),
             pltpu.VMEM((8, AUX, LANES), F32),
             pltpu.VMEM((8, AUX, LANES), BF),
-            pltpu.SemaphoreType.DMA((10,)),
+            pltpu.VMEM((1024 + AUX, 1024), BF),
+            pltpu.VMEM((512, 1024), BF),
+            pltpu.SemaphoreType.DMA((12,)),
         ]
         scratch += [pltpu.VMEM(e.shape, e.dtype) for e in extra]
     return pl.pallas_call(

time: 165 us -> 164 us (level)
  no operation moved by 1% of the time
where the time goes in v6:
time: 164 us
  Pallas kernels  105 us (64%)
  starting transfers between devices  28.9 us (18%)
  waiting for transfers between devices  24.9 us (15%)
  local copies, waits for them, and re-layouts  3.85 us (2%)
    pallas_call x1, Pallas kernels, gates_layer(): pl.pallas_call(functools.partial(gates_body, split, subs), grid=(steps,),...  57.1 us
    ppermute x21, waiting for transfers between devices, swap(): return lax.ppermute(x, BOTH, pairs)  24.1 us
    ppermute x21, starting transfers between devices, swap(): return lax.ppermute(x, BOTH, pairs)  21.9 us
    pallas_call x1, Pallas kernels, input_layer(): pl.pallas_call(input_body, grid=(steps,), in_specs=[by_row(512), by_row(1...  20.8 us
    pallas_call x2, Pallas kernels, mixed_layer(): pl.pallas_call(patch_body if patched else mixed_body, grid=(steps,), in_s...  16.2 us
    pallas_call x1, Pallas kernels, update(): pl.pallas_call(update_body, in_specs=[VMEM] * 17, out_specs=[VMEM] * 13,...  4.63 us
    ppermute x3, starting transfers between devices, from_behind(): return lax.ppermute(x, axis, pairs)  4.05 us
    unnamed x52, local copies, waits for them, and re-layouts  3.83 us
  transfers between devices with their start and end apart: 25, of which 9 were waited for; matrix products, arithmetic and copies ran while one was open for 1% of the time, Pallas kernels for 25%

profile of v6, /device:TPU:0, one launch (start us, length us, event | category | flops | bytes accessed | tf_op | source)
XLA Modules:
  0.0 163.9 jit_solution(13365636220430499884)
XLA Ops:
  0.7 2.6 %pack_weights.1 = (bf16[4,416,128]{2,1,0:T(8,128)(2,1)}, bf16[416,128]{1,0:T(8,128)(2,1)}) custom-call(f32[64,2,1024]{2,1,0:T(2,128)} %refs_7_.1, f32[80,128]{1,0:T(8,128)} %refs_10_.1, f32[2,128]{1,0:T(2,128)} %bitcast.16, f32[64,1024]{1,0:T(8,128)} %refs_13_.1), custom_call_target="tpu_custom_call" | custom-call | tf_op jit(solution)/shard_map/pack_weights/pallas_call | solution.py:111
  3.3 3.0 %collective-permute-start = (bf16[416,128]{1,0:T(8,128)(2,1)}, bf16[416,128]{1,0:T(8,128)(2,1)S(1)}, u32[]{:S(2)}, u32[]{:S(2)}) collective-permute-start(bf16[416,128]{1,0:T(8,128)(2,1)} %get-tuple-element.59), channel_id=1, source_target_pairs={{0,2},{1,3},{2,0},{3,1},{4,6},{5,7},{6,4},{7,5},{8,10},{9,11},{10,... | collective-permute-start | bytes 319496 | tf_op jit(solution)/shard_map/ppermute | solution.py:48
  6.3 2.5 %collective-permute-start.5 = (bf16[416,128]{1,0:T(8,128)(2,1)}, bf16[416,128]{1,0:T(8,128)(2,1)S(1)}, u32[]{:S(2)}, u32[]{:S(2)}) collective-permute-start(bf16[416,128]{1,0:T(8,128)(2,1)} %get-tuple-element.59), channel_id=1, source_target_pairs={{0,6},{1,7},{2,4},{3,5},{4,2},{5,3},{6,0},{7,1},{8,14},{9,15},{10,... | collective-permute-start | bytes 319496 | tf_op jit(solution)/shard_map/ppermute | solution.py:48
  8.8 0.1 collective-permute-start.4
  8.9 0.6 collective-permute-done._
  9.5 0.6 copy-done.24
  10.1 1.9 %last_rows.1 = bf16[512,512]{1,0:T(8,128)(2,1)} custom-call(bf16[6144,512]{1,0:T(8,128)(2,1)} %x.7, bf16[416,128]{1,0:T(8,128)(2,1)} %copy-done.24), custom_call_target="tpu_custom_call" | custom-call | tf_op jit(solution)/shard_map/last_rows/pallas_call | solution.py:130
  12.0 1.3 collective-permute-start.1
  13.3 0.9 constant_dynamic-update-slice_fusion.2
  14.2 4.5 %collective-permute-done.4 = bf16[416,128]{1,0:T(8,128)(2,1)S(1)} collective-permute-done((bf16[416,128]{1,0:T(8,128)(2,1)}, bf16[416,128]{1,0:T(8,128)(2,1)S(1)}, u32[]{:S(2)}, u32[]{:S(2)}) %collective-permute-start.4) | collective-permute-done | bytes 106528 | tf_op jit(solution)/shard_map/ppermute | solution.py:48
  18.7 2.5 %collective-permute-start.9 = (bf16[1248,128]{1,0:T(8,128)(2,1)S(1)}, bf16[1248,128]{1,0:T(8,128)(2,1)S(1)}, u32[]{:S(2)}, u32[]{:S(2)}) collective-permute-start(bf16[1248,128]{1,0:T(8,128)(2,1)S(1)} %constant_dynamic-update-slice_fusion.refs_2_), channel_id=1, source_target_pairs={{0,24},{1,25},{2,26},{3,27},{4,28},{5,29},{6,30},{7,31},{8,16},{9,... | collective-permute-start | bytes 958472 | tf_op jit(solution)/shard_map/ppermute | solution.py:48
  21.3 0.5 collective-permute-start.8
  21.8 0.5 collective-permute-start.7
  22.3 1.3 collective-permute-start.2
  23.6 0.8 collective-permute-done.2
  24.4 0.5 collective-permute-start.3
  24.9 6.7 %collective-permute-done.9.refs_6_ = bf16[1248,128]{1,0:T(8,128)(2,1)S(1)} collective-permute-done((bf16[1248,128]{1,0:T(8,128)(2,1)S(1)}, bf16[1248,128]{1,0:T(8,128)(2,1)S(1)}, u32[]{:S(2)}, u32[]{:S(2)}) %collective-permute-start.9) | collective-permute-done | bytes 319520 | tf_op jit(solution)/shard_map/ppermute | solution.py:48
  31.6 7.6 %collective-permute-done.8.refs_5_ = bf16[1248,128]{1,0:T(8,128)(2,1)S(1)} collective-permute-done((bf16[1248,128]{1,0:T(8,128)(2,1)S(1)}, bf16[1248,128]{1,0:T(8,128)(2,1)S(1)}, u32[]{:S(2)}, u32[]{:S(2)}) %collective-permute-start.8) | collective-permute-done | bytes 319520 | tf_op jit(solution)/shard_map/ppermute | solution.py:48
  39.2 0.0 collective-permute-start.12
  39.2 1.0 collective-permute-done.7.refs_4_
  40.3 0.5 collective-permute-start.10
  40.8 0.1 flag_rows.1.flags
  40.9 1.0 collective-permute-done.11.refs_8_
  41.9 0.5 collective-permute-done.10.refs_7_
  42.4 57.1 %gates_layer.1 = (bf16[6144,1024]{1,0:T(8,128)(2,1)}, bf16[6144,512]{1,0:T(8,128)(2,1)}, bf16[512,512]{1,0:T(8,128)(2,1)S(1)}, bf16[1152,1024]{1,0:T(8,128)(2,1)...) custom-call(bf16[6144,512]{1,0:T(8,128)(2,1)} %x.7, ...), custom_call_target="tpu_custom_call" | custom-call | flops 43486543872 | bytes 49152000 | tf_op jit(solution)/shard_map/gates_layer/pallas_call | solution.py:414
  99.5 0.2 collective-permute-start.13
  99.7 1.5 collective-permute-start.14
  101.2 2.2 %collective-permute-done.13.got = bf16[4,4,416,128]{3,2,1,0:T(8,128)(2,1)S(1)} collective-permute-done((bf16[4,4,416,128]{3,2,1,0:T(8,128)(2,1)}, bf16[4,4,416,128]{3,2,1,0:T(8,128)(2,1)S(1)}, u32[]{:S(2)}, u32[]{:S(2)}) %collective-permute-start.13) | collective-permute-done | bytes 1703968 | tf_op jit(solution)/shard_map/ppermute | solution.py:48
  103.4 0.7 add_cores.1
  104.1 1.9 %collective-permute-start.16 = (bf16[4,416,128]{2,1,0:T(8,128)(2,1)S(1)}, bf16[4,416,128]{2,1,0:T(8,128)(2,1)S(1)}, u32[]{:S(2)}, u32[]{:S(2)}) collective-permute-start(bf16[4,416,128]{2,1,0:T(8,128)(2,1)S(1)} %get-tuple-element.73), channel_id=1, source_target_pairs={{0,16},{1,17},{2,18},{3,19},{4,20},{5,21},{6,22},{7,23},{8,24},{9,... | collective-permute-start | bytes 1277960 | tf_op jit(solution)/shard_map/ppermute | solution.py:48
  106.1 0.1 collective-permute-start.17
  106.2 1.5 collective-permute-start.15
  107.7 20.8 %input_layer.1 = (bf16[6144,512]{1,0:T(8,128)(2,1)}, f32[512,512]{1,0:T(8,128)}, f32[8,128]{1,0:T(8,128)}) custom-call(bf16[6144,512]{1,0:T(8,128)(2,1)} %res.3, bf16[6144,1024]{1,0:T(8,128)(2,1)} %get-tuple-element.64.p, bf16[16,6144]{1,0:T(8,128)(2,1)} %copy-done.22, bf16[1152,1024]{1,0:T(8,128)(2,1)} %get-tuple-element.65.w, bf16[4,416,128]{2,1,0:T(8,128)(2,1)} %copy-done.19), custom_call_target="tpu_custom_call" | custom-call | flops 12884901888 | bytes 25165824 | tf_op jit(solution)/shard_map/input_layer/pallas_call | solution.py:503
  128.5 0.7 copy-done.11
  129.2 0.2 add_hop.1
  129.4 0.5 collective-permute-start.18
  129.9 1.5 collective-permute-start.19
  131.4 2.4 %collective-permute-start.20 = (bf16[416,128]{1,0:T(8,128)(2,1)S(1)}, bf16[416,128]{1,0:T(8,128)(2,1)S(1)}, u32[]{:S(2)}, u32[]{:S(2)}) collective-permute-start(bf16[416,128]{1,0:T(8,128)(2,1)S(1)} %get-tuple-element.82), channel_id=1, source_target_pairs={{0,6},{1,7},{2,4},{3,5},{4,2},{5,3},{6,0},{7,1},{8,14},{9,15},{10,... | collective-permute-start | bytes 319496 | tf_op jit(solution)/shard_map/ppermute | solution.py:48
  133.8 9.6 %mixed_layer_0.1 = (bf16[6144,512]{1,0:T(8,128)(2,1)}, bf16[6144,512]{1,0:T(8,128)(2,1)}, f32[8,128]{1,0:T(8,128)}) custom-call(bf16[6144,512]{1,0:T(8,128)(2,1)} %x.7, bf16[6144,512]{1,0:T(8,128)(2,1)} %get-tuple-element.61.hid, bf16[512,1024]{1,0:T(8,128)(2,1)} %copy-done.1, f32[8,1024]{1,0:T(8,128)} %copy-done.10, f32[8,128]{1,0:T(8,128)} %copy-done.21), custom_call_target="tpu_custom_call" | custom-call | flops 4294967296 | bytes 16777216 | tf_op jit(solution)/shard_map/mixed_layer_0/pallas_call | solution.py:465
  143.5 0.7 copy-done.12
  144.1 0.8 add_last.1
  145.0 1.5 collective-permute-start.23
  146.5 0.5 collective-permute-start.22
  147.0 1.5 collective-permute-start.21
  148.4 2.9 %all-to-all-start = ((f32[32,1,128]{2,1,0:T(1,128)}), f32[32,1,128]{2,1,0:T(1,128)S(1)}, u32[]{:S(2)}, u32[]{:S(2)}) async-start(f32[32,1,128]{2,1,0:T(1,128)} %bitcast.5), calls=%async_computation | async-start | bytes 32768 | tf_op jit(solution)/shard_map/all_to_all | solution.py:709
  151.4 0.8 copy-done.23
  152.3 6.6 %mixed_layer_4.1 = (bf16[6144,512]{1,0:T(8,128)(2,1)}, bf16[6144,512]{1,0:T(8,128)(2,1)}, bf16[6144,512]{1,0:T(8,128)(2,1)}, f32[8,128]{1,0:T(8,128)}) custom-call(bf16[6144,512]{1,0:T(8,128)(2,1)} %x.7, bf16[6144,512]{1,0:T(8,128)(2,1)} %get-tuple-element.61.hid, ...), custom_call_target="tpu_custom_call", output_to_operand_aliasing={{2}: (6, {}), {0}: (7, {}), {1}: (8, {})} | custom-call | flops 2147483648 | bytes 8388608 | tf_op jit(solution)/shard_map/mixed_layer_4/pallas_call | solution.py:465
  159.1 4.6 %update.1 = (f32[1,128]{1,0:T(1,128)}, f32[64,2,1024]{2,1,0:T(2,128)}, f32[64,2,1024]{2,1,0:T(2,128)}, f32[64,2,1024]{2,1,0:T(2,128)}, f32[80,128]{1,0:T(8,128)}...) custom-call(f32[32,128]{1,0:T(8,128)S(1)} %bitcast.15, ...), custom_call_target="tpu_custom_call" | custom-call | tf_op jit(solution)/shard_map/update/pallas_call | solution.py:630
  (67 shorter events, 0.2 us)
Async XLA Ops:
  0.6 21.7 %copy-start.16 = (s32[6144]{0:T(1024)S(1)}, s32[6144]{0:T(1024)}, u32[]{:S(2)}) copy-start(s32[6144]{0:T(1024)} %param.20) | copy-start | bytes 73732
  0.7 40.1 %copy-start.20 = (s32[6144]{0:T(1024)S(1)}, s32[6144]{0:T(1024)}, u32[]{:S(2)}) copy-start(s32[6144]{0:T(1024)} %param.21) | copy-start | bytes 73732
  3.3 21.1 %copy-start.18 = (bf16[4,416,128]{2,1,0:T(8,128)(2,1)S(1)}, bf16[4,416,128]{2,1,0:T(8,128)(2,1)}, u32[]{:S(2)}) copy-start(bf16[4,416,128]{2,1,0:T(8,128)(2,1)} %get-tuple-element.60.refs_0_) | copy-start | bytes 1277956
  3.3 6.2 %collective-permute-start = (bf16[416,128]{1,0:T(8,128)(2,1)}, bf16[416,128]{1,0:T(8,128)(2,1)S(1)}, u32[]{:S(2)}, u32[]{:S(2)}) collective-permute-start(bf16[416,128]{1,0:T(8,128)(2,1)} %get-tuple-element.59), channel_id=1, source_target_pairs={{0,2},{1,3},{2,0},{3,1},{4,6},{5,7},{6,4},{7,5},{8,10},{9,11},{10,... | collective-permute-start | bytes 319496 | tf_op jit(solution)/shard_map/ppermute | solution.py:48
  6.3 12.4 %collective-permute-start.5 = (bf16[416,128]{1,0:T(8,128)(2,1)}, bf16[416,128]{1,0:T(8,128)(2,1)S(1)}, u32[]{:S(2)}, u32[]{:S(2)}) collective-permute-start(bf16[416,128]{1,0:T(8,128)(2,1)} %get-tuple-element.59), channel_id=1, source_target_pairs={{0,6},{1,7},{2,4},{3,5},{4,2},{5,3},{6,0},{7,1},{8,14},{9,15},{10,... | collective-permute-start | bytes 319496 | tf_op jit(solution)/shard_map/ppermute | solution.py:48
  8.8 9.9 %collective-permute-start.4 = (bf16[416,128]{1,0:T(8,128)(2,1)}, bf16[416,128]{1,0:T(8,128)(2,1)S(1)}, u32[]{:S(2)}, u32[]{:S(2)}) collective-permute-start(bf16[416,128]{1,0:T(8,128)(2,1)} %get-tuple-element.59), channel_id=1, source_target_pairs={{0,4},{1,5},{2,6},{3,7},{4,0},{5,1},{6,2},{7,3},{8,12},{9,13},{10,... | collective-permute-start | bytes 319496 | tf_op jit(solution)/shard_map/ppermute | solution.py:48
  12.0 28.3 %collective-permute-start.1 = (bf16[512,512]{1,0:T(8,128)(2,1)}, bf16[512,512]{1,0:T(8,128)(2,1)S(1)}, u32[]{:S(2)}, u32[]{:S(2)}) collective-permute-start(bf16[512,512]{1,0:T(8,128)(2,1)} %last_rows.1), channel_id=1, source_target_pairs={{0,1},{1,2},{2,3},{3,4},{4,5},{5,6},{6,7},{7,8},{8,9},{9,10},{10,1... | collective-permute-start | bytes 1572872 | tf_op jit(solution)/shard_map/ppermute | solution.py:38
  18.7 12.9 %collective-permute-start.9 = (bf16[1248,128]{1,0:T(8,128)(2,1)S(1)}, bf16[1248,128]{1,0:T(8,128)(2,1)S(1)}, u32[]{:S(2)}, u32[]{:S(2)}) collective-permute-start(bf16[1248,128]{1,0:T(8,128)(2,1)S(1)} %constant_dynamic-update-slice_fusion.refs_2_), channel_id=1, source_target_pairs={{0,24},{1,25},{2,26},{3,27},{4,28},{5,29},{6,30},{7,31},{8,16},{9,... | collective-permute-start | bytes 958472 | tf_op jit(solution)/shard_map/ppermute | solution.py:48
  21.3 18.0 %collective-permute-start.8 = (bf16[1248,128]{1,0:T(8,128)(2,1)S(1)}, bf16[1248,128]{1,0:T(8,128)(2,1)S(1)}, u32[]{:S(2)}, u32[]{:S(2)}) collective-permute-start(bf16[1248,128]{1,0:T(8,128)(2,1)S(1)} %constant_dynamic-update-slice_fusion.refs_2_), channel_id=1, source_target_pairs={{0,16},{1,17},{2,18},{3,19},{4,20},{5,21},{6,22},{7,23},{8,24},{9,... | collective-permute-start | bytes 958472 | tf_op jit(solution)/shard_map/ppermute | solution.py:48
  21.8 18.5 %collective-permute-start.7 = (bf16[1248,128]{1,0:T(8,128)(2,1)S(1)}, bf16[1248,128]{1,0:T(8,128)(2,1)S(1)}, u32[]{:S(2)}, u32[]{:S(2)}) collective-permute-start(bf16[1248,128]{1,0:T(8,128)(2,1)S(1)} %constant_dynamic-update-slice_fusion.refs_2_), channel_id=1, source_target_pairs={{0,8},{1,9},{2,10},{3,11},{4,12},{5,13},{6,14},{7,15},{8,0},{9,1},... | collective-permute-start | bytes 958472 | tf_op jit(solution)/shard_map/ppermute | solution.py:48
  22.3 2.1 %collective-permute-start.2 = (s32[512]{0:T(512)S(1)}, s32[512]{0:T(512)S(1)}, u32[]{:S(2)}, u32[]{:S(2)}) collective-permute-start(s32[512]{0:T(512)S(1)} %slice.6), channel_id=1, source_target_pairs={{0,1},{1,2},{2,3},{3,4},{4,5},{5,6},{6,7},{7,8},{8,9},{9,10},{10,1... | collective-permute-start | bytes 6152 | tf_op jit(solution)/shard_map/ppermute | solution.py:38
  24.4 16.5 %collective-permute-start.3 = (bf16[4,416,128]{2,1,0:T(8,128)(2,1)S(1)}, bf16[4,416,128]{2,1,0:T(8,128)(2,1)S(1)}, u32[]{:S(2)}, u32[]{:S(2)}) collective-permute-start(bf16[4,416,128]{2,1,0:T(8,128)(2,1)S(1)} %copy-done.18), channel_id=1, source_target_pairs={{0,1},{1,0},{2,3},{3,2},{4,5},{5,4},{6,7},{7,6},{8,9},{9,8},{10,11... | collective-permute-start | bytes 1277960 | tf_op jit(solution)/shard_map/ppermute | solution.py:48
  31.6 9.3 %collective-permute-start.6 = (bf16[1248,128]{1,0:T(8,128)(2,1)S(1)}, bf16[1248,128]{1,0:T(8,128)(2,1)S(1)}, u32[]{:S(2)}, u32[]{:S(2)}) collective-permute-start(bf16[1248,128]{1,0:T(8,128)(2,1)S(1)} %constant_dynamic-update-slice_fusion.refs_2_), channel_id=1, source_target_pairs={{0,1},{1,0},{2,3},{3,2},{4,5},{5,4},{6,7},{7,6},{8,9},{9,8},{10,11... | collective-permute-start | bytes 958472 | tf_op jit(solution)/shard_map/ppermute | solution.py:48
  39.2 1.7 %collective-permute-start.12 = (bf16[1248,128]{1,0:T(8,128)(2,1)S(1)}, bf16[1248,128]{1,0:T(8,128)(2,1)S(1)}, u32[]{:S(2)}, u32[]{:S(2)}) collective-permute-start(bf16[1248,128]{1,0:T(8,128)(2,1)S(1)} %collective-permute-done.9.refs_6_), channel_id=1, source_target_pairs={{0,1},{1,0},{2,3},{3,2},{4,5},{5,4},{6,7},{7,6},{8,9},{9,8},{10,11... | collective-permute-start | bytes 958472 | tf_op jit(solution)/shard_map/ppermute | solution.py:48
  40.3 1.6 collective-permute-start.11
  40.3 2.1 %collective-permute-start.10 = (bf16[1248,128]{1,0:T(8,128)(2,1)S(1)}, bf16[1248,128]{1,0:T(8,128)(2,1)S(1)}, u32[]{:S(2)}, u32[]{:S(2)}) collective-permute-start(bf16[1248,128]{1,0:T(8,128)(2,1)S(1)} %collective-permute-done.7.refs_4_), channel_id=1, source_target_pairs={{0,1},{1,0},{2,3},{3,2},{4,5},{5,4},{6,7},{7,6},{8,9},{9,8},{10,11... | collective-permute-start | bytes 958472 | tf_op jit(solution)/shard_map/ppermute | solution.py:48
  40.8 1.6 copy-start.17
  40.9 58.6 %copy-start.22 = (bf16[16,6144]{1,0:T(8,128)(2,1)}, bf16[16,6144]{1,0:T(8,128)(2,1)S(1)}, u32[]{:S(2)}) copy-start(bf16[16,6144]{1,0:T(8,128)(2,1)S(1)} %flag_rows.1.flags) | copy-start | bytes 589828
  99.5 4.6 %copy-start.1 = (bf16[512,1024]{1,0:T(8,128)(2,1)}, bf16[512,1024]{1,0:T(8,128)(2,1)S(1)}, u32[]{:S(2)}) copy-start(bf16[512,1024]{1,0:T(8,128)(2,1)S(1)} %get-tuple-element.62.o) | copy-start | bytes 3145732
  99.5 6.7 %copy-start.10 = (f32[8,1024]{1,0:T(8,128)}, f32[8,1024]{1,0:T(8,128)S(1)}, u32[]{:S(2)}) copy-start(f32[8,1024]{1,0:T(8,128)S(1)} %get-tuple-element.63.bias) | copy-start | bytes 98308
  99.5 3.9 %collective-permute-start.13 = (bf16[4,4,416,128]{3,2,1,0:T(8,128)(2,1)}, bf16[4,4,416,128]{3,2,1,0:T(8,128)(2,1)S(1)}, u32[]{:S(2)}, u32[]{:S(2)}) collective-permute-start(bf16[4,4,416,128]{3,2,1,0:T(8,128)(2,1)} %get-tuple-element.67), channel_id=1, source_target_pairs={{0,1},{1,0},{2,3},{3,2},{4,5},{5,4},{6,7},{7,6},{8,9},{9,8},{10,11... | collective-permute-start | bytes 5111816 | tf_op jit(solution)/shard_map/ppermute | solution.py:48
  99.7 51.7 %collective-permute-start.14 = (bf16[512,512]{1,0:T(8,128)(2,1)S(1)}, bf16[512,512]{1,0:T(8,128)(2,1)S(1)}, u32[]{:S(2)}, u32[]{:S(2)}) collective-permute-start(bf16[512,512]{1,0:T(8,128)(2,1)S(1)} %get-tuple-element.70), channel_id=1, source_target_pairs={{1,0},{2,1},{3,2},{4,3},{5,4},{6,5},{7,6},{8,7},{9,8},{10,9},{11,1... | collective-permute-start | bytes 1572872 | tf_op jit(solution)/shard_map/ppermute | solution.py:38
  104.1 3.6 %copy-start.19 = (bf16[4,416,128]{2,1,0:T(8,128)(2,1)}, bf16[4,416,128]{2,1,0:T(8,128)(2,1)S(1)}, u32[]{:S(2)}) copy-start(bf16[4,416,128]{2,1,0:T(8,128)(2,1)S(1)} %get-tuple-element.68.refs_0_) | copy-start | bytes 1277956
  104.1 24.3 %collective-permute-start.16 = (bf16[4,416,128]{2,1,0:T(8,128)(2,1)S(1)}, bf16[4,416,128]{2,1,0:T(8,128)(2,1)S(1)}, u32[]{:S(2)}, u32[]{:S(2)}) collective-permute-start(bf16[4,416,128]{2,1,0:T(8,128)(2,1)S(1)} %get-tuple-element.73), channel_id=1, source_target_pairs={{0,16},{1,17},{2,18},{3,19},{4,20},{5,21},{6,22},{7,23},{8,24},{9,... | collective-permute-start | bytes 1277960 | tf_op jit(solution)/shard_map/ppermute | solution.py:48
  106.1 22.4 %collective-permute-start.17 = (bf16[4,416,128]{2,1,0:T(8,128)(2,1)S(1)}, bf16[4,416,128]{2,1,0:T(8,128)(2,1)S(1)}, u32[]{:S(2)}, u32[]{:S(2)}) collective-permute-start(bf16[4,416,128]{2,1,0:T(8,128)(2,1)S(1)} %get-tuple-element.74), channel_id=1, source_target_pairs={{0,24},{1,25},{2,26},{3,27},{4,28},{5,29},{6,30},{7,31},{8,16},{9,... | collective-permute-start | bytes 1277960 | tf_op jit(solution)/shard_map/ppermute | solution.py:48
  106.2 22.3 %collective-permute-start.15 = (bf16[4,416,128]{2,1,0:T(8,128)(2,1)S(1)}, bf16[4,416,128]{2,1,0:T(8,128)(2,1)S(1)}, u32[]{:S(2)}, u32[]{:S(2)}) collective-permute-start(bf16[4,416,128]{2,1,0:T(8,128)(2,1)S(1)} %get-tuple-element.68.refs_0_), channel_id=1, source_target_pairs={{0,8},{1,9},{2,10},{3,11},{4,12},{5,13},{6,14},{7,15},{8,0},{9,1},... | collective-permute-start | bytes 1277960 | tf_op jit(solution)/shard_map/ppermute | solution.py:48
  128.5 0.7 copy-start.11
  129.4 4.5 %copy-start.21 = (f32[8,128]{1,0:T(8,128)}, f32[8,128]{1,0:T(8,128)S(1)}, u32[]{:S(2)}) copy-start(f32[8,128]{1,0:T(8,128)S(1)} %get-tuple-element.76.refs_0_) | copy-start | bytes 12292
  129.4 14.0 %collective-permute-start.18 = (bf16[416,128]{1,0:T(8,128)(2,1)S(1)}, bf16[416,128]{1,0:T(8,128)(2,1)S(1)}, u32[]{:S(2)}, u32[]{:S(2)}) collective-permute-start(bf16[416,128]{1,0:T(8,128)(2,1)S(1)} %get-tuple-element.80), channel_id=1, source_target_pairs={{0,2},{1,3},{2,0},{3,1},{4,6},{5,7},{6,4},{7,5},{8,10},{9,11},{10,... | collective-permute-start | bytes 319496 | tf_op jit(solution)/shard_map/ppermute | solution.py:48
  129.9 13.5 %collective-permute-start.19 = (bf16[416,128]{1,0:T(8,128)(2,1)S(1)}, bf16[416,128]{1,0:T(8,128)(2,1)S(1)}, u32[]{:S(2)}, u32[]{:S(2)}) collective-permute-start(bf16[416,128]{1,0:T(8,128)(2,1)S(1)} %get-tuple-element.81), channel_id=1, source_target_pairs={{0,4},{1,5},{2,6},{3,7},{4,0},{5,1},{6,2},{7,3},{8,12},{9,13},{10,... | collective-permute-start | bytes 319496 | tf_op jit(solution)/shard_map/ppermute | solution.py:48
  131.4 12.0 %collective-permute-start.20 = (bf16[416,128]{1,0:T(8,128)(2,1)S(1)}, bf16[416,128]{1,0:T(8,128)(2,1)S(1)}, u32[]{:S(2)}, u32[]{:S(2)}) collective-permute-start(bf16[416,128]{1,0:T(8,128)(2,1)S(1)} %get-tuple-element.82), channel_id=1, source_target_pairs={{0,6},{1,7},{2,4},{3,5},{4,2},{5,3},{6,0},{7,1},{8,14},{9,15},{10,... | collective-permute-start | bytes 319496 | tf_op jit(solution)/shard_map/ppermute | solution.py:48
  145.0 14.0 %collective-permute-start.23 = (f32[416,128]{1,0:T(8,128)S(1)}, f32[416,128]{1,0:T(8,128)S(1)}, u32[]{:S(2)}, u32[]{:S(2)}) collective-permute-start(f32[416,128]{1,0:T(8,128)S(1)} %get-tuple-element.88.refs_1_), channel_id=1, source_target_pairs={{0,24},{1,25},{2,26},{3,27},{4,28},{5,29},{6,30},{7,31},{8,16},{9,... | collective-permute-start | bytes 638984 | tf_op jit(solution)/shard_map/ppermute | solution.py:48
  146.5 12.5 %collective-permute-start.22 = (f32[416,128]{1,0:T(8,128)S(1)}, f32[416,128]{1,0:T(8,128)S(1)}, u32[]{:S(2)}, u32[]{:S(2)}) collective-permute-start(f32[416,128]{1,0:T(8,128)S(1)} %get-tuple-element.88.refs_1_), channel_id=1, source_target_pairs={{0,16},{1,17},{2,18},{3,19},{4,20},{5,21},{6,22},{7,23},{8,24},{9,... | collective-permute-start | bytes 638984 | tf_op jit(solution)/shard_map/ppermute | solution.py:48
  147.0 12.0 %collective-permute-start.21 = (f32[416,128]{1,0:T(8,128)S(1)}, f32[416,128]{1,0:T(8,128)S(1)}, u32[]{:S(2)}, u32[]{:S(2)}) collective-permute-start(f32[416,128]{1,0:T(8,128)S(1)} %get-tuple-element.88.refs_1_), channel_id=1, source_target_pairs={{0,8},{1,9},{2,10},{3,11},{4,12},{5,13},{6,14},{7,15},{8,0},{9,1},... | collective-permute-start | bytes 638984 | tf_op jit(solution)/shard_map/ppermute | solution.py:48
  148.4 10.5 %all-to-all-start = ((f32[32,1,128]{2,1,0:T(1,128)}), f32[32,1,128]{2,1,0:T(1,128)S(1)}, u32[]{:S(2)}, u32[]{:S(2)}) async-start(f32[32,1,128]{2,1,0:T(1,128)} %bitcast.5), calls=%async_computation | async-start | bytes 32768 | tf_op jit(solution)/shard_map/all_to_all | solution.py:709
  151.4 0.8 copy-start.23
  152.2 6.8 %copy-start = (f32[64,2,1024]{2,1,0:T(2,128)S(1)}, f32[64,2,1024]{2,1,0:T(2,128)}, u32[]{:S(2)}) copy-start(f32[64,2,1024]{2,1,0:T(2,128)} %refs_7_.1) | copy-start | bytes 1572868
  152.2 6.8 %copy-start.2 = (f32[64,1024]{1,0:T(8,128)S(1)}, f32[64,1024]{1,0:T(8,128)}, u32[]{:S(2)}) copy-start(f32[64,1024]{1,0:T(8,128)} %refs_13_.1) | copy-start | bytes 786436
  152.2 6.8 %copy-start.3 = (f32[64,2,1024]{2,1,0:T(2,128)S(1)}, f32[64,2,1024]{2,1,0:T(2,128)}, u32[]{:S(2)}) copy-start(f32[64,2,1024]{2,1,0:T(2,128)} %refs_5_.1) | copy-start | bytes 1572868
  152.2 6.8 %copy-start.4 = (f32[64,2,1024]{2,1,0:T(2,128)S(1)}, f32[64,2,1024]{2,1,0:T(2,128)}, u32[]{:S(2)}) copy-start(f32[64,2,1024]{2,1,0:T(2,128)} %refs_6_.1) | copy-start | bytes 1572868
  152.2 6.8 %copy-start.5 = (f32[64,1024]{1,0:T(8,128)S(1)}, f32[64,1024]{1,0:T(8,128)}, u32[]{:S(2)}) copy-start(f32[64,1024]{1,0:T(8,128)} %refs_11_.1) | copy-start | bytes 786436
  152.2 6.8 %copy-start.6 = (f32[64,1024]{1,0:T(8,128)S(1)}, f32[64,1024]{1,0:T(8,128)}, u32[]{:S(2)}) copy-start(f32[64,1024]{1,0:T(8,128)} %refs_12_.1) | copy-start | bytes 786436
  152.2 6.8 %copy-start.7 = (f32[80,128]{1,0:T(8,128)S(1)}, f32[80,128]{1,0:T(8,128)}, u32[]{:S(2)}) copy-start(f32[80,128]{1,0:T(8,128)} %refs_10_.1) | copy-start | bytes 122884
  152.3 6.8 %copy-start.8 = (f32[80,128]{1,0:T(8,128)S(1)}, f32[80,128]{1,0:T(8,128)}, u32[]{:S(2)}) copy-start(f32[80,128]{1,0:T(8,128)} %refs_8_.1) | copy-start | bytes 122884
  152.3 6.8 %copy-start.9 = (f32[80,128]{1,0:T(8,128)S(1)}, f32[80,128]{1,0:T(8,128)}, u32[]{:S(2)}) copy-start(f32[80,128]{1,0:T(8,128)} %refs_9_.1) | copy-start | bytes 122884
  152.3 6.8 %copy-start.13 = (f32[256]{0:T(256)S(1)}, f32[256]{0:T(256)}, u32[]{:S(2)}) copy-start(f32[256]{0:T(256)} %param.27) | copy-start | bytes 3076
  152.3 6.8 %copy-start.14 = (f32[256]{0:T(256)S(1)}, f32[256]{0:T(256)}, u32[]{:S(2)}) copy-start(f32[256]{0:T(256)} %param.34) | copy-start | bytes 3076
  152.3 6.8 %copy-start.15 = (f32[256]{0:T(256)S(1)}, f32[256]{0:T(256)}, u32[]{:S(2)}) copy-start(f32[256]{0:T(256)} %param.35) | copy-start | bytes 3076
  (2 other events, 1.3 us)
